TPU v7x, 512 devices: a whole 4x4x16 slice. The times are simulated.
512 devices in a mesh: gx: 32 (over z_lo, x), gy: 16 (over y, z_hi, core).
Axes of the slice: x: 4, y: 4, z: 16 (z_hi: 2, z_lo: 8; z = z_hi * 8 + z_lo), core: 2. Of those that a mesh axis runs over, the one named last changes fastest.
Arguments:
- volts_start: float32 [8, 512, 16384], P(None, 'gx', 'gy'), may hold values from 0.55 to 1, as said below
- seg_cond: float32 [8, 512, 16384], P(None, 'gx', 'gy'), may hold values from 0.5 to 2
- via_cond: float32 [7, 512, 16384], P(None, 'gx', 'gy'), may hold values from 1 to 4
- via_mask: int32 [7, 512, 16384], P(None, 'gx', 'gy'), may hold values 0 or 1
- pad_mask: int32 [512, 16384], P('gx', 'gy'), may hold values 0 or 1
- load_current: float32 [512, 16384], P('gx', 'gy'), may hold values from 0 to 2.7, as said below
- stress_start: float32 [8, 512, 16384], P(None, 'gx', 'gy'), may hold values from -6 to 6
- mobility: float32 [8, 512, 16384], P(None, 'gx', 'gy'), may hold values from 0.1 to 0.45
- blocked: int32 [8, 512, 16384], P(None, 'gx', 'gy'), may hold values 0 or 1
- layer_dirs: int32 [8], replicated, may hold values from 0 to 1, as said below
Outputs:
- volts_final: float32 [8, 512, 16384], P(None, 'gx', 'gy')
- stress_final: float32 [8, 512, 16384], P(None, 'gx', 'gy')
- resid_rms: float32 [], replicated
Inputs may be any that keep to these rules, and one draw needn't show every extreme that they name: `volts_start`: node voltages near the supply level, one sign. `load_current`: positive load currents. `layer_dirs`: exactly 4 layers run along x and the others along y.
All inputs are finite; a program needn't handle non-finite values. No bound on the sum of `via_mask` or of `pad_mask` or of `blocked` on one device may be relied on, other than what follows from the above.
Results may differ from a plain program's by a relative error of at most 0.00002.
Values sent between devices are 32-bit elements; how exact they have to be, the bound alone decides.
No kernel may reach another device: no remote copies, remote signals or barrier semaphores. Data moves between devices by JAX's collectives and lax.ppermute only.
A program may use at most 64 MiB of HBM per device.

v0:
```python
import jax
import jax.numpy as jnp
from jax import lax
from jax.sharding import PartitionSpec as P

SWEEPS = 3
STEPS = 3


damping = 0.8
pad_conductance = 4.0
supply_volts = 1.0
wind_factor = 4.0


def from_behind(value, axis, steps):
    count = lax.axis_size(axis)
    initial, last = (max(0, -steps), min(count, count - steps))
    return lax.ppermute(value, axis, [(source, source + steps) for source in range(initial, last)])


def with_halo(cells, sides, width):
    for axis, dim in sides:
        count = lax.axis_size(axis)
        ends = count - 1
        head = lax.slice_in_dim(cells, 0, width, axis=dim)
        tail = lax.slice_in_dim(cells, cells.shape[dim] - width, cells.shape[dim], axis=dim)
        cells = jnp.concatenate(
            [
                lax.ppermute(tail, axis, [(i, (i + 1) % count) for i in range(ends)]),
                cells,
                lax.ppermute(head, axis, [((i + 1) % count, i) for i in range(ends)]),
            ],
            axis=dim,
        )
    return cells


def layer_pair(field):
    zero = jnp.zeros_like(field[:1])
    return (jnp.concatenate([zero, field[:-1]], 0), jnp.concatenate([field[1:], zero], 0))


def lateral_both(padded, cond_xl, cond_xr, cond_yl, cond_yr):
    total = cond_xl * padded[:, :-2, 1:-1] + cond_xr * padded[:, 2:, 1:-1]
    return total + cond_yl * padded[:, 1:-1, :-2] + cond_yr * padded[:, 1:-1, 2:]


def finish(lateral, volts, via_below, via_above, sources):
    below, above = layer_pair(volts)
    return lateral + via_below * below + via_above * above + sources


def body(
    volts_start,
    seg_cond,
    via_cond,
    via_mask,
    pad_mask,
    load_current,
    stress_start,
    mobility,
    blocked,
    layer_dirs,
):
    layers, rows_x, rows_y = seg_cond.shape
    total_x = rows_x * lax.axis_size("gx")
    total_y = rows_y * lax.axis_size("gy")
    index_x = lax.axis_index("gx") * rows_x + jnp.arange(rows_x, dtype=jnp.int32)
    index_y = lax.axis_index("gy") * rows_y + jnp.arange(rows_y, dtype=jnp.int32)
    inner_x = (index_x < total_x - 1).astype(jnp.float32)[None, :, None]
    inner_y = (index_y < total_y - 1).astype(jnp.float32)[None, None, :]
    along_y = layer_dirs.astype(jnp.float32)[:, None, None]
    along_x = 1.0 - along_y
    cond_xr = seg_cond * along_x * inner_x
    cond_yr = seg_cond * along_y * inner_y
    via_both = via_cond * via_mask.astype(jnp.float32)
    zero = jnp.zeros((1, rows_x, rows_y), jnp.float32)
    via_below = jnp.concatenate([zero, via_both], 0)
    via_above = jnp.concatenate([via_both, zero], 0)
    pads = pad_conductance * pad_mask.astype(jnp.float32)
    level = jnp.arange(layers)[:, None, None]
    top_cond = jnp.where(level == layers - 1, pads[None], jnp.float32(0.0))
    sources = top_cond * supply_volts - jnp.where(level == 0, load_current[None], jnp.float32(0.0))
    open_seg = 1.0 - blocked.astype(jnp.float32)
    mobile_x = mobility * open_seg * along_x * inner_x
    mobile_y = mobility * open_seg * along_y * inner_y
    edge_x = from_behind(jnp.stack([cond_xr[:, -1:, :], mobile_x[:, -1:, :]]), "gx", 1)
    edge_y = from_behind(jnp.stack([cond_yr[:, :, -1:], mobile_y[:, :, -1:]]), "gy", 1)
    cond_xl = jnp.concatenate([edge_x[0], cond_xr[:, :-1, :]], 1)
    mobile_xl = jnp.concatenate([edge_x[1], mobile_x[:, :-1, :]], 1)
    cond_yl = jnp.concatenate([edge_y[0], cond_yr[:, :, :-1]], 2)
    mobile_yl = jnp.concatenate([edge_y[1], mobile_y[:, :, :-1]], 2)
    diagonal = cond_xl + cond_xr + cond_yl + cond_yr + via_below + via_above + top_cond
    volts = volts_start
    for sweep in range(SWEEPS):
        padded = with_halo(volts, (("gx", 1), ("gy", 2)), 1)
        lateral = lateral_both(padded, cond_xl, cond_xr, cond_yl, cond_yr)
        volts = (1.0 - damping) * volts + damping * finish(
            lateral, volts, via_below, via_above, sources
        ) / diagonal
    padded = with_halo(volts, (("gx", 1), ("gy", 2)), 1)
    lateral = lateral_both(padded, cond_xl, cond_xr, cond_yl, cond_yr)
    current_x = cond_xr * (volts - padded[:, 2:, 1:-1])
    current_y = cond_yr * (volts - padded[:, 1:-1, 2:])
    current_xl = cond_xl * (padded[:, :-2, 1:-1] - volts)
    current_yl = cond_yl * (padded[:, 1:-1, :-2] - volts)
    resid = finish(lateral, volts, via_below, via_above, sources) - diagonal * volts
    squared = lax.psum(jnp.sum(resid * resid), ("gx", "gy"))
    resid_rms = jnp.sqrt(squared / (layers * total_x * total_y))
    wind_x = mobile_x * wind_factor * current_x
    wind_y = mobile_y * wind_factor * current_y
    wind_xl = mobile_xl * wind_factor * current_xl
    wind_yl = mobile_yl * wind_factor * current_yl
    drift = wind_x - wind_xl + wind_y - wind_yl
    stress = stress_start
    for step in range(STEPS):
        side = with_halo(stress, (("gx", 1), ("gy", 2)), 1)
        stress = (
            stress
            + mobile_x * (side[:, 2:, 1:-1] - stress)
            - mobile_xl * (stress - side[:, :-2, 1:-1])
            + mobile_y * (side[:, 1:-1, 2:] - stress)
            - mobile_yl * (stress - side[:, 1:-1, :-2])
            + drift
        )
    return (volts, stress, resid_rms)


def solution(mesh):
    in_specs = (
        P(None, "gx", "gy"),
        P(None, "gx", "gy"),
        P(None, "gx", "gy"),
        P(None, "gx", "gy"),
        P("gx", "gy"),
        P("gx", "gy"),
        P(None, "gx", "gy"),
        P(None, "gx", "gy"),
        P(None, "gx", "gy"),
        P(),
    )
    out_specs = (P(None, "gx", "gy"), P(None, "gx", "gy"), P())
    return jax.shard_map(body, mesh=mesh, in_specs=in_specs, out_specs=out_specs, check_vma=False)
```

profile of v0, /device:TPU:1, one launch (start us, length us, event | category | flops | bytes accessed | tf_op | source)
XLA Modules:
  0.0 337.8 jit_solution(10733594241635382952)
XLA Ops:
  0.6 0.6 copy-done.17
  1.3 1.8 multiply_multiply_fusion.3
  3.1 0.2 slice_reduce_fusion
  3.4 16.8 %collective-permute-start.3 = (f32[2,8,16,1]{2,1,3,0:T(8,128)S(1)}, f32[2,8,16,1]{2,1,3,0:T(8,128)S(1)}, u32[]{:S(2)}, u32[]{:S(2)}) collective-permute-start(f32[2,8,16,1]{2,1,3,0:T(8,128)S(1)} %pad_maximum_fusion.82), channel_id=1, source_target_pairs={{0,1},{1,2},{2,3},{3,4},{4,5},{5,6},{6,7},{7,8},{8,9},{9,10},{10,1... | collective-permute-start | bytes 3080 | tf_op jit(solution)/shard_map/ppermute | solution.py:19
  20.3 3.1 collective-permute-start
  23.5 3.1 collective-permute-start.1
  26.7 1.4 collective-permute-start.2
  28.1 1.0 fusion.109
  29.3 0.1 copy.82
  29.4 2.0 collective-permute-done.2
  31.5 0.1 pad_maximum_fusion.80
  31.6 3.6 %collective-permute-start.4 = (f32[8,18,1]{2,1,0:T(8,128)S(1)}, f32[8,18,1]{2,1,0:T(8,128)S(1)}, u32[]{:S(2)}, u32[]{:S(2)}) collective-permute-start(f32[8,18,1]{2,1,0:T(8,128)S(1)} %get-tuple-element.25), channel_id=1, source_target_pairs={{0,1},{1,2},{2,3},{3,4},{4,5},{5,6},{6,7},{7,8},{8,9},{9,10},{10,1... | collective-permute-start | bytes 1736 | tf_op jit(solution)/shard_map/ppermute | solution.py:30
  35.2 1.9 collective-permute-start.5
  37.2 2.1 collective-permute-done.4
  39.3 10.8 %collective-permute-done.5 = f32[8,18,1]{2,1,0:T(8,128)S(1)} collective-permute-done((f32[8,18,1]{2,1,0:T(8,128)S(1)}, f32[8,18,1]{2,1,0:T(8,128)S(1)}, u32[]{:S(2)}, u32[]{:S(2)}) %collective-permute-start.5) | collective-permute-done | bytes 608 | tf_op jit(solution)/shard_map/ppermute | solution.py:32
  50.1 0.9 fusion.5
  51.1 2.7 collective-permute-start.6
  53.8 1.3 collective-permute-start.7
  55.1 3.3 collective-permute-done.7
  58.5 0.1 pad_maximum_fusion.77
  58.6 3.5 %collective-permute-start.8 = (f32[8,18,1]{2,1,0:T(8,128)S(1)}, f32[8,18,1]{2,1,0:T(8,128)S(1)}, u32[]{:S(2)}, u32[]{:S(2)}) collective-permute-start(f32[8,18,1]{2,1,0:T(8,128)S(1)} %get-tuple-element.23), channel_id=1, source_target_pairs={{0,1},{1,2},{2,3},{3,4},{4,5},{5,6},{6,7},{7,8},{8,9},{9,10},{10,1... | collective-permute-start | bytes 1736 | tf_op jit(solution)/shard_map/ppermute | solution.py:30
  62.1 1.9 collective-permute-start.9
  64.1 13.5 %collective-permute-done.9 = f32[8,18,1]{2,1,0:T(8,128)S(1)} collective-permute-done((f32[8,18,1]{2,1,0:T(8,128)S(1)}, f32[8,18,1]{2,1,0:T(8,128)S(1)}, u32[]{:S(2)}, u32[]{:S(2)}) %collective-permute-start.9) | collective-permute-done | bytes 608 | tf_op jit(solution)/shard_map/ppermute | solution.py:32
  77.6 0.9 fusion.11
  78.6 3.7 %collective-permute-start.10 = (f32[8,1,1024]{2,1,0:T(1,128)S(1)}, f32[8,1,1024]{2,1,0:T(1,128)S(1)}, u32[]{:S(2)}, u32[]{:S(2)}) collective-permute-start(f32[8,1,1024]{2,1,0:T(1,128)S(1)} %get-tuple-element.39), channel_id=1, source_target_pairs={{0,16},{16,32},{32,48},{48,64},{64,80},{80,96},{96,112},{112,128},... | collective-permute-start | bytes 98312 | tf_op jit(solution)/shard_map/ppermute | solution.py:30
  82.3 1.3 collective-permute-start.11
  83.7 1.3 collective-permute-start.14
  85.0 4.9 %collective-permute-start.15 = (f32[8,1,1024]{2,1,0:T(1,128)S(1)}, f32[8,1,1024]{2,1,0:T(1,128)S(1)}, u32[]{:S(2)}, u32[]{:S(2)}) collective-permute-start(f32[8,1,1024]{2,1,0:T(1,128)S(1)} %get-tuple-element.35), channel_id=1, source_target_pairs={{0,16},{16,32},{32,48},{48,64},{64,80},{80,96},{96,112},{112,128},... | collective-permute-start | bytes 98312 | tf_op jit(solution)/shard_map/ppermute | solution.py:30
  89.9 0.1 pad_maximum_fusion.74
  90.0 2.4 collective-permute-start.12
  92.4 1.9 collective-permute-start.13
  94.5 13.6 %collective-permute-done.13 = f32[8,18,1]{2,1,0:T(8,128)S(1)} collective-permute-done((f32[8,18,1]{2,1,0:T(8,128)S(1)}, f32[8,18,1]{2,1,0:T(8,128)S(1)}, u32[]{:S(2)}, u32[]{:S(2)}) %collective-permute-start.13) | collective-permute-done | bytes 608 | tf_op jit(solution)/shard_map/ppermute | solution.py:32
  108.1 0.9 fusion.17
  109.1 1.3 collective-permute-start.18
  110.4 4.8 %collective-permute-start.19 = (f32[8,1,1024]{2,1,0:T(1,128)S(1)}, f32[8,1,1024]{2,1,0:T(1,128)S(1)}, u32[]{:S(2)}, u32[]{:S(2)}) collective-permute-start(f32[8,1,1024]{2,1,0:T(1,128)S(1)} %get-tuple-element.33), channel_id=1, source_target_pairs={{0,16},{16,32},{32,48},{48,64},{64,80},{80,96},{96,112},{112,128},... | collective-permute-start | bytes 98312 | tf_op jit(solution)/shard_map/ppermute | solution.py:30
  115.2 0.7 pad_maximum_fusion.71
  116.0 1.9 collective-permute-start.16
  117.9 12.4 %collective-permute-start.17 = (f32[8,18,1]{2,1,0:T(8,128)}, f32[8,18,1]{2,1,0:T(8,128)}, u32[]{:S(2)}, u32[]{:S(2)}) collective-permute-start(f32[8,18,1]{2,1,0:T(8,128)} %get-tuple-element.20), channel_id=1, source_target_pairs={{0,1},{1,2},{2,3},{3,4},{4,5},{5,6},{6,7},{7,8},{8,9},{9,10},{10,1... | collective-permute-start | bytes 1736 | tf_op jit(solution)/shard_map/ppermute | solution.py:30
  130.3 0.7 pad_maximum_fusion.68
  131.0 1.9 collective-permute-start.20
  133.0 12.4 %collective-permute-start.21 = (f32[8,18,1]{2,1,0:T(8,128)}, f32[8,18,1]{2,1,0:T(8,128)}, u32[]{:S(2)}, u32[]{:S(2)}) collective-permute-start(f32[8,18,1]{2,1,0:T(8,128)} %get-tuple-element.18), channel_id=1, source_target_pairs={{0,1},{1,2},{2,3},{3,4},{4,5},{5,6},{6,7},{7,8},{8,9},{9,10},{10,1... | collective-permute-start | bytes 1736 | tf_op jit(solution)/shard_map/ppermute | solution.py:30
  145.3 0.1 copy.83
  145.5 0.5 collective-permute-done.20
  146.0 2.5 collective-permute-done.21
  148.4 3.9 %fusion.67 = (f32[8,16,1024]{2,1,0:T(8,128)S(1)}, f32[8,16,1024]{2,1,0:T(8,128)S(1)}) fusion(f32[8,16,1024]{2,1,0:T(8,128)} %param.16, f32[8,18,1]{2,1,0:T(8,128)} %collective-permute-done.17, f32[8,1,1024]{2,1,0:T(1,128)} %copy-done.12, f32[8,1,1024]{2,1,0:T(1,128)} %copy-done.13, f32[8,16,1024]{2,1,0:T(8,128)S(1)} %get-tuple-element.56, ...), kind=kLoop, calls=%fused_computation.104 | loop fusion | flops 6815744 | bytes 6424832 | tf_op jit(solution)/shard_map/add | solution.py:120
  152.4 1.3 collective-permute-start.22
  153.7 5.2 %collective-permute-start.23 = (f32[8,1,1024]{2,1,0:T(1,128)S(1)}, f32[8,1,1024]{2,1,0:T(1,128)S(1)}, u32[]{:S(2)}, u32[]{:S(2)}) collective-permute-start(f32[8,1,1024]{2,1,0:T(1,128)S(1)} %get-tuple-element.31), channel_id=1, source_target_pairs={{0,16},{16,32},{32,48},{48,64},{64,80},{80,96},{96,112},{112,128},... | collective-permute-start | bytes 98312 | tf_op jit(solution)/shard_map/ppermute | solution.py:30
  158.9 1.0 collective-permute-done.23
  159.9 0.1 pad_maximum_fusion.65
  160.0 1.9 collective-permute-start.24
  162.0 14.2 %collective-permute-start.25 = (f32[8,18,1]{2,1,0:T(8,128)S(1)}, f32[8,18,1]{2,1,0:T(8,128)S(1)}, u32[]{:S(2)}, u32[]{:S(2)}) collective-permute-start(f32[8,18,1]{2,1,0:T(8,128)S(1)} %get-tuple-element.16), channel_id=1, source_target_pairs={{0,1},{1,2},{2,3},{3,4},{4,5},{5,6},{6,7},{7,8},{8,9},{9,10},{10,1... | collective-permute-start | bytes 1736 | tf_op jit(solution)/shard_map/ppermute | solution.py:30
  176.1 0.4 collective-permute-done.24
  176.5 1.3 collective-permute-done.25
  177.7 0.8 fusion.40
  178.6 1.3 collective-permute-start.26
  179.9 4.9 %collective-permute-start.27 = (f32[8,1,1024]{2,1,0:T(1,128)S(1)}, f32[8,1,1024]{2,1,0:T(1,128)S(1)}, u32[]{:S(2)}, u32[]{:S(2)}) collective-permute-start(f32[8,1,1024]{2,1,0:T(1,128)S(1)} %get-tuple-element.29), channel_id=1, source_target_pairs={{0,16},{16,32},{32,48},{48,64},{64,80},{80,96},{96,112},{112,128},... | collective-permute-start | bytes 98312 | tf_op jit(solution)/shard_map/ppermute | solution.py:30
  184.8 0.1 fusion.100
  184.9 0.9 collective-permute-done.27
  185.8 0.7 pad_maximum_fusion.62
  186.6 1.9 collective-permute-start.28
  188.5 14.0 %collective-permute-start.29 = (f32[8,18,1]{2,1,0:T(8,128)}, f32[8,18,1]{2,1,0:T(8,128)}, u32[]{:S(2)}, u32[]{:S(2)}) collective-permute-start(f32[8,18,1]{2,1,0:T(8,128)} %get-tuple-element.14), channel_id=1, source_target_pairs={{0,1},{1,2},{2,3},{3,4},{4,5},{5,6},{6,7},{7,8},{8,9},{9,10},{10,1... | collective-permute-start | bytes 1736 | tf_op jit(solution)/shard_map/ppermute | solution.py:30
  202.5 2.4 fusion.23
  204.9 127.4 %psum.7 = f32[]{:T(128)} all-reduce(f32[]{:T(128)} %fusion.23), channel_id=1, replica_groups=mesh['gx'=32,'gy'=16] {'gx','gy'}, use_global_device_ids=true, to_apply=%region_1.2 | all-reduce | flops 1 | bytes 8 | tf_op jit(solution)/shard_map/psum | solution.py:109
  333.1 3.6 %fusion.27 = f32[8,16,1024]{2,1,0:T(8,128)} fusion(f32[8,16,1024]{2,1,0:T(8,128)} %copy-done.3, f32[8,16,1024]{2,1,0:T(8,128)} %copy-done.2, f32[8,18,1]{2,1,0:T(8,128)} %collective-permute-done.29, f32[8,1,1024]{2,1,0:T(1,128)} %copy-done.14, f32[8,1,1024]{2,1,0:T(1,128)} %copy-done.15, f32[8,16,1024]{2,1,0:T(8,128)S(1)} %get-tuple-element.56, ...), kind=kLoop, calls=%fused_computation.40 | loop fusion | flops 3014656 | bytes 3736704 | tf_op jit(solution)/shard_map/add | solution.py:120
  (74 shorter events, 0.9 us)
Async XLA Ops:
  0.6 0.7 copy-start.17
  1.3 22.1 %copy-start.1 = (f32[8,16,1024]{2,1,0:T(8,128)S(1)}, f32[8,16,1024]{2,1,0:T(8,128)}, u32[]{:S(2)}) copy-start(f32[8,16,1024]{2,1,0:T(8,128)} %param.10) | copy-start | bytes 1572868
  3.4 25.9 %collective-permute-start.3 = (f32[2,8,16,1]{2,1,3,0:T(8,128)S(1)}, f32[2,8,16,1]{2,1,3,0:T(8,128)S(1)}, u32[]{:S(2)}, u32[]{:S(2)}) collective-permute-start(f32[2,8,16,1]{2,1,3,0:T(8,128)S(1)} %pad_maximum_fusion.82), channel_id=1, source_target_pairs={{0,1},{1,2},{2,3},{3,4},{4,5},{5,6},{6,7},{7,8},{8,9},{9,10},{10,1... | collective-permute-start | bytes 3080 | tf_op jit(solution)/shard_map/ppermute | solution.py:19
  20.3 16.8 %collective-permute-start = (f32[2,8,1,1024]{3,2,1,0:T(1,128)S(1)}, f32[2,8,1,1024]{3,2,1,0:T(1,128)S(1)}, u32[]{:S(2)}, u32[]{:S(2)}) collective-permute-start(f32[2,8,1,1024]{3,2,1,0:T(1,128)S(1)} %pad_maximum_fusion.81), channel_id=1, source_target_pairs={{0,16},{16,32},{32,48},{48,64},{64,80},{80,96},{96,112},{112,128},... | collective-permute-start | bytes 196616 | tf_op jit(solution)/shard_map/ppermute | solution.py:19
  23.5 5.9 %collective-permute-start.1 = (f32[8,1,1024]{2,1,0:T(1,128)S(1)}, f32[8,1,1024]{2,1,0:T(1,128)S(1)}, u32[]{:S(2)}, u32[]{:S(2)}) collective-permute-start(f32[8,1,1024]{2,1,0:T(1,128)S(1)} %get-tuple-element.49), channel_id=1, source_target_pairs={{0,16},{16,32},{32,48},{48,64},{64,80},{80,96},{96,112},{112,128},... | collective-permute-start | bytes 98312 | tf_op jit(solution)/shard_map/ppermute | solution.py:30
  26.7 2.5 copy-start.16
  26.7 2.5 copy-start.8
  26.7 2.5 copy-start.9
  26.7 4.8 %collective-permute-start.2 = (f32[8,1,1024]{2,1,0:T(1,128)S(1)}, f32[8,1,1024]{2,1,0:T(1,128)S(1)}, u32[]{:S(2)}, u32[]{:S(2)}) collective-permute-start(f32[8,1,1024]{2,1,0:T(1,128)S(1)} %get-tuple-element.50), channel_id=1, source_target_pairs={{16,0},{32,16},{48,32},{64,48},{80,64},{96,80},{112,96},{128,112},... | collective-permute-start | bytes 98312 | tf_op jit(solution)/shard_map/ppermute | solution.py:32
  29.3 20.8 %copy-start.7 = (f32[16,1024]{1,0:T(8,128)S(1)}, f32[16,1024]{1,0:T(8,128)}, u32[]{:S(2)}) copy-start(f32[16,1024]{1,0:T(8,128)} %param.15) | copy-start | bytes 196612
  29.4 20.7 %copy-start.5 = (f32[7,16,1024]{2,1,0:T(8,128)S(1)}, f32[7,16,1024]{2,1,0:T(8,128)}, u32[]{:S(2)}) copy-start(f32[7,16,1024]{2,1,0:T(8,128)} %get-tuple-element.45) | copy-start | bytes 1376260
  29.4 20.7 %copy-start.6 = (f32[7,16,1024]{2,1,0:T(8,128)S(1)}, f32[7,16,1024]{2,1,0:T(8,128)}, u32[]{:S(2)}) copy-start(f32[7,16,1024]{2,1,0:T(8,128)} %get-tuple-element.46) | copy-start | bytes 1376260
  31.6 7.7 %collective-permute-start.4 = (f32[8,18,1]{2,1,0:T(8,128)S(1)}, f32[8,18,1]{2,1,0:T(8,128)S(1)}, u32[]{:S(2)}, u32[]{:S(2)}) collective-permute-start(f32[8,18,1]{2,1,0:T(8,128)S(1)} %get-tuple-element.25), channel_id=1, source_target_pairs={{0,1},{1,2},{2,3},{3,4},{4,5},{5,6},{6,7},{7,8},{8,9},{9,10},{10,1... | collective-permute-start | bytes 1736 | tf_op jit(solution)/shard_map/ppermute | solution.py:30
  35.2 14.8 %collective-permute-start.5 = (f32[8,18,1]{2,1,0:T(8,128)S(1)}, f32[8,18,1]{2,1,0:T(8,128)S(1)}, u32[]{:S(2)}, u32[]{:S(2)}) collective-permute-start(f32[8,18,1]{2,1,0:T(8,128)S(1)} %get-tuple-element.26), channel_id=1, source_target_pairs={{1,0},{2,1},{3,2},{4,3},{5,4},{6,5},{7,6},{8,7},{9,8},{10,9},{11,1... | collective-permute-start | bytes 1736 | tf_op jit(solution)/shard_map/ppermute | solution.py:32
  51.1 4.0 %collective-permute-start.6 = (f32[8,1,1024]{2,1,0:T(1,128)S(1)}, f32[8,1,1024]{2,1,0:T(1,128)S(1)}, u32[]{:S(2)}, u32[]{:S(2)}) collective-permute-start(f32[8,1,1024]{2,1,0:T(1,128)S(1)} %get-tuple-element.43), channel_id=1, source_target_pairs={{0,16},{16,32},{32,48},{48,64},{64,80},{80,96},{96,112},{112,128},... | collective-permute-start | bytes 98312 | tf_op jit(solution)/shard_map/ppermute | solution.py:30
  53.8 4.7 %collective-permute-start.7 = (f32[8,1,1024]{2,1,0:T(1,128)S(1)}, f32[8,1,1024]{2,1,0:T(1,128)S(1)}, u32[]{:S(2)}, u32[]{:S(2)}) collective-permute-start(f32[8,1,1024]{2,1,0:T(1,128)S(1)} %get-tuple-element.44), channel_id=1, source_target_pairs={{16,0},{32,16},{48,32},{64,48},{80,64},{96,80},{112,96},{128,112},... | collective-permute-start | bytes 98312 | tf_op jit(solution)/shard_map/ppermute | solution.py:32
  58.6 5.5 %collective-permute-start.8 = (f32[8,18,1]{2,1,0:T(8,128)S(1)}, f32[8,18,1]{2,1,0:T(8,128)S(1)}, u32[]{:S(2)}, u32[]{:S(2)}) collective-permute-start(f32[8,18,1]{2,1,0:T(8,128)S(1)} %get-tuple-element.23), channel_id=1, source_target_pairs={{0,1},{1,2},{2,3},{3,4},{4,5},{5,6},{6,7},{7,8},{8,9},{9,10},{10,1... | collective-permute-start | bytes 1736 | tf_op jit(solution)/shard_map/ppermute | solution.py:30
  62.1 15.5 %collective-permute-start.9 = (f32[8,18,1]{2,1,0:T(8,128)S(1)}, f32[8,18,1]{2,1,0:T(8,128)S(1)}, u32[]{:S(2)}, u32[]{:S(2)}) collective-permute-start(f32[8,18,1]{2,1,0:T(8,128)S(1)} %get-tuple-element.24), channel_id=1, source_target_pairs={{1,0},{2,1},{3,2},{4,3},{5,4},{6,5},{7,6},{8,7},{9,8},{10,9},{11,1... | collective-permute-start | bytes 1736 | tf_op jit(solution)/shard_map/ppermute | solution.py:32
  77.6 6.0 %copy-start.4 = (f32[8,16,1024]{2,1,0:T(8,128)S(1)}, f32[8,16,1024]{2,1,0:T(8,128)}, u32[]{:S(2)}) copy-start(f32[8,16,1024]{2,1,0:T(8,128)} %param.16) | copy-start | bytes 1572868
  78.6 11.3 %collective-permute-start.10 = (f32[8,1,1024]{2,1,0:T(1,128)S(1)}, f32[8,1,1024]{2,1,0:T(1,128)S(1)}, u32[]{:S(2)}, u32[]{:S(2)}) collective-permute-start(f32[8,1,1024]{2,1,0:T(1,128)S(1)} %get-tuple-element.39), channel_id=1, source_target_pairs={{0,16},{16,32},{32,48},{48,64},{64,80},{80,96},{96,112},{112,128},... | collective-permute-start | bytes 98312 | tf_op jit(solution)/shard_map/ppermute | solution.py:30
  82.3 7.6 %collective-permute-start.11 = (f32[8,1,1024]{2,1,0:T(1,128)S(1)}, f32[8,1,1024]{2,1,0:T(1,128)S(1)}, u32[]{:S(2)}, u32[]{:S(2)}) collective-permute-start(f32[8,1,1024]{2,1,0:T(1,128)S(1)} %get-tuple-element.40), channel_id=1, source_target_pairs={{16,0},{32,16},{48,32},{64,48},{80,64},{96,80},{112,96},{128,112},... | collective-permute-start | bytes 98312 | tf_op jit(solution)/shard_map/ppermute | solution.py:32
  83.7 31.5 %collective-permute-start.14 = (f32[8,1,1024]{2,1,0:T(1,128)S(1)}, f32[8,1,1024]{2,1,0:T(1,128)S(1)}, u32[]{:S(2)}, u32[]{:S(2)}) collective-permute-start(f32[8,1,1024]{2,1,0:T(1,128)S(1)} %get-tuple-element.36), channel_id=1, source_target_pairs={{16,0},{32,16},{48,32},{64,48},{80,64},{96,80},{112,96},{128,112},... | collective-permute-start | bytes 98312 | tf_op jit(solution)/shard_map/ppermute | solution.py:32
  85.0 30.3 %collective-permute-start.15 = (f32[8,1,1024]{2,1,0:T(1,128)S(1)}, f32[8,1,1024]{2,1,0:T(1,128)S(1)}, u32[]{:S(2)}, u32[]{:S(2)}) collective-permute-start(f32[8,1,1024]{2,1,0:T(1,128)S(1)} %get-tuple-element.35), channel_id=1, source_target_pairs={{0,16},{16,32},{32,48},{48,64},{64,80},{80,96},{96,112},{112,128},... | collective-permute-start | bytes 98312 | tf_op jit(solution)/shard_map/ppermute | solution.py:30
  90.0 4.5 %collective-permute-start.12 = (f32[8,18,1]{2,1,0:T(8,128)S(1)}, f32[8,18,1]{2,1,0:T(8,128)S(1)}, u32[]{:S(2)}, u32[]{:S(2)}) collective-permute-start(f32[8,18,1]{2,1,0:T(8,128)S(1)} %get-tuple-element.21), channel_id=1, source_target_pairs={{0,1},{1,2},{2,3},{3,4},{4,5},{5,6},{6,7},{7,8},{8,9},{9,10},{10,1... | collective-permute-start | bytes 1736 | tf_op jit(solution)/shard_map/ppermute | solution.py:30
  92.4 15.7 %collective-permute-start.13 = (f32[8,18,1]{2,1,0:T(8,128)S(1)}, f32[8,18,1]{2,1,0:T(8,128)S(1)}, u32[]{:S(2)}, u32[]{:S(2)}) collective-permute-start(f32[8,18,1]{2,1,0:T(8,128)S(1)} %get-tuple-element.22), channel_id=1, source_target_pairs={{1,0},{2,1},{3,2},{4,3},{5,4},{6,5},{7,6},{8,7},{9,8},{10,9},{11,1... | collective-permute-start | bytes 1736 | tf_op jit(solution)/shard_map/ppermute | solution.py:32
  109.0 93.5 %copy-start = (f32[8,16,1024]{2,1,0:T(8,128)}, f32[8,16,1024]{2,1,0:T(8,128)S(1)}, u32[]{:S(2)}) copy-start(f32[8,16,1024]{2,1,0:T(8,128)S(1)} %fusion.17) | copy-start | bytes 1572868
  109.1 21.2 %collective-permute-start.18 = (f32[8,1,1024]{2,1,0:T(1,128)S(1)}, f32[8,1,1024]{2,1,0:T(1,128)S(1)}, u32[]{:S(2)}, u32[]{:S(2)}) collective-permute-start(f32[8,1,1024]{2,1,0:T(1,128)S(1)} %get-tuple-element.34), channel_id=1, source_target_pairs={{16,0},{32,16},{48,32},{64,48},{80,64},{96,80},{112,96},{128,112},... | collective-permute-start | bytes 98312 | tf_op jit(solution)/shard_map/ppermute | solution.py:32
  110.4 19.9 %collective-permute-start.19 = (f32[8,1,1024]{2,1,0:T(1,128)S(1)}, f32[8,1,1024]{2,1,0:T(1,128)S(1)}, u32[]{:S(2)}, u32[]{:S(2)}) collective-permute-start(f32[8,1,1024]{2,1,0:T(1,128)S(1)} %get-tuple-element.33), channel_id=1, source_target_pairs={{0,16},{16,32},{32,48},{48,64},{64,80},{80,96},{96,112},{112,128},... | collective-permute-start | bytes 98312 | tf_op jit(solution)/shard_map/ppermute | solution.py:30
  115.2 0.8 copy-start.12
  115.2 0.8 copy-start.13
  116.0 29.5 %collective-permute-start.16 = (f32[8,18,1]{2,1,0:T(8,128)}, f32[8,18,1]{2,1,0:T(8,128)}, u32[]{:S(2)}, u32[]{:S(2)}) collective-permute-start(f32[8,18,1]{2,1,0:T(8,128)} %get-tuple-element.19), channel_id=1, source_target_pairs={{1,0},{2,1},{3,2},{4,3},{5,4},{6,5},{7,6},{8,7},{9,8},{10,9},{11,1... | collective-permute-start | bytes 1736 | tf_op jit(solution)/shard_map/ppermute | solution.py:32
  117.9 27.6 %collective-permute-start.17 = (f32[8,18,1]{2,1,0:T(8,128)}, f32[8,18,1]{2,1,0:T(8,128)}, u32[]{:S(2)}, u32[]{:S(2)}) collective-permute-start(f32[8,18,1]{2,1,0:T(8,128)} %get-tuple-element.20), channel_id=1, source_target_pairs={{0,1},{1,2},{2,3},{3,4},{4,5},{5,6},{6,7},{7,8},{8,9},{9,10},{10,1... | collective-permute-start | bytes 1736 | tf_op jit(solution)/shard_map/ppermute | solution.py:30
  130.3 0.8 copy-start.10
  131.0 14.9 %collective-permute-start.20 = (f32[8,18,1]{2,1,0:T(8,128)}, f32[8,18,1]{2,1,0:T(8,128)S(1)}, u32[]{:S(2)}, u32[]{:S(2)}) collective-permute-start(f32[8,18,1]{2,1,0:T(8,128)} %get-tuple-element.17), channel_id=1, source_target_pairs={{1,0},{2,1},{3,2},{4,3},{5,4},{6,5},{7,6},{8,7},{9,8},{10,9},{11,1... | collective-permute-start | bytes 1736 | tf_op jit(solution)/shard_map/ppermute | solution.py:32
  133.0 15.5 %collective-permute-start.21 = (f32[8,18,1]{2,1,0:T(8,128)}, f32[8,18,1]{2,1,0:T(8,128)}, u32[]{:S(2)}, u32[]{:S(2)}) collective-permute-start(f32[8,18,1]{2,1,0:T(8,128)} %get-tuple-element.18), channel_id=1, source_target_pairs={{0,1},{1,2},{2,3},{3,4},{4,5},{5,6},{6,7},{7,8},{8,9},{9,10},{10,1... | collective-permute-start | bytes 1736 | tf_op jit(solution)/shard_map/ppermute | solution.py:30
  152.4 26.2 %copy-start.3 = (f32[8,16,1024]{2,1,0:T(8,128)}, f32[8,16,1024]{2,1,0:T(8,128)S(1)}, u32[]{:S(2)}) copy-start(f32[8,16,1024]{2,1,0:T(8,128)S(1)} %get-tuple-element.10) | copy-start | bytes 1572868
  152.4 6.5 %collective-permute-start.22 = (f32[8,1,1024]{2,1,0:T(1,128)S(1)}, f32[8,1,1024]{2,1,0:T(1,128)S(1)}, u32[]{:S(2)}, u32[]{:S(2)}) collective-permute-start(f32[8,1,1024]{2,1,0:T(1,128)S(1)} %get-tuple-element.32), channel_id=1, source_target_pairs={{16,0},{32,16},{48,32},{64,48},{80,64},{96,80},{112,96},{128,112},... | collective-permute-start | bytes 98312 | tf_op jit(solution)/shard_map/ppermute | solution.py:32
  153.7 6.2 %collective-permute-start.23 = (f32[8,1,1024]{2,1,0:T(1,128)S(1)}, f32[8,1,1024]{2,1,0:T(1,128)S(1)}, u32[]{:S(2)}, u32[]{:S(2)}) collective-permute-start(f32[8,1,1024]{2,1,0:T(1,128)S(1)} %get-tuple-element.31), channel_id=1, source_target_pairs={{0,16},{16,32},{32,48},{48,64},{64,80},{80,96},{96,112},{112,128},... | collective-permute-start | bytes 98312 | tf_op jit(solution)/shard_map/ppermute | solution.py:30
  160.0 16.5 %collective-permute-start.24 = (f32[8,18,1]{2,1,0:T(8,128)S(1)}, f32[8,18,1]{2,1,0:T(8,128)S(1)}, u32[]{:S(2)}, u32[]{:S(2)}) collective-permute-start(f32[8,18,1]{2,1,0:T(8,128)S(1)} %get-tuple-element.15), channel_id=1, source_target_pairs={{1,0},{2,1},{3,2},{4,3},{5,4},{6,5},{7,6},{8,7},{9,8},{10,9},{11,1... | collective-permute-start | bytes 1736 | tf_op jit(solution)/shard_map/ppermute | solution.py:32
  162.0 15.8 %collective-permute-start.25 = (f32[8,18,1]{2,1,0:T(8,128)S(1)}, f32[8,18,1]{2,1,0:T(8,128)S(1)}, u32[]{:S(2)}, u32[]{:S(2)}) collective-permute-start(f32[8,18,1]{2,1,0:T(8,128)S(1)} %get-tuple-element.16), channel_id=1, source_target_pairs={{0,1},{1,2},{2,3},{3,4},{4,5},{5,6},{6,7},{7,8},{8,9},{9,10},{10,1... | collective-permute-start | bytes 1736 | tf_op jit(solution)/shard_map/ppermute | solution.py:30
  178.6 7.2 %copy-start.2 = (f32[8,16,1024]{2,1,0:T(8,128)}, f32[8,16,1024]{2,1,0:T(8,128)S(1)}, u32[]{:S(2)}) copy-start(f32[8,16,1024]{2,1,0:T(8,128)S(1)} %fusion.40) | copy-start | bytes 1572868
  178.6 6.3 %collective-permute-start.26 = (f32[8,1,1024]{2,1,0:T(1,128)S(1)}, f32[8,1,1024]{2,1,0:T(1,128)S(1)}, u32[]{:S(2)}, u32[]{:S(2)}) collective-permute-start(f32[8,1,1024]{2,1,0:T(1,128)S(1)} %get-tuple-element.30), channel_id=1, source_target_pairs={{16,0},{32,16},{48,32},{64,48},{80,64},{96,80},{112,96},{128,112},... | collective-permute-start | bytes 98312 | tf_op jit(solution)/shard_map/ppermute | solution.py:32
  179.9 5.9 %collective-permute-start.27 = (f32[8,1,1024]{2,1,0:T(1,128)S(1)}, f32[8,1,1024]{2,1,0:T(1,128)S(1)}, u32[]{:S(2)}, u32[]{:S(2)}) collective-permute-start(f32[8,1,1024]{2,1,0:T(1,128)S(1)} %get-tuple-element.29), channel_id=1, source_target_pairs={{0,16},{16,32},{32,48},{48,64},{64,80},{80,96},{96,112},{112,128},... | collective-permute-start | bytes 98312 | tf_op jit(solution)/shard_map/ppermute | solution.py:30
  184.9 17.6 %copy-start.11 = (f32[8,1,1024]{2,1,0:T(1,128)S(1)}, f32[8,1,1024]{2,1,0:T(1,128)}, u32[]{:S(2)}) copy-start(f32[8,1,1024]{2,1,0:T(1,128)} %copy-done.10) | copy-start | bytes 98308
  184.9 1.6 copy-start.14
  185.8 0.8 copy-start.15
  186.6 146.5 %collective-permute-start.28 = (f32[8,18,1]{2,1,0:T(8,128)}, f32[8,18,1]{2,1,0:T(8,128)}, u32[]{:S(2)}, u32[]{:S(2)}) collective-permute-start(f32[8,18,1]{2,1,0:T(8,128)} %get-tuple-element.13), channel_id=1, source_target_pairs={{1,0},{2,1},{3,2},{4,3},{5,4},{6,5},{7,6},{8,7},{9,8},{10,9},{11,1... | collective-permute-start | bytes 1736 | tf_op jit(solution)/shard_map/ppermute | solution.py:32
  188.5 144.6 %collective-permute-start.29 = (f32[8,18,1]{2,1,0:T(8,128)}, f32[8,18,1]{2,1,0:T(8,128)}, u32[]{:S(2)}, u32[]{:S(2)}) collective-permute-start(f32[8,18,1]{2,1,0:T(8,128)} %get-tuple-element.14), channel_id=1, source_target_pairs={{0,1},{1,2},{2,3},{3,4},{4,5},{5,6},{6,7},{7,8},{8,9},{9,10},{10,1... | collective-permute-start | bytes 1736 | tf_op jit(solution)/shard_map/ppermute | solution.py:30
where the time goes:
time: 339 us; the launch traced here: 338 us
  starting transfers between devices  134 us (40%)
  blocking collectives  127 us (37%)
  waiting for transfers between devices  51.9 us (15%)
  other arithmetic  18.1 us (5%)
    psum x1, blocking collectives, body(): squared = lax.psum(jnp.sum(resid * resid), ('gx', 'gy'))  127 us
    ppermute x14, starting transfers between devices, with_halo(): lax.ppermute(tail, axis, [(i, (i + 1) % count) for i in range(ends)])  91.7 us
    ppermute x14, waiting for transfers between devices, with_halo(): lax.ppermute(head, axis, [((i + 1) % count, i) for i in range(ends)])  44.2 us
    ppermute x14, starting transfers between devices, with_halo(): lax.ppermute(head, axis, [((i + 1) % count, i) for i in range(ends)])  22.6 us
    ppermute x2, starting transfers between devices, from_behind(): lax.ppermute(value, axis, [(source, source + steps) for source in range(i...  20 us
    add x3, other arithmetic, body(): stress + mobile_x * (side[:, 2:, 1:-1] - stress)  8.37 us
    ppermute x14, waiting for transfers between devices, with_halo(): lax.ppermute(tail, axis, [(i, (i + 1) % count) for i in range(ends)])  7.72 us
  transfers between devices with their start and end apart: 30, of which 12 were waited for; matrix products, arithmetic and copies ran while one was open for 2% of the time, Pallas kernels for 0%

commit v1 on v0

--- a/solution.py
+++ b/solution.py
@@ -5,6 +5,18 @@
 
 SWEEPS = 3
 STEPS = 3
+
+
+X = ("z_lo", "x")
+Y = ("y", "z_hi", "core")
+
+
+def sum_all(value):
+    for axes in (("z_hi", "z_lo"), ("x", "y", "core")):
+        count = lax.axis_size(axes)
+        held = jnp.broadcast_to(value, (count, 8, 128))
+        value = jnp.sum(lax.all_to_all(held, axes, 0, 0)[:, 0, 0])
+    return value
 
 
 damping = 0.8
@@ -64,10 +76,10 @@
     layer_dirs,
 ):
     layers, rows_x, rows_y = seg_cond.shape
-    total_x = rows_x * lax.axis_size("gx")
-    total_y = rows_y * lax.axis_size("gy")
-    index_x = lax.axis_index("gx") * rows_x + jnp.arange(rows_x, dtype=jnp.int32)
-    index_y = lax.axis_index("gy") * rows_y + jnp.arange(rows_y, dtype=jnp.int32)
+    total_x = rows_x * lax.axis_size(X)
+    total_y = rows_y * lax.axis_size(Y)
+    index_x = lax.axis_index(X) * rows_x + jnp.arange(rows_x, dtype=jnp.int32)
+    index_y = lax.axis_index(Y) * rows_y + jnp.arange(rows_y, dtype=jnp.int32)
     inner_x = (index_x < total_x - 1).astype(jnp.float32)[None, :, None]
     inner_y = (index_y < total_y - 1).astype(jnp.float32)[None, None, :]
     along_y = layer_dirs.astype(jnp.float32)[:, None, None]
@@ -85,8 +97,8 @@
     open_seg = 1.0 - blocked.astype(jnp.float32)
     mobile_x = mobility * open_seg * along_x * inner_x
     mobile_y = mobility * open_seg * along_y * inner_y
-    edge_x = from_behind(jnp.stack([cond_xr[:, -1:, :], mobile_x[:, -1:, :]]), "gx", 1)
-    edge_y = from_behind(jnp.stack([cond_yr[:, :, -1:], mobile_y[:, :, -1:]]), "gy", 1)
+    edge_x = from_behind(jnp.stack([cond_xr[:, -1:, :], mobile_x[:, -1:, :]]), X, 1)
+    edge_y = from_behind(jnp.stack([cond_yr[:, :, -1:], mobile_y[:, :, -1:]]), Y, 1)
     cond_xl = jnp.concatenate([edge_x[0], cond_xr[:, :-1, :]], 1)
     mobile_xl = jnp.concatenate([edge_x[1], mobile_x[:, :-1, :]], 1)
     cond_yl = jnp.concatenate([edge_y[0], cond_yr[:, :, :-1]], 2)
@@ -94,19 +106,19 @@
     diagonal = cond_xl + cond_xr + cond_yl + cond_yr + via_below + via_above + top_cond
     volts = volts_start
     for sweep in range(SWEEPS):
-        padded = with_halo(volts, (("gx", 1), ("gy", 2)), 1)
+        padded = with_halo(volts, ((X, 1), (Y, 2)), 1)
         lateral = lateral_both(padded, cond_xl, cond_xr, cond_yl, cond_yr)
         volts = (1.0 - damping) * volts + damping * finish(
             lateral, volts, via_below, via_above, sources
         ) / diagonal
-    padded = with_halo(volts, (("gx", 1), ("gy", 2)), 1)
+    padded = with_halo(volts, ((X, 1), (Y, 2)), 1)
     lateral = lateral_both(padded, cond_xl, cond_xr, cond_yl, cond_yr)
     current_x = cond_xr * (volts - padded[:, 2:, 1:-1])
     current_y = cond_yr * (volts - padded[:, 1:-1, 2:])
     current_xl = cond_xl * (padded[:, :-2, 1:-1] - volts)
     current_yl = cond_yl * (padded[:, 1:-1, :-2] - volts)
     resid = finish(lateral, volts, via_below, via_above, sources) - diagonal * volts
-    squared = lax.psum(jnp.sum(resid * resid), ("gx", "gy"))
+    squared = sum_all(jnp.sum(resid * resid))
     resid_rms = jnp.sqrt(squared / (layers * total_x * total_y))
     wind_x = mobile_x * wind_factor * current_x
     wind_y = mobile_y * wind_factor * current_y
@@ -115,7 +127,7 @@
     drift = wind_x - wind_xl + wind_y - wind_yl
     stress = stress_start
     for step in range(STEPS):
-        side = with_halo(stress, (("gx", 1), ("gy", 2)), 1)
+        side = with_halo(stress, ((X, 1), (Y, 2)), 1)
         stress = (
             stress
             + mobile_x * (side[:, 2:, 1:-1] - stress)
@@ -129,16 +141,17 @@
 
 def solution(mesh):
     in_specs = (
-        P(None, "gx", "gy"),
-        P(None, "gx", "gy"),
-        P(None, "gx", "gy"),
-        P(None, "gx", "gy"),
-        P("gx", "gy"),
-        P("gx", "gy"),
-        P(None, "gx", "gy"),
-        P(None, "gx", "gy"),
-        P(None, "gx", "gy"),
+        P(None, X, Y),
+        P(None, X, Y),
+        P(None, X, Y),
+        P(None, X, Y),
+        P(X, Y),
+        P(X, Y),
+        P(None, X, Y),
+        P(None, X, Y),
+        P(None, X, Y),
         P(),
     )
-    out_specs = (P(None, "gx", "gy"), P(None, "gx", "gy"), P())
-    return jax.shard_map(body, mesh=mesh, in_specs=in_specs, out_specs=out_specs, check_vma=False)
+    out_specs = (P(None, X, Y), P(None, X, Y), P())
+    fine = jax.sharding.Mesh(mesh.devices.reshape(8, 4, 4, 2, 2), X + Y)
+    return jax.shard_map(body, mesh=fine, in_specs=in_specs, out_specs=out_specs, check_vma=False)

time: 339 us -> 255 us (0.75)
  blocking collectives: 127 us -> 0 us
  starting transfers between devices: 134 us -> 167 us
  waiting for transfers between devices: 51.9 us -> 56.5 us
    psum x1 -> x0, blocking collectives: 127 us -> none  [body(): squared = lax.psum(jnp.sum(resid * resid), ('gx', 'gy'))]
    all_to_all x0 -> x2, starting transfers between devices: none -> 35.3 us  [sum_all(): value = jnp.sum(lax.all_to_all(held, axes, 0, 0)[:, 0, 0])]
    all_to_all x0 -> x2, waiting for transfers between devices: none -> 6.24 us  [sum_all(): value = jnp.sum(lax.all_to_all(held, axes, 0, 0)[:, 0, 0])]
  transfers between devices with their start and end apart: 30 -> 32, of which waited for: 12 -> 11; matrix products, arithmetic and copies ran while one was open for 2% -> 6% of each run, Pallas kernels for 0% -> 0%
where the time goes in v1:
time: 255 us; the launch traced here: 252 us
  starting transfers between devices  167 us (65%)
  waiting for transfers between devices  56.5 us (22%)
  other arithmetic  20 us (8%)
  local copies, waits for them, and re-layouts  5.5 us (2%)
  between operations  3.27 us (1%)
    ppermute x14, starting transfers between devices, with_halo(): lax.ppermute(tail, axis, [(i, (i + 1) % count) for i in range(ends)])  89.3 us
    ppermute x14, waiting for transfers between devices, with_halo(): lax.ppermute(head, axis, [((i + 1) % count, i) for i in range(ends)])  43.8 us
    all_to_all x2, starting transfers between devices, sum_all(): value = jnp.sum(lax.all_to_all(held, axes, 0, 0)[:, 0, 0])  35.3 us
    ppermute x14, starting transfers between devices, with_halo(): lax.ppermute(head, axis, [((i + 1) % count, i) for i in range(ends)])  22.6 us
    ppermute x2, starting transfers between devices, from_behind(): lax.ppermute(value, axis, [(source, source + steps) for source in range(i...  20 us
    add x3, other arithmetic, body(): stress + mobile_x * (side[:, 2:, 1:-1] - stress)  8.91 us
    ppermute x14, waiting for transfers between devices, with_halo(): lax.ppermute(tail, axis, [(i, (i + 1) % count) for i in range(ends)])  6.47 us
    all_to_all x2, waiting for transfers between devices, sum_all(): value = jnp.sum(lax.all_to_all(held, axes, 0, 0)[:, 0, 0])  6.24 us
  transfers between devices with their start and end apart: 32, of which 11 were waited for; matrix products, arithmetic and copies ran while one was open for 6% of the time, Pallas kernels for 0%

profile of v1, /device:TPU:1, one launch (start us, length us, event | category | flops | bytes accessed | tf_op | source)
XLA Modules:
  0.0 252.4 jit_solution(16081834427744736000)
XLA Ops:
  0.6 0.6 copy-done.19
  1.3 1.8 multiply_multiply_fusion.3
  3.1 0.2 slice_reduce_fusion
  3.4 16.8 %collective-permute-start.3 = (f32[2,8,16,1]{2,1,3,0:T(8,128)S(1)}, f32[2,8,16,1]{2,1,3,0:T(8,128)S(1)}, u32[]{:S(2)}, u32[]{:S(2)}) collective-permute-start(f32[2,8,16,1]{2,1,3,0:T(8,128)S(1)} %pad_maximum_fusion.82), channel_id=1, source_target_pairs={{0,1},{1,2},{2,3},{3,4},{4,5},{5,6},{6,7},{7,8},{8,9},{9,10},{10,1... | collective-permute-start | bytes 3080 | tf_op jit(solution)/shard_map/ppermute | solution.py:31
  20.3 3.1 %collective-permute-start = (f32[2,8,1,1024]{3,2,1,0:T(1,128)S(1)}, f32[2,8,1,1024]{3,2,1,0:T(1,128)S(1)}, u32[]{:S(2)}, u32[]{:S(2)}) collective-permute-start(f32[2,8,1,1024]{3,2,1,0:T(1,128)S(1)} %pad_maximum_fusion.81), channel_id=1, source_target_pairs={{0,16},{16,32},{32,48},{48,64},{64,80},{80,96},{96,112},{112,128},... | collective-permute-start | bytes 196616 | tf_op jit(solution)/shard_map/ppermute | solution.py:31
  23.5 3.1 %collective-permute-start.1 = (f32[8,1,1024]{2,1,0:T(1,128)S(1)}, f32[8,1,1024]{2,1,0:T(1,128)S(1)}, u32[]{:S(2)}, u32[]{:S(2)}) collective-permute-start(f32[8,1,1024]{2,1,0:T(1,128)S(1)} %get-tuple-element.55), channel_id=1, source_target_pairs={{0,16},{16,32},{32,48},{48,64},{64,80},{80,96},{96,112},{112,128},... | collective-permute-start | bytes 98312 | tf_op jit(solution)/shard_map/ppermute | solution.py:42
  26.7 1.4 collective-permute-start.2
  28.1 1.0 fusion.109
  29.3 0.1 copy.146
  29.4 2.0 collective-permute-done.2
  31.6 3.6 %collective-permute-start.4 = (f32[8,18,1]{2,1,0:T(8,128)S(1)}, f32[8,18,1]{2,1,0:T(8,128)S(1)}, u32[]{:S(2)}, u32[]{:S(2)}) collective-permute-start(f32[8,18,1]{2,1,0:T(8,128)S(1)} %get-tuple-element.31), channel_id=1, source_target_pairs={{0,1},{1,2},{2,3},{3,4},{4,5},{5,6},{6,7},{7,8},{8,9},{9,10},{10,1... | collective-permute-start | bytes 1736 | tf_op jit(solution)/shard_map/ppermute | solution.py:42
  35.2 1.9 collective-permute-start.5
  37.2 2.1 collective-permute-done.4
  39.3 10.8 %collective-permute-done.5 = f32[8,18,1]{2,1,0:T(8,128)S(1)} collective-permute-done((f32[8,18,1]{2,1,0:T(8,128)S(1)}, f32[8,18,1]{2,1,0:T(8,128)S(1)}, u32[]{:S(2)}, u32[]{:S(2)}) %collective-permute-start.5) | collective-permute-done | bytes 608 | tf_op jit(solution)/shard_map/ppermute | solution.py:44
  50.1 0.9 fusion.5
  51.1 2.7 %collective-permute-start.6 = (f32[8,1,1024]{2,1,0:T(1,128)S(1)}, f32[8,1,1024]{2,1,0:T(1,128)S(1)}, u32[]{:S(2)}, u32[]{:S(2)}) collective-permute-start(f32[8,1,1024]{2,1,0:T(1,128)S(1)} %get-tuple-element.49), channel_id=1, source_target_pairs={{0,16},{16,32},{32,48},{48,64},{64,80},{80,96},{96,112},{112,128},... | collective-permute-start | bytes 98312 | tf_op jit(solution)/shard_map/ppermute | solution.py:42
  53.8 1.3 collective-permute-start.7
  55.1 3.3 %collective-permute-done.7 = f32[8,1,1024]{2,1,0:T(1,128)S(1)} collective-permute-done((f32[8,1,1024]{2,1,0:T(1,128)S(1)}, f32[8,1,1024]{2,1,0:T(1,128)S(1)}, u32[]{:S(2)}, u32[]{:S(2)}) %collective-permute-start.7) | collective-permute-done | bytes 32800 | tf_op jit(solution)/shard_map/ppermute | solution.py:44
  58.6 3.5 %collective-permute-start.8 = (f32[8,18,1]{2,1,0:T(8,128)S(1)}, f32[8,18,1]{2,1,0:T(8,128)S(1)}, u32[]{:S(2)}, u32[]{:S(2)}) collective-permute-start(f32[8,18,1]{2,1,0:T(8,128)S(1)} %get-tuple-element.29), channel_id=1, source_target_pairs={{0,1},{1,2},{2,3},{3,4},{4,5},{5,6},{6,7},{7,8},{8,9},{9,10},{10,1... | collective-permute-start | bytes 1736 | tf_op jit(solution)/shard_map/ppermute | solution.py:42
  62.1 1.9 collective-permute-start.9
  64.1 13.5 %collective-permute-done.9 = f32[8,18,1]{2,1,0:T(8,128)S(1)} collective-permute-done((f32[8,18,1]{2,1,0:T(8,128)S(1)}, f32[8,18,1]{2,1,0:T(8,128)S(1)}, u32[]{:S(2)}, u32[]{:S(2)}) %collective-permute-start.9) | collective-permute-done | bytes 608 | tf_op jit(solution)/shard_map/ppermute | solution.py:44
  77.6 0.9 fusion.11
  78.6 3.7 %collective-permute-start.10 = (f32[8,1,1024]{2,1,0:T(1,128)S(1)}, f32[8,1,1024]{2,1,0:T(1,128)S(1)}, u32[]{:S(2)}, u32[]{:S(2)}) collective-permute-start(f32[8,1,1024]{2,1,0:T(1,128)S(1)} %get-tuple-element.45), channel_id=1, source_target_pairs={{0,16},{16,32},{32,48},{48,64},{64,80},{80,96},{96,112},{112,128},... | collective-permute-start | bytes 98312 | tf_op jit(solution)/shard_map/ppermute | solution.py:42
  82.3 1.3 collective-permute-start.11
  83.7 1.3 collective-permute-start.14
  85.0 4.9 %collective-permute-start.15 = (f32[8,1,1024]{2,1,0:T(1,128)S(1)}, f32[8,1,1024]{2,1,0:T(1,128)S(1)}, u32[]{:S(2)}, u32[]{:S(2)}) collective-permute-start(f32[8,1,1024]{2,1,0:T(1,128)S(1)} %get-tuple-element.41), channel_id=1, source_target_pairs={{0,16},{16,32},{32,48},{48,64},{64,80},{80,96},{96,112},{112,128},... | collective-permute-start | bytes 98312 | tf_op jit(solution)/shard_map/ppermute | solution.py:42
  89.9 0.1 pad_maximum_fusion.74
  90.0 2.4 collective-permute-start.12
  92.4 1.9 collective-permute-start.13
  94.5 13.6 %collective-permute-done.13 = f32[8,18,1]{2,1,0:T(8,128)S(1)} collective-permute-done((f32[8,18,1]{2,1,0:T(8,128)S(1)}, f32[8,18,1]{2,1,0:T(8,128)S(1)}, u32[]{:S(2)}, u32[]{:S(2)}) %collective-permute-start.13) | collective-permute-done | bytes 608 | tf_op jit(solution)/shard_map/ppermute | solution.py:44
  108.1 0.9 fusion.17
  109.1 1.3 collective-permute-start.18
  110.4 4.8 %collective-permute-start.19 = (f32[8,1,1024]{2,1,0:T(1,128)S(1)}, f32[8,1,1024]{2,1,0:T(1,128)S(1)}, u32[]{:S(2)}, u32[]{:S(2)}) collective-permute-start(f32[8,1,1024]{2,1,0:T(1,128)S(1)} %get-tuple-element.39), channel_id=1, source_target_pairs={{0,16},{16,32},{32,48},{48,64},{64,80},{80,96},{96,112},{112,128},... | collective-permute-start | bytes 98312 | tf_op jit(solution)/shard_map/ppermute | solution.py:42
  115.2 0.7 pad_maximum_fusion.71
  116.0 1.9 collective-permute-start.16
  117.9 12.4 %collective-permute-start.17 = (f32[8,18,1]{2,1,0:T(8,128)}, f32[8,18,1]{2,1,0:T(8,128)}, u32[]{:S(2)}, u32[]{:S(2)}) collective-permute-start(f32[8,18,1]{2,1,0:T(8,128)} %get-tuple-element.26), channel_id=1, source_target_pairs={{0,1},{1,2},{2,3},{3,4},{4,5},{5,6},{6,7},{7,8},{8,9},{9,10},{10,1... | collective-permute-start | bytes 1736 | tf_op jit(solution)/shard_map/ppermute | solution.py:42
  130.3 0.8 pad_maximum_fusion.68
  131.1 1.9 collective-permute-start.20
  133.0 12.4 %collective-permute-start.21 = (f32[8,18,1]{2,1,0:T(8,128)}, f32[8,18,1]{2,1,0:T(8,128)}, u32[]{:S(2)}, u32[]{:S(2)}) collective-permute-start(f32[8,18,1]{2,1,0:T(8,128)} %get-tuple-element.24), channel_id=1, source_target_pairs={{0,1},{1,2},{2,3},{3,4},{4,5},{5,6},{6,7},{7,8},{8,9},{9,10},{10,1... | collective-permute-start | bytes 1736 | tf_op jit(solution)/shard_map/ppermute | solution.py:42
  145.3 0.1 copy.147
  145.5 0.5 collective-permute-done.20
  146.0 2.5 collective-permute-done.21
  148.5 4.6 %fusion.67 = (f32[8,16,1024]{2,1,0:T(8,128)S(1)}, f32[8,16,1024]{2,1,0:T(8,128)}) fusion(f32[8,16,1024]{2,1,0:T(8,128)} %param.16, f32[8,18,1]{2,1,0:T(8,128)} %collective-permute-done.17, f32[8,1,1024]{2,1,0:T(1,128)} %copy-done.12, f32[8,1,1024]{2,1,0:T(1,128)} %copy-done.13, f32[8,16,1024]{2,1,0:T(8,128)S(1)} %get-tuple-element.62, ...), kind=kLoop, calls=%fused_computation.104 | loop fusion | flops 6815744 | bytes 6424832 | tf_op jit(solution)/shard_map/add | solution.py:132
  153.1 1.3 collective-permute-start.22
  154.4 5.2 %collective-permute-start.23 = (f32[8,1,1024]{2,1,0:T(1,128)S(1)}, f32[8,1,1024]{2,1,0:T(1,128)S(1)}, u32[]{:S(2)}, u32[]{:S(2)}) collective-permute-start(f32[8,1,1024]{2,1,0:T(1,128)S(1)} %get-tuple-element.37), channel_id=1, source_target_pairs={{0,16},{16,32},{32,48},{48,64},{64,80},{80,96},{96,112},{112,128},... | collective-permute-start | bytes 98312 | tf_op jit(solution)/shard_map/ppermute | solution.py:42
  159.7 0.9 collective-permute-done.23
  160.6 0.8 pad_maximum_fusion.65
  161.4 1.9 collective-permute-start.24
  163.3 14.2 %collective-permute-start.25 = (f32[8,18,1]{2,1,0:T(8,128)}, f32[8,18,1]{2,1,0:T(8,128)}, u32[]{:S(2)}, u32[]{:S(2)}) collective-permute-start(f32[8,18,1]{2,1,0:T(8,128)} %get-tuple-element.22), channel_id=1, source_target_pairs={{0,1},{1,2},{2,3},{3,4},{4,5},{5,6},{6,7},{7,8},{8,9},{9,10},{10,1... | collective-permute-start | bytes 1736 | tf_op jit(solution)/shard_map/ppermute | solution.py:42
  177.5 2.4 fusion.23
  179.9 1.3 broadcast_in_dim.48
  181.2 30.6 %all-to-all-start = ((f32[16,8,128]{2,1,0:T(8,128)}), f32[16,8,128]{2,1,0:T(8,128)S(1)}, u32[]{:S(2)}, u32[]{:S(2)}) async-start(f32[16,8,128]{2,1,0:T(8,128)} %broadcast_in_dim.48), calls=%async_computation | async-start | bytes 131072 | tf_op jit(solution)/shard_map/all_to_all | solution.py:18
  211.8 2.9 %fusion.40 = f32[8,16,1024]{2,1,0:T(8,128)S(1)} fusion(f32[8,16,1024]{2,1,0:T(8,128)} %get-tuple-element.16, f32[8,16,1024]{2,1,0:T(8,128)} %copy-done.2, f32[8,18,1]{2,1,0:T(8,128)} %collective-permute-done.25, f32[8,1,1024]{2,1,0:T(1,128)S(1)} %copy-done.15, f32[8,1,1024]{2,1,0:T(1,128)S(1)} %copy-done.17, f32[8,16,1024]{2,1,0:T(8,128)S(1)} %get-tuple-element.62, ...), kind=kLoop, calls=%fused_computation.61 | loop fusion | flops 3014656 | bytes 3736704 | tf_op jit(solution)/shard_map/add | solution.py:132
  214.7 1.3 collective-permute-start.26
  216.0 4.1 %collective-permute-start.27 = (f32[8,1,1024]{2,1,0:T(1,128)S(1)}, f32[8,1,1024]{2,1,0:T(1,128)S(1)}, u32[]{:S(2)}, u32[]{:S(2)}) collective-permute-start(f32[8,1,1024]{2,1,0:T(1,128)S(1)} %get-tuple-element.35), channel_id=1, source_target_pairs={{0,16},{16,32},{32,48},{48,64},{64,80},{80,96},{96,112},{112,128},... | collective-permute-start | bytes 98312 | tf_op jit(solution)/shard_map/ppermute | solution.py:42
  220.2 1.0 collective-permute-done.27
  221.3 1.9 collective-permute-start.28
  223.2 12.4 %collective-permute-start.29 = (f32[8,18,1]{2,1,0:T(8,128)S(1)}, f32[8,18,1]{2,1,0:T(8,128)S(1)}, u32[]{:S(2)}, u32[]{:S(2)}) collective-permute-start(f32[8,18,1]{2,1,0:T(8,128)S(1)} %get-tuple-element.20), channel_id=1, source_target_pairs={{0,1},{1,2},{2,3},{3,4},{4,5},{5,6},{6,7},{7,8},{8,9},{9,10},{10,1... | collective-permute-start | bytes 1736 | tf_op jit(solution)/shard_map/ppermute | solution.py:42
  235.6 0.6 slice_reduce_fusion.3
  236.2 1.3 broadcast_in_dim.49
  237.5 4.7 %all-to-all-start.1 = ((f32[32,8,128]{2,1,0:T(8,128)}), f32[32,8,128]{2,1,0:T(8,128)S(1)}, u32[]{:S(2)}, u32[]{:S(2)}) async-start(f32[32,8,128]{2,1,0:T(8,128)} %broadcast_in_dim.49), calls=%async_computation.1 | async-start | bytes 262144 | tf_op jit(solution)/shard_map/all_to_all | solution.py:18
  242.2 1.4 fusion.27
  243.7 6.2 %all-to-all-done.1 = f32[32,8,128]{2,1,0:T(8,128)S(1)} async-done(((f32[32,8,128]{2,1,0:T(8,128)}), f32[32,8,128]{2,1,0:T(8,128)S(1)}, u32[]{:S(2)}, u32[]{:S(2)}) %all-to-all-start.1) | async-done | bytes 131104 | tf_op jit(solution)/shard_map/all_to_all | solution.py:18
  249.9 0.6 slice_reduce_fusion.2
  (85 shorter events, 1.3 us)
Async XLA Ops:
  0.6 0.7 copy-start.19
  1.3 22.1 %copy-start.1 = (f32[8,16,1024]{2,1,0:T(8,128)S(1)}, f32[8,16,1024]{2,1,0:T(8,128)}, u32[]{:S(2)}) copy-start(f32[8,16,1024]{2,1,0:T(8,128)} %param.10) | copy-start | bytes 1572868
  3.4 25.9 %collective-permute-start.3 = (f32[2,8,16,1]{2,1,3,0:T(8,128)S(1)}, f32[2,8,16,1]{2,1,3,0:T(8,128)S(1)}, u32[]{:S(2)}, u32[]{:S(2)}) collective-permute-start(f32[2,8,16,1]{2,1,3,0:T(8,128)S(1)} %pad_maximum_fusion.82), channel_id=1, source_target_pairs={{0,1},{1,2},{2,3},{3,4},{4,5},{5,6},{6,7},{7,8},{8,9},{9,10},{10,1... | collective-permute-start | bytes 3080 | tf_op jit(solution)/shard_map/ppermute | solution.py:31
  20.3 16.8 %collective-permute-start = (f32[2,8,1,1024]{3,2,1,0:T(1,128)S(1)}, f32[2,8,1,1024]{3,2,1,0:T(1,128)S(1)}, u32[]{:S(2)}, u32[]{:S(2)}) collective-permute-start(f32[2,8,1,1024]{3,2,1,0:T(1,128)S(1)} %pad_maximum_fusion.81), channel_id=1, source_target_pairs={{0,16},{16,32},{32,48},{48,64},{64,80},{80,96},{96,112},{112,128},... | collective-permute-start | bytes 196616 | tf_op jit(solution)/shard_map/ppermute | solution.py:31
  23.5 5.9 %collective-permute-start.1 = (f32[8,1,1024]{2,1,0:T(1,128)S(1)}, f32[8,1,1024]{2,1,0:T(1,128)S(1)}, u32[]{:S(2)}, u32[]{:S(2)}) collective-permute-start(f32[8,1,1024]{2,1,0:T(1,128)S(1)} %get-tuple-element.55), channel_id=1, source_target_pairs={{0,16},{16,32},{32,48},{48,64},{64,80},{80,96},{96,112},{112,128},... | collective-permute-start | bytes 98312 | tf_op jit(solution)/shard_map/ppermute | solution.py:42
  26.7 2.5 copy-start.18
  26.7 2.5 copy-start.8
  26.7 2.5 copy-start.9
  26.7 4.8 %collective-permute-start.2 = (f32[8,1,1024]{2,1,0:T(1,128)S(1)}, f32[8,1,1024]{2,1,0:T(1,128)S(1)}, u32[]{:S(2)}, u32[]{:S(2)}) collective-permute-start(f32[8,1,1024]{2,1,0:T(1,128)S(1)} %get-tuple-element.56), channel_id=1, source_target_pairs={{16,0},{32,16},{48,32},{64,48},{80,64},{96,80},{112,96},{128,112},... | collective-permute-start | bytes 98312 | tf_op jit(solution)/shard_map/ppermute | solution.py:44
  29.3 20.8 %copy-start.7 = (f32[16,1024]{1,0:T(8,128)S(1)}, f32[16,1024]{1,0:T(8,128)}, u32[]{:S(2)}) copy-start(f32[16,1024]{1,0:T(8,128)} %param.15) | copy-start | bytes 196612
  29.4 20.7 %copy-start.5 = (f32[7,16,1024]{2,1,0:T(8,128)S(1)}, f32[7,16,1024]{2,1,0:T(8,128)}, u32[]{:S(2)}) copy-start(f32[7,16,1024]{2,1,0:T(8,128)} %get-tuple-element.51) | copy-start | bytes 1376260
  29.4 20.7 %copy-start.6 = (f32[7,16,1024]{2,1,0:T(8,128)S(1)}, f32[7,16,1024]{2,1,0:T(8,128)}, u32[]{:S(2)}) copy-start(f32[7,16,1024]{2,1,0:T(8,128)} %get-tuple-element.52) | copy-start | bytes 1376260
  31.6 7.7 %collective-permute-start.4 = (f32[8,18,1]{2,1,0:T(8,128)S(1)}, f32[8,18,1]{2,1,0:T(8,128)S(1)}, u32[]{:S(2)}, u32[]{:S(2)}) collective-permute-start(f32[8,18,1]{2,1,0:T(8,128)S(1)} %get-tuple-element.31), channel_id=1, source_target_pairs={{0,1},{1,2},{2,3},{3,4},{4,5},{5,6},{6,7},{7,8},{8,9},{9,10},{10,1... | collective-permute-start | bytes 1736 | tf_op jit(solution)/shard_map/ppermute | solution.py:42
  35.2 14.8 %collective-permute-start.5 = (f32[8,18,1]{2,1,0:T(8,128)S(1)}, f32[8,18,1]{2,1,0:T(8,128)S(1)}, u32[]{:S(2)}, u32[]{:S(2)}) collective-permute-start(f32[8,18,1]{2,1,0:T(8,128)S(1)} %get-tuple-element.32), channel_id=1, source_target_pairs={{1,0},{2,1},{3,2},{4,3},{5,4},{6,5},{7,6},{8,7},{9,8},{10,9},{11,1... | collective-permute-start | bytes 1736 | tf_op jit(solution)/shard_map/ppermute | solution.py:44
  51.1 4.0 %collective-permute-start.6 = (f32[8,1,1024]{2,1,0:T(1,128)S(1)}, f32[8,1,1024]{2,1,0:T(1,128)S(1)}, u32[]{:S(2)}, u32[]{:S(2)}) collective-permute-start(f32[8,1,1024]{2,1,0:T(1,128)S(1)} %get-tuple-element.49), channel_id=1, source_target_pairs={{0,16},{16,32},{32,48},{48,64},{64,80},{80,96},{96,112},{112,128},... | collective-permute-start | bytes 98312 | tf_op jit(solution)/shard_map/ppermute | solution.py:42
  53.8 4.7 %collective-permute-start.7 = (f32[8,1,1024]{2,1,0:T(1,128)S(1)}, f32[8,1,1024]{2,1,0:T(1,128)S(1)}, u32[]{:S(2)}, u32[]{:S(2)}) collective-permute-start(f32[8,1,1024]{2,1,0:T(1,128)S(1)} %get-tuple-element.50), channel_id=1, source_target_pairs={{16,0},{32,16},{48,32},{64,48},{80,64},{96,80},{112,96},{128,112},... | collective-permute-start | bytes 98312 | tf_op jit(solution)/shard_map/ppermute | solution.py:44
  58.6 5.5 %collective-permute-start.8 = (f32[8,18,1]{2,1,0:T(8,128)S(1)}, f32[8,18,1]{2,1,0:T(8,128)S(1)}, u32[]{:S(2)}, u32[]{:S(2)}) collective-permute-start(f32[8,18,1]{2,1,0:T(8,128)S(1)} %get-tuple-element.29), channel_id=1, source_target_pairs={{0,1},{1,2},{2,3},{3,4},{4,5},{5,6},{6,7},{7,8},{8,9},{9,10},{10,1... | collective-permute-start | bytes 1736 | tf_op jit(solution)/shard_map/ppermute | solution.py:42
  62.1 15.5 %collective-permute-start.9 = (f32[8,18,1]{2,1,0:T(8,128)S(1)}, f32[8,18,1]{2,1,0:T(8,128)S(1)}, u32[]{:S(2)}, u32[]{:S(2)}) collective-permute-start(f32[8,18,1]{2,1,0:T(8,128)S(1)} %get-tuple-element.30), channel_id=1, source_target_pairs={{1,0},{2,1},{3,2},{4,3},{5,4},{6,5},{7,6},{8,7},{9,8},{10,9},{11,1... | collective-permute-start | bytes 1736 | tf_op jit(solution)/shard_map/ppermute | solution.py:44
  77.6 6.0 %copy-start.4 = (f32[8,16,1024]{2,1,0:T(8,128)S(1)}, f32[8,16,1024]{2,1,0:T(8,128)}, u32[]{:S(2)}) copy-start(f32[8,16,1024]{2,1,0:T(8,128)} %param.16) | copy-start | bytes 1572868
  78.6 11.3 %collective-permute-start.10 = (f32[8,1,1024]{2,1,0:T(1,128)S(1)}, f32[8,1,1024]{2,1,0:T(1,128)S(1)}, u32[]{:S(2)}, u32[]{:S(2)}) collective-permute-start(f32[8,1,1024]{2,1,0:T(1,128)S(1)} %get-tuple-element.45), channel_id=1, source_target_pairs={{0,16},{16,32},{32,48},{48,64},{64,80},{80,96},{96,112},{112,128},... | collective-permute-start | bytes 98312 | tf_op jit(solution)/shard_map/ppermute | solution.py:42
  82.3 7.6 %collective-permute-start.11 = (f32[8,1,1024]{2,1,0:T(1,128)S(1)}, f32[8,1,1024]{2,1,0:T(1,128)S(1)}, u32[]{:S(2)}, u32[]{:S(2)}) collective-permute-start(f32[8,1,1024]{2,1,0:T(1,128)S(1)} %get-tuple-element.46), channel_id=1, source_target_pairs={{16,0},{32,16},{48,32},{64,48},{80,64},{96,80},{112,96},{128,112},... | collective-permute-start | bytes 98312 | tf_op jit(solution)/shard_map/ppermute | solution.py:44
  83.7 31.5 %collective-permute-start.14 = (f32[8,1,1024]{2,1,0:T(1,128)S(1)}, f32[8,1,1024]{2,1,0:T(1,128)S(1)}, u32[]{:S(2)}, u32[]{:S(2)}) collective-permute-start(f32[8,1,1024]{2,1,0:T(1,128)S(1)} %get-tuple-element.42), channel_id=1, source_target_pairs={{16,0},{32,16},{48,32},{64,48},{80,64},{96,80},{112,96},{128,112},... | collective-permute-start | bytes 98312 | tf_op jit(solution)/shard_map/ppermute | solution.py:44
  85.0 30.3 %collective-permute-start.15 = (f32[8,1,1024]{2,1,0:T(1,128)S(1)}, f32[8,1,1024]{2,1,0:T(1,128)S(1)}, u32[]{:S(2)}, u32[]{:S(2)}) collective-permute-start(f32[8,1,1024]{2,1,0:T(1,128)S(1)} %get-tuple-element.41), channel_id=1, source_target_pairs={{0,16},{16,32},{32,48},{48,64},{64,80},{80,96},{96,112},{112,128},... | collective-permute-start | bytes 98312 | tf_op jit(solution)/shard_map/ppermute | solution.py:42
  90.0 4.5 %collective-permute-start.12 = (f32[8,18,1]{2,1,0:T(8,128)S(1)}, f32[8,18,1]{2,1,0:T(8,128)S(1)}, u32[]{:S(2)}, u32[]{:S(2)}) collective-permute-start(f32[8,18,1]{2,1,0:T(8,128)S(1)} %get-tuple-element.27), channel_id=1, source_target_pairs={{0,1},{1,2},{2,3},{3,4},{4,5},{5,6},{6,7},{7,8},{8,9},{9,10},{10,1... | collective-permute-start | bytes 1736 | tf_op jit(solution)/shard_map/ppermute | solution.py:42
  92.4 15.7 %collective-permute-start.13 = (f32[8,18,1]{2,1,0:T(8,128)S(1)}, f32[8,18,1]{2,1,0:T(8,128)S(1)}, u32[]{:S(2)}, u32[]{:S(2)}) collective-permute-start(f32[8,18,1]{2,1,0:T(8,128)S(1)} %get-tuple-element.28), channel_id=1, source_target_pairs={{1,0},{2,1},{3,2},{4,3},{5,4},{6,5},{7,6},{8,7},{9,8},{10,9},{11,1... | collective-permute-start | bytes 1736 | tf_op jit(solution)/shard_map/ppermute | solution.py:44
  109.0 68.4 %copy-start = (f32[8,16,1024]{2,1,0:T(8,128)}, f32[8,16,1024]{2,1,0:T(8,128)S(1)}, u32[]{:S(2)}) copy-start(f32[8,16,1024]{2,1,0:T(8,128)S(1)} %fusion.17) | copy-start | bytes 1572868
  109.1 21.2 %collective-permute-start.18 = (f32[8,1,1024]{2,1,0:T(1,128)S(1)}, f32[8,1,1024]{2,1,0:T(1,128)S(1)}, u32[]{:S(2)}, u32[]{:S(2)}) collective-permute-start(f32[8,1,1024]{2,1,0:T(1,128)S(1)} %get-tuple-element.40), channel_id=1, source_target_pairs={{16,0},{32,16},{48,32},{64,48},{80,64},{96,80},{112,96},{128,112},... | collective-permute-start | bytes 98312 | tf_op jit(solution)/shard_map/ppermute | solution.py:44
  110.4 19.9 %collective-permute-start.19 = (f32[8,1,1024]{2,1,0:T(1,128)S(1)}, f32[8,1,1024]{2,1,0:T(1,128)S(1)}, u32[]{:S(2)}, u32[]{:S(2)}) collective-permute-start(f32[8,1,1024]{2,1,0:T(1,128)S(1)} %get-tuple-element.39), channel_id=1, source_target_pairs={{0,16},{16,32},{32,48},{48,64},{64,80},{80,96},{96,112},{112,128},... | collective-permute-start | bytes 98312 | tf_op jit(solution)/shard_map/ppermute | solution.py:42
  115.2 0.8 copy-start.12
  115.2 0.8 copy-start.13
  116.0 29.5 %collective-permute-start.16 = (f32[8,18,1]{2,1,0:T(8,128)}, f32[8,18,1]{2,1,0:T(8,128)}, u32[]{:S(2)}, u32[]{:S(2)}) collective-permute-start(f32[8,18,1]{2,1,0:T(8,128)} %get-tuple-element.25), channel_id=1, source_target_pairs={{1,0},{2,1},{3,2},{4,3},{5,4},{6,5},{7,6},{8,7},{9,8},{10,9},{11,1... | collective-permute-start | bytes 1736 | tf_op jit(solution)/shard_map/ppermute | solution.py:44
  117.9 27.6 %collective-permute-start.17 = (f32[8,18,1]{2,1,0:T(8,128)}, f32[8,18,1]{2,1,0:T(8,128)}, u32[]{:S(2)}, u32[]{:S(2)}) collective-permute-start(f32[8,18,1]{2,1,0:T(8,128)} %get-tuple-element.26), channel_id=1, source_target_pairs={{0,1},{1,2},{2,3},{3,4},{4,5},{5,6},{6,7},{7,8},{8,9},{9,10},{10,1... | collective-permute-start | bytes 1736 | tf_op jit(solution)/shard_map/ppermute | solution.py:42
  130.3 0.8 copy-start.10
  131.1 14.9 %collective-permute-start.20 = (f32[8,18,1]{2,1,0:T(8,128)}, f32[8,18,1]{2,1,0:T(8,128)S(1)}, u32[]{:S(2)}, u32[]{:S(2)}) collective-permute-start(f32[8,18,1]{2,1,0:T(8,128)} %get-tuple-element.23), channel_id=1, source_target_pairs={{1,0},{2,1},{3,2},{4,3},{5,4},{6,5},{7,6},{8,7},{9,8},{10,9},{11,1... | collective-permute-start | bytes 1736 | tf_op jit(solution)/shard_map/ppermute | solution.py:44
  133.0 15.5 %collective-permute-start.21 = (f32[8,18,1]{2,1,0:T(8,128)}, f32[8,18,1]{2,1,0:T(8,128)}, u32[]{:S(2)}, u32[]{:S(2)}) collective-permute-start(f32[8,18,1]{2,1,0:T(8,128)} %get-tuple-element.24), channel_id=1, source_target_pairs={{0,1},{1,2},{2,3},{3,4},{4,5},{5,6},{6,7},{7,8},{8,9},{9,10},{10,1... | collective-permute-start | bytes 1736 | tf_op jit(solution)/shard_map/ppermute | solution.py:42
  153.0 7.5 %copy-start.2 = (f32[8,16,1024]{2,1,0:T(8,128)}, f32[8,16,1024]{2,1,0:T(8,128)S(1)}, u32[]{:S(2)}) copy-start(f32[8,16,1024]{2,1,0:T(8,128)S(1)} %get-tuple-element.15) | copy-start | bytes 1572868
  153.1 6.6 %collective-permute-start.22 = (f32[8,1,1024]{2,1,0:T(1,128)S(1)}, f32[8,1,1024]{2,1,0:T(1,128)S(1)}, u32[]{:S(2)}, u32[]{:S(2)}) collective-permute-start(f32[8,1,1024]{2,1,0:T(1,128)S(1)} %get-tuple-element.38), channel_id=1, source_target_pairs={{16,0},{32,16},{48,32},{64,48},{80,64},{96,80},{112,96},{128,112},... | collective-permute-start | bytes 98312 | tf_op jit(solution)/shard_map/ppermute | solution.py:44
  154.4 6.2 %collective-permute-start.23 = (f32[8,1,1024]{2,1,0:T(1,128)S(1)}, f32[8,1,1024]{2,1,0:T(1,128)S(1)}, u32[]{:S(2)}, u32[]{:S(2)}) collective-permute-start(f32[8,1,1024]{2,1,0:T(1,128)S(1)} %get-tuple-element.37), channel_id=1, source_target_pairs={{0,16},{16,32},{32,48},{48,64},{64,80},{80,96},{96,112},{112,128},... | collective-permute-start | bytes 98312 | tf_op jit(solution)/shard_map/ppermute | solution.py:42
  159.7 17.8 %copy-start.11 = (f32[8,1,1024]{2,1,0:T(1,128)S(1)}, f32[8,1,1024]{2,1,0:T(1,128)}, u32[]{:S(2)}) copy-start(f32[8,1,1024]{2,1,0:T(1,128)} %copy-done.10) | copy-start | bytes 98308
  159.7 1.7 copy-start.14
  160.6 0.8 copy-start.16
  161.4 50.4 %collective-permute-start.24 = (f32[8,18,1]{2,1,0:T(8,128)}, f32[8,18,1]{2,1,0:T(8,128)}, u32[]{:S(2)}, u32[]{:S(2)}) collective-permute-start(f32[8,18,1]{2,1,0:T(8,128)} %get-tuple-element.21), channel_id=1, source_target_pairs={{1,0},{2,1},{3,2},{4,3},{5,4},{6,5},{7,6},{8,7},{9,8},{10,9},{11,1... | collective-permute-start | bytes 1736 | tf_op jit(solution)/shard_map/ppermute | solution.py:44
  163.3 48.5 %collective-permute-start.25 = (f32[8,18,1]{2,1,0:T(8,128)}, f32[8,18,1]{2,1,0:T(8,128)}, u32[]{:S(2)}, u32[]{:S(2)}) collective-permute-start(f32[8,18,1]{2,1,0:T(8,128)} %get-tuple-element.22), channel_id=1, source_target_pairs={{0,1},{1,2},{2,3},{3,4},{4,5},{5,6},{6,7},{7,8},{8,9},{9,10},{10,1... | collective-permute-start | bytes 1736 | tf_op jit(solution)/shard_map/ppermute | solution.py:42
  181.1 30.6 %copy-start.15 = (f32[8,1,1024]{2,1,0:T(1,128)S(1)}, f32[8,1,1024]{2,1,0:T(1,128)}, u32[]{:S(2)}) copy-start(f32[8,1,1024]{2,1,0:T(1,128)} %copy-done.14) | copy-start | bytes 98308
  181.1 30.6 %copy-start.17 = (f32[8,1,1024]{2,1,0:T(1,128)S(1)}, f32[8,1,1024]{2,1,0:T(1,128)}, u32[]{:S(2)}) copy-start(f32[8,1,1024]{2,1,0:T(1,128)} %copy-done.16) | copy-start | bytes 98308
  181.2 54.4 %all-to-all-start = ((f32[16,8,128]{2,1,0:T(8,128)}), f32[16,8,128]{2,1,0:T(8,128)S(1)}, u32[]{:S(2)}, u32[]{:S(2)}) async-start(f32[16,8,128]{2,1,0:T(8,128)} %broadcast_in_dim.48), calls=%async_computation | async-start | bytes 131072 | tf_op jit(solution)/shard_map/all_to_all | solution.py:18
  214.7 5.4 %collective-permute-start.26 = (f32[8,1,1024]{2,1,0:T(1,128)S(1)}, f32[8,1,1024]{2,1,0:T(1,128)S(1)}, u32[]{:S(2)}, u32[]{:S(2)}) collective-permute-start(f32[8,1,1024]{2,1,0:T(1,128)S(1)} %get-tuple-element.36), channel_id=1, source_target_pairs={{16,0},{32,16},{48,32},{64,48},{80,64},{96,80},{112,96},{128,112},... | collective-permute-start | bytes 98312 | tf_op jit(solution)/shard_map/ppermute | solution.py:44
  216.0 26.2 %copy-start.3 = (f32[8,16,1024]{2,1,0:T(8,128)S(1)}, f32[8,16,1024]{2,1,0:T(8,128)}, u32[]{:S(2)}) copy-start(f32[8,16,1024]{2,1,0:T(8,128)} %get-tuple-element.16) | copy-start | bytes 1572868
  216.0 5.1 %collective-permute-start.27 = (f32[8,1,1024]{2,1,0:T(1,128)S(1)}, f32[8,1,1024]{2,1,0:T(1,128)S(1)}, u32[]{:S(2)}, u32[]{:S(2)}) collective-permute-start(f32[8,1,1024]{2,1,0:T(1,128)S(1)} %get-tuple-element.35), channel_id=1, source_target_pairs={{0,16},{16,32},{32,48},{48,64},{64,80},{80,96},{96,112},{112,128},... | collective-permute-start | bytes 98312 | tf_op jit(solution)/shard_map/ppermute | solution.py:42
  221.3 20.9 %collective-permute-start.28 = (f32[8,18,1]{2,1,0:T(8,128)S(1)}, f32[8,18,1]{2,1,0:T(8,128)S(1)}, u32[]{:S(2)}, u32[]{:S(2)}) collective-permute-start(f32[8,18,1]{2,1,0:T(8,128)S(1)} %get-tuple-element.19), channel_id=1, source_target_pairs={{1,0},{2,1},{3,2},{4,3},{5,4},{6,5},{7,6},{8,7},{9,8},{10,9},{11,1... | collective-permute-start | bytes 1736 | tf_op jit(solution)/shard_map/ppermute | solution.py:44
  223.2 19.0 %collective-permute-start.29 = (f32[8,18,1]{2,1,0:T(8,128)S(1)}, f32[8,18,1]{2,1,0:T(8,128)S(1)}, u32[]{:S(2)}, u32[]{:S(2)}) collective-permute-start(f32[8,18,1]{2,1,0:T(8,128)S(1)} %get-tuple-element.20), channel_id=1, source_target_pairs={{0,1},{1,2},{2,3},{3,4},{4,5},{5,6},{6,7},{7,8},{8,9},{9,10},{10,1... | collective-permute-start | bytes 1736 | tf_op jit(solution)/shard_map/ppermute | solution.py:42
  237.5 12.4 %all-to-all-start.1 = ((f32[32,8,128]{2,1,0:T(8,128)}), f32[32,8,128]{2,1,0:T(8,128)S(1)}, u32[]{:S(2)}, u32[]{:S(2)}) async-start(f32[32,8,128]{2,1,0:T(8,128)} %broadcast_in_dim.49), calls=%async_computation.1 | async-start | bytes 262144 | tf_op jit(solution)/shard_map/all_to_all | solution.py:18

commit v2 on v0

v2 whole, which is shorter than its diff:
```python
import functools

import jax
import jax.numpy as jnp
from jax import lax
from jax.experimental import pallas as pl
from jax.experimental.pallas import tpu as pltpu
from jax.sharding import PartitionSpec as P

SWEEPS = 3
STEPS = 3
LAYERS = 8
ROWS = 16
LANES = 128
REACH = 8
OWN = 16
STRIP = REACH + OWN
SLOTS = 4
EDGE = 12
FIELDS = 6

damping = 0.8
pad_conductance = 4.0
supply_volts = 1.0
wind_factor = 4.0

X = ("z_lo", "x")
Y = ("y", "z_hi", "core")


def iota(shape, dim):
    return lax.broadcasted_iota(jnp.int32, shape, dim)


def lane_dirs(dirs, shape):
    layer = iota(shape, len(shape) - 1) // ROWS
    found = jnp.zeros(shape, jnp.int32)
    for l in range(LAYERS):
        found = jnp.where(layer == l, dirs[l], found)
    return found == 1


def slots_of(dirs):
    slot, count = [], jnp.int32(0)
    for l in range(LAYERS):
        slot.append(count)
        count = count + (1 - dirs[l])
    return slot


def pack_columns(total_x, total_y, width, dirs, pos, *refs):
    ins, (own_ref, a_ref, b_ref) = refs[:18], refs[18:]
    gx, gy = pos[0], pos[1]
    col = iota((1, 1, LANES), 2)

    def pick(i):
        first, last = ins[2 * i][...], ins[2 * i + 1][...]
        return jnp.where(col.reshape((1,) * (first.ndim - 1) + (LANES,)) < LANES // 2, first, last)

    volts, seg, via_cond, via_mask, pad, load, stress, mob, blk = (pick(i) for i in range(9))
    none = jnp.zeros((1, ROWS, LANES), jnp.float32)
    via = jnp.concatenate([via_cond * via_mask.astype(jnp.float32), none], 0)
    ends = jnp.concatenate(
        [load[None]] + [none] * (LAYERS - 2) + [pad_conductance * pad.astype(jnp.float32)[None]], 0
    )
    mobile = mob * (1.0 - blk.astype(jnp.float32))
    shape = (OWN, LANES)
    along_y = lane_dirs(dirs, shape)
    x = gx * ROWS + iota(shape, 1) % ROWS
    even = gy % 2 == 0
    for f, field in enumerate((volts, seg, via, ends, stress, mobile)):
        turned = field.reshape(LANES, LANES).T
        pieces = []
        for side, start in enumerate((0, LANES - OWN)):
            piece = turned[start : start + OWN]
            if f in (1, 5):
                y = gy * width + (0 if side == 0 else width - OWN) + iota(shape, 0)
                inner = jnp.where(along_y, y, x) < jnp.where(along_y, total_y - 1, total_x - 1)
                piece = jnp.where(inner, piece, 0.0)
            own_ref[side, f] = piece
            pieces.append(piece)
        left, right = pieces[0][:REACH], pieces[1][OWN - REACH :]
        a_ref[f] = jnp.where(even, right, left)
        b_ref[f] = jnp.where(even, left, right)


def inner_x(gx, total_x, shape):
    return (gx * ROWS + iota(shape, 0) < total_x - 1).astype(jnp.float32)


def inner_y(gy, total_y, shape):
    return (gy * shape[1] + iota(shape, 1) < total_y - 1).astype(jnp.float32)


def pack_rows(total_x, dirs, pos, volts, seg, via_cond, via_mask, pad, load, stress, mob, blk, a_ref, b_ref):
    gx = pos[0]
    even = gx % 2 == 0
    width = volts.shape[2]
    inner = inner_x(gx, total_x, (ROWS, width))
    slot = slots_of(dirs)
    for l in range(LAYERS):

        @pl.when(dirs[l] == 0)
        def _(l=l):
            cond = seg[l] * inner
            mobile = mob[l] * (1.0 - blk[l].astype(jnp.float32)) * inner
            held, s = volts[l], stress[l]
            out = []
            for edge in (ROWS - 1, 0):
                here = slice(edge, edge + 1)
                num = jnp.zeros((1, width), jnp.float32)
                diag = cond[here]
                if edge:
                    num = cond[edge - 1 : edge] * held[edge - 1 : edge]
                    diag = diag + cond[edge - 1 : edge]
                else:
                    num = cond[here] * held[1:2]
                if l > 0:
                    below = via_cond[l - 1, here] * via_mask[l - 1, here].astype(jnp.float32)
                    num, diag = num + below * volts[l - 1, here], diag + below
                if l < LAYERS - 1:
                    above = via_cond[l, here] * via_mask[l, here].astype(jnp.float32)
                    num, diag = num + above * volts[l + 1, here], diag + above
                if l == LAYERS - 1:
                    top = pad_conductance * pad[here].astype(jnp.float32)
                    num, diag = num + top * supply_volts, diag + top
                if l == 0:
                    num = num - load[here]
                three = slice(ROWS - 3, ROWS) if edge else slice(0, 3)
                out.append([cond[three], mobile[three], s[three], held[here], num, diag])
            base = slot[l] * EDGE
            at = 0
            for right, left in zip(*out):
                for i in range(right.shape[0]):
                    row = slice(i, i + 1)
                    a_ref[pl.ds(base + at, 1), :] = jnp.where(even, right[row], left[row])
                    b_ref[pl.ds(base + at, 1), :] = jnp.where(even, left[row], right[row])
                    at += 1


def guarded(diag):
    return jnp.where(diag == 0.0, 1.0, diag)


def blocks(width, along_y):
    if along_y:
        return [(slice(r, r + 8), slice(0, width)) for r in range(0, ROWS, 8)]
    step = min(512, width)
    return [(slice(0, ROWS), slice(c, c + step)) for c in range(0, width, step)]


def rest_of(l, at, v, via, pad, load):
    total = None
    if l > 0:
        total = via[(l - 1, *at)] * v[(l - 1, *at)]
    if l < LAYERS - 1:
        above = via[(l, *at)] * v[(l + 1, *at)]
        total = above if total is None else total + above
    if l == LAYERS - 1:
        total = total + pad_conductance * supply_volts * pad[at].astype(jnp.float32)
    if l == 0:
        total = total - load[at]
    return total


def shifted(value, dim, before, after):
    n = value.shape[dim]
    prior, later = pltpu.roll(value, 1, dim), pltpu.roll(value, n - 1, dim)
    if dim == 0:
        row = iota(value.shape, 0)
        if before is not None:
            prior = jnp.where(row == 0, before, prior)
            later = jnp.where(row == n - 1, after, later)
    return prior, later


def strip_pair(recv_a, recv_b, even, own, f):
    from_right = jnp.where(even, recv_a[f], recv_b[f])
    from_left = jnp.where(even, recv_b[f], recv_a[f])
    return (
        jnp.concatenate([from_left, own[0, f]], 0),
        jnp.concatenate([own[1, f], from_right], 0),
    )


def early_sweeps(
    total_x, total_y, dirs, pos, volts, seg, via_cond, via_mask, pad, load, gxa, gxb, own, gya, gyb,
    cond_o, prior_o, via_o, diag_o, volts_o, edges_o, a_ref, b_ref, rate, one, two, halo, to_right, to_left,
):
    gx, gy = pos[0], pos[1]
    even = gx % 2 == 0
    width = volts.shape[2]
    slot = slots_of(dirs)

    def near(right, row, lanes=slice(None)):
        a, b = gxa[pl.ds(row, 1), lanes], gxb[pl.ds(row, 1), lanes]
        return jnp.where(even, a, b) if right else jnp.where(even, b, a)

    for l in range(LAYERS):
        if l < LAYERS - 1:
            via_o[l] = via_cond[l] * via_mask[l].astype(jnp.float32)

        @pl.when(dirs[l] == 0)
        def _(l=l):
            cond = seg[l] * inner_x(gx, total_x, (ROWS, width))
            cond_o[l] = cond
            prior_o[l] = shifted(cond, 0, near(False, slot[l] * EDGE + 2), 0.0)[0]

        @pl.when(dirs[l] == 1)
        def _(l=l):
            cond = seg[l] * inner_y(gy, total_y, (ROWS, width))
            cond_o[l] = cond
            prior_o[l] = pltpu.roll(cond, 1, 1)

    for l in range(LAYERS):
        diag = cond_o[l] + prior_o[l]
        if l > 0:
            diag = diag + via_o[l - 1]
        if l < LAYERS - 1:
            diag = diag + via_o[l]
        else:
            diag = diag + pad_conductance * pad[...].astype(jnp.float32)
        diag_o[l] = diag
        rate[l] = damping / guarded(diag)

    for sweep, (old, new) in enumerate(((volts, one), (one, two), (two, volts_o))):
        for l in range(LAYERS):

            @pl.when(dirs[l] == 0)
            def _(l=l):
                base = slot[l] * EDGE
                for at in blocks(width, False):
                    lanes = at[1]
                    v = old[(l, *at)]
                    if sweep == 0:
                        before, after = near(False, base + 9, lanes), near(True, base + 9, lanes)
                        cond_left = near(False, base + 2, lanes)
                        last = cond_o[l, ROWS - 1 :, lanes]
                        halo[0, pl.ds(slot[l], 1), lanes] = (1.0 - damping) * before + damping * (
                            near(False, base + 10, lanes) + cond_left * v[:1]
                        ) / guarded(near(False, base + 11, lanes))
                        halo[1, pl.ds(slot[l], 1), lanes] = (1.0 - damping) * after + damping * (
                            near(True, base + 10, lanes) + last * v[ROWS - 1 :]
                        ) / guarded(near(True, base + 11, lanes) + last)
                    elif sweep == 1:
                        before, after = halo[0, pl.ds(slot[l], 1), lanes], halo[1, pl.ds(slot[l], 1), lanes]
                    else:
                        before = after = 0.0
                    prior, later = shifted(v, 0, before, after)
                    num = prior_o[(l, *at)] * prior + cond_o[(l, *at)] * later + rest_of(l, at, old, via_o, pad, load)
                    result = (1.0 - damping) * v + rate[(l, *at)] * num
                    new[(l, *at)] = result
                    if sweep == 2:
                        edges_o[0, l : l + 1, lanes] = v[:1]
                        edges_o[1, l : l + 1, lanes] = v[ROWS - 1 :]
                        send = slot[l] * 4
                        for ref, e, d in ((to_right, ROWS - 1, -1), (to_left, 0, 1)):
                            ref[pl.ds(send, 1), lanes] = v[e : e + 1]
                            ref[pl.ds(send + 1, 1), lanes] = num[e : e + 1]
                            ref[pl.ds(send + 2, 1), lanes] = result[e + d : e + d + 1]
                            ref[pl.ds(send + 3, 1), lanes] = result[e + 2 * d : e + 2 * d + 1]

            @pl.when(dirs[l] == 1)
            def _(l=l):
                for at in blocks(width, True):
                    v = old[(l, *at)]
                    prior, later = shifted(v, 1, None, None)
                    num = prior_o[(l, *at)] * prior + cond_o[(l, *at)] * later + rest_of(l, at, old, via_o, pad, load)
                    new[(l, *at)] = (1.0 - damping) * v + rate[(l, *at)] * num
                    if sweep == 2:
                        edges_o[:, l : l + 1, :] = jnp.zeros((2, 1, width), jnp.float32)

    x = iota((STRIP, LANES), 1) % ROWS
    for f in range(FIELDS):
        left, right = strip_pair(gya, gyb, gy % 2 == 0, own, f)
        right_going = jnp.where(x >= 8, left, pltpu.roll(right, LANES - 8, 1))
        left_going = jnp.where(x < 8, left, pltpu.roll(right, 8, 1))
        a_ref[f * STRIP : (f + 1) * STRIP] = jnp.where(even, right_going, left_going)
        b_ref[f * STRIP : (f + 1) * STRIP] = jnp.where(even, left_going, right_going)
    for j in range(width // LANES):
        start = FIELDS * STRIP + j * ROWS
        lanes = slice(j * LANES, (j + 1) * LANES)
        a_ref[start : start + ROWS] = jnp.where(even, to_right[:, lanes], to_left[:, lanes])
        b_ref[start : start + ROWS] = jnp.where(even, to_left[:, lanes], to_right[:, lanes])


def strips(dirs, even_y, even_x, own, gya, gyb, ma, mb):
    tall = (2 * STRIP, LANES)
    x = iota((STRIP, LANES), 1) % ROWS
    own_f, far_f = [], []
    for f in range(FIELDS):
        left, right = strip_pair(gya, gyb, even_y, own, f)
        a, b = ma[f * STRIP : (f + 1) * STRIP], mb[f * STRIP : (f + 1) * STRIP]
        from_right, from_left = jnp.where(even_x, a, b), jnp.where(even_x, b, a)
        far_left = jnp.where(x >= 8, from_left, from_right)
        far_right = jnp.where(x >= 8, pltpu.roll(from_left, 8, 1), pltpu.roll(from_right, LANES - 8, 1))
        own_f.append(jnp.concatenate([left, right], 0))
        far_f.append(jnp.concatenate([far_left, far_right], 0))
    fields = list(zip(own_f, far_f))
    along_y = lane_dirs(dirs, tall)
    layer, x = iota(tall, 1) // ROWS, iota(tall, 1) % ROWS

    def later(pair):
        o, h = pair
        out = []
        for this, other in ((o, h), (h, o)):
            across = jnp.where(x == ROWS - 1, pltpu.roll(other, ROWS - 1, 1), pltpu.roll(this, LANES - 1, 1))
            out.append(jnp.where(along_y, pltpu.roll(this, tall[0] - 1, 0), across))
        return out

    def prior(pair):
        o, h = pair
        out = []
        for this, other in ((o, h), (h, o)):
            across = jnp.where(x == 0, pltpu.roll(other, LANES - ROWS + 1, 1), pltpu.roll(this, 1, 1))
            out.append(jnp.where(along_y, pltpu.roll(this, 1, 0), across))
        return out

    volts, cond, via, ends, stress, mobile = fields
    via_below = [pltpu.roll(a, ROWS, 1) for a in via]
    top = [jnp.where(layer == LAYERS - 1, a, 0.0) for a in ends]
    load = [jnp.where(layer == 0, a, 0.0) for a in ends]
    cond_prior = prior(cond)
    diag = [guarded(p + c + vb + va + t) for p, c, vb, va, t in zip(cond_prior, cond, via_below, via, top)]
    rate = [damping / d for d in diag]

    def inflow(v):
        before, after = prior(v), later(v)
        return [
            cond_prior[i] * before[i]
            + cond[i] * after[i]
            + via_below[i] * pltpu.roll(v[i], ROWS, 1)
            + via[i] * pltpu.roll(v[i], LANES - ROWS, 1)
            + top[i] * supply_volts
            - load[i]
            for i in range(2)
        ]

    for _ in range(SWEEPS):
        num = inflow(volts)
        volts = [(1.0 - damping) * v + r * n for v, r, n in zip(volts, rate, num)]
    resid = inflow(volts)[0] - diag[0] * volts[0]
    sub = iota(tall, 0)
    inside = ((sub >= REACH) & (sub < 2 * REACH)) | ((sub >= STRIP + REACH) & (sub < STRIP + 2 * REACH))
    squares = jnp.where(inside, resid * resid, 0.0)
    after = later(volts)
    wind = [mobile[i] * wind_factor * (cond[i] * (volts[i] - after[i])) for i in range(2)]
    for _ in range(STEPS):
        after = later(stress)
        flux = [mobile[i] * (after[i] - stress[i]) + wind[i] for i in range(2)]
        back = prior(flux)
        stress = [stress[i] + flux[i] - back[i] for i in range(2)]

    def turned(value):
        middle = jnp.zeros((LANES - 2 * OWN, LANES), jnp.float32)
        whole = jnp.concatenate([value[REACH:STRIP], middle, value[STRIP : STRIP + OWN]], 0)
        return whole.T.reshape(LAYERS, ROWS, LANES)

    return turned(volts[0]), turned(stress[0]), squares


def finish(
    total_x, total_y, dirs, pos, cond, prior, via, diag, pad, load, early, edges, stress, mob, blk, gxa, gxb, own,
    gya, gyb, ma, mb, volts_o, stress_o, sum_o, sums, near_left, near_right, ext_c, ext_m, ext_v, ext_s,
):
    gx, gy = pos[0], pos[1]
    even = gx % 2 == 0
    width = early.shape[2]
    slot = slots_of(dirs)

    def near(right, row, lanes=slice(None)):
        a, b = gxa[pl.ds(row, 1), lanes], gxb[pl.ds(row, 1), lanes]
        return jnp.where(even, a, b) if right else jnp.where(even, b, a)

    for j in range(width // LANES):
        start = FIELDS * STRIP + j * ROWS
        lanes = slice(j * LANES, (j + 1) * LANES)
        a, b = ma[start : start + ROWS], mb[start : start + ROWS]
        near_right[:, lanes] = jnp.where(even, a, b)
        near_left[:, lanes] = jnp.where(even, b, a)
    for ref in (ext_c, ext_m, ext_v, ext_s):
        ref[0:8] = jnp.zeros((8, width), jnp.float32)
        ref[24:32] = jnp.zeros((8, width), jnp.float32)
    sums[...] = jnp.zeros_like(sums)

    for l in range(LAYERS):

        @pl.when(dirs[l] == 0)
        def _(l=l):
            v = early[l]
            row = iota(v.shape, 0)
            v2_left, v2_right = near_left[pl.ds(slot[l] * 4, 1), :], near_right[pl.ds(slot[l] * 4, 1), :]
            extra = jnp.where(row == 0, prior[l] * v2_left, jnp.where(row == ROWS - 1, cond[l] * v2_right, 0.0))
            volts_o[l] = v + damping * extra / guarded(diag[l])

        @pl.when(dirs[l] == 1)
        def _(l=l):
            volts_o[l] = early[l]

    for l in range(LAYERS):

        def add(at, before, after, dim, l=l):
            v = volts_o[(l, *at)]
            first, second = shifted(v, dim, before, after)
            resid = (
                prior[(l, *at)] * first
                + cond[(l, *at)] * second
                + rest_of(l, at, volts_o, via, pad, load)
                - diag[(l, *at)] * v
            )
            col = at[1].start + iota(v.shape, 1)
            squares = jnp.where((col >= REACH) & (col < width - REACH), resid * resid, 0.0)
            total = jnp.zeros((8, LANES), jnp.float32)
            for r in range(0, v.shape[0], 8):
                for c in range(0, v.shape[1], LANES):
                    total = total + squares[r : r + 8, c : c + LANES]
            sums[...] += total

        @pl.when(dirs[l] == 0)
        def _(l=l):
            base, low = slot[l] * EDGE, slot[l] * 4
            last = cond[l, ROWS - 1 :, :]
            v_before = (1.0 - damping) * near_left[pl.ds(low, 1), :] + damping * (
                near_left[pl.ds(low + 1, 1), :] + near(False, base + 2) * edges[0, l : l + 1, :]
            ) / guarded(near(False, base + 11))
            v_after = (1.0 - damping) * near_right[pl.ds(low, 1), :] + damping * (
                near_right[pl.ds(low + 1, 1), :] + last * edges[1, l : l + 1, :]
            ) / guarded(near(True, base + 11) + last)
            ext_v[7:8] = v_before
            ext_v[6:7] = near_left[pl.ds(low + 2, 1), :]
            ext_v[5:6] = near_left[pl.ds(low + 3, 1), :]
            ext_v[24:25] = v_after
            ext_v[25:26] = near_right[pl.ds(low + 2, 1), :]
            ext_v[26:27] = near_right[pl.ds(low + 3, 1), :]
            ext_v[8:24] = volts_o[l]
            for at in blocks(width, False):
                add(at, ext_v[7:8, at[1]], ext_v[24:25, at[1]], 0)
            for ref, first in ((ext_c, 0), (ext_m, 3), (ext_s, 6)):
                for i in range(3):
                    ref[5 + i : 6 + i] = near(False, base + first + i)
                    ref[24 + i : 25 + i] = near(True, base + first + i)
            ext_c[8:24] = cond[l]
            ext_m[8:24] = mob[l] * (1.0 - blk[l].astype(jnp.float32)) * inner_x(gx, total_x, (ROWS, width))
            ext_s[8:24] = stress[l]
            n = 32
            step = min(256, width)
            for start in range(0, width, step):
                lanes = slice(start, start + step)
                v, m, s = ext_v[:, lanes], ext_m[:, lanes], ext_s[:, lanes]
                wind = m * wind_factor * (ext_c[:, lanes] * (v - pltpu.roll(v, n - 1, 0)))
                for _ in range(STEPS):
                    flux = m * (pltpu.roll(s, n - 1, 0) - s) + wind
                    s = s + flux - pltpu.roll(flux, 1, 0)
                stress_o[l, :, lanes] = s[8:24]

        @pl.when(dirs[l] == 1)
        def _(l=l):
            for at in blocks(width, True):
                add(at, None, None, 1)
                v, s = volts_o[(l, *at)], stress[(l, *at)]
                inner = inner_y(gy, total_y, (8, width))
                m = mob[(l, *at)] * (1.0 - blk[(l, *at)].astype(jnp.float32)) * inner
                wind = m * wind_factor * (cond[(l, *at)] * (v - pltpu.roll(v, width - 1, 1)))
                for _ in range(STEPS):
                    flux = m * (pltpu.roll(s, width - 1, 1) - s) + wind
                    s = s + flux - pltpu.roll(flux, 1, 1)
                stress_o[(l, *at)] = s

    strip_v, strip_s, squares = strips(dirs, gy % 2 == 0, even, own, gya, gyb, ma, mb)
    lane = iota((1, 1, LANES), 2)
    for ref, strip in ((volts_o, strip_v), (stress_o, strip_s)):
        ref[:, :, :LANES] = jnp.where(lane < REACH, strip, ref[:, :, :LANES])
        ref[:, :, width - LANES :] = jnp.where(lane >= LANES - REACH, strip, ref[:, :, width - LANES :])
    total = jnp.sum(sums[...]) + jnp.sum(squares)
    sum_o[...] = jnp.full(sum_o.shape, total, jnp.float32)


def call(kernel, ins, outs, scratch=(), scalars=2, in_specs=None, grid=None):
    smem = pl.BlockSpec(memory_space=pltpu.SMEM)
    if in_specs is None:
        in_specs = [pl.BlockSpec(memory_space=pltpu.VMEM)] * (len(ins) - scalars)
    out_specs = [pl.BlockSpec(memory_space=pltpu.VMEM)] * len(outs)
    return pl.pallas_call(
        kernel,
        out_shape=[jax.ShapeDtypeStruct(s, jnp.float32) for s in outs],
        in_specs=[smem] * scalars + in_specs,
        out_specs=out_specs,
        scratch_shapes=[pltpu.VMEM(s, jnp.float32) for s in scratch],
        compiler_params=pltpu.CompilerParams(vmem_limit_bytes=48 * 2**20),
        **({"grid": grid} if grid else {}),
    )(*ins)


def swap(value, axes, first):
    count = lax.axis_size(axes)
    pairs = [(i, i + 1) for i in range(first, count - 1, 2)]
    return lax.ppermute(value, axes, pairs + [(b, a) for a, b in pairs])


def sum_all(held):
    for axes, then in ((("z_hi", "z_lo"), ("x", "y", "core")), (("x", "y", "core"), ())):
        total = jnp.sum(lax.all_to_all(held, axes, 0, 0), 0)
        held = jnp.broadcast_to(total, (lax.axis_size(then), 8, LANES)) if then else total
    return held[0, 0]


def body(volts_start, seg_cond, via_cond, via_mask, pad_mask, load_current, stress_start, mobility, blocked, layer_dirs):
    layers, rows, width = seg_cond.shape
    total_x, total_y = rows * lax.axis_size(X), width * lax.axis_size(Y)
    pos = jnp.stack([lax.axis_index(X), lax.axis_index(Y)]).astype(jnp.int32)
    shape = (layers, rows, width)
    fields = (volts_start, seg_cond, via_cond, via_mask, pad_mask, load_current, stress_start, mobility, blocked)
    ends, specs = [], []
    for a in fields:
        for at in (0, width // LANES - 1):
            ends.append(a)
            index = (0,) * (a.ndim - 1) + (at,)
            specs.append(pl.BlockSpec(a.shape[:-1] + (LANES,), lambda i, index=index: index))
    column = (FIELDS, REACH, LANES)
    own, gya, gyb = call(
        functools.partial(pack_columns, total_x, total_y, width),
        (layer_dirs, pos, *ends),
        [(2, FIELDS, OWN, LANES), column, column],
        in_specs=specs,
        grid=(1,),
    )
    gyb = swap(gyb, Y, 1)
    gya = swap(gya, Y, 0)
    gxa, gxb = call(functools.partial(pack_rows, total_x), (layer_dirs, pos, *fields), [(SLOTS * EDGE, width)] * 2)
    gxa, gxb = swap(gxa, X, 0), swap(gxb, X, 1)
    message = (FIELDS * STRIP + ROWS * (width // LANES), LANES)
    cond, prior, via, diag, early, edges, ma, mb = call(
        functools.partial(early_sweeps, total_x, total_y),
        (layer_dirs, pos, *fields[:6], gxa, gxb, own, gya, gyb),
        [shape, shape, (layers - 1, rows, width), shape, shape, (2, layers, width), message, message],
        scratch=[shape, shape, shape, (2, SLOTS, width), (ROWS, width), (ROWS, width)],
    )
    ma, mb = swap(ma, X, 0), swap(mb, X, 1)
    volts, stress, held = call(
        functools.partial(finish, total_x, total_y),
        (layer_dirs, pos, cond, prior, via, diag, pad_mask, load_current, early, edges, *fields[6:], gxa, gxb, own,
         gya, gyb, ma, mb),
        [shape, shape, (lax.axis_size(("z_hi", "z_lo")), 8, LANES)],
        scratch=[(8, LANES), (ROWS, width), (ROWS, width)] + [(32, width)] * 4,
    )
    resid_rms = jnp.sqrt(sum_all(held) / (layers * total_x * total_y))
    return volts, stress, resid_rms


def solution(mesh):
    gx, gy = mesh.shape["gx"], mesh.shape["gy"]
    fine = jax.sharding.Mesh(mesh.devices.reshape(gx // 4, 4, gy // 4, 2, 2), X + Y)
    cells, plane = P(None, X, Y), P(X, Y)
    in_specs = (cells, cells, cells, cells, plane, plane, cells, cells, cells, P())
    return jax.shard_map(body, mesh=fine, in_specs=in_specs, out_specs=(cells, cells, P()), check_vma=False)
```

time: 339 us -> 102 us (0.30)
  starting transfers between devices: 134 us -> 28.4 us
  blocking collectives: 127 us -> 45.5 us
  waiting for transfers between devices: 51.9 us -> 4.16 us
  other arithmetic: 18.1 us -> 0.13 us
  Pallas kernels: 0 us -> 10.8 us
  local copies, waits for them, and re-layouts: 2.91 us -> 10 us
    psum x1 -> x0, blocking collectives: 127 us -> none  [body(): squared = lax.psum(jnp.sum(resid * resid), ('gx', 'gy'))]
    ppermute x30 -> x6, starting transfers between devices: 134 us -> 28.4 us  [swap(): return lax.ppermute(value, axes, pairs + [(b, a) for a, b in pairs])]
    ppermute x30 -> x6, waiting for transfers between devices: 51.9 us -> 4.16 us  [swap(): return lax.ppermute(value, axes, pairs + [(b, a) for a, b in pairs])]
    all_to_all x0 -> x2, blocking collectives: none -> 45.5 us  [sum_all(): total = jnp.sum(lax.all_to_all(held, axes, 0, 0), 0)]
    add x6 -> x0, other arithmetic: 11.1 us -> none  [the longest x3 8.37 us: body(): stress + mobile_x * (side[:, 2:, 1:-1] - stress)]
    pallas_call x0 -> x4, Pallas kernels: none -> 10.8 us  [call(): pl.pallas_call(kernel, out_shape=[jax.ShapeDtypeStruct(s, jnp.float32) fo...]
    unnamed x36 -> x30, local copies, waits for them, and re-layouts: 0.73 us -> 9.52 us
  transfers between devices with their start and end apart: 30 -> 6, of which waited for: 12 -> 2; matrix products, arithmetic and copies ran while one was open for 2% -> 0% of each run, Pallas kernels for 0% -> 1%
where the time goes in v2:
time: 102 us
  blocking collectives  45.5 us (45%)
  starting transfers between devices  28.4 us (28%)
  Pallas kernels  10.8 us (11%)
  local copies, waits for them, and re-layouts  10 us (10%)
  waiting for transfers between devices  4.16 us (4%)
  between operations  2.63 us (3%)
    all_to_all x2, blocking collectives, sum_all(): total = jnp.sum(lax.all_to_all(held, axes, 0, 0), 0)  45.5 us
    ppermute x6, starting transfers between devices, swap(): return lax.ppermute(value, axes, pairs + [(b, a) for a, b in pairs])  28.4 us
    pallas_call x4, Pallas kernels, call(): pl.pallas_call(kernel, out_shape=[jax.ShapeDtypeStruct(s, jnp.float32) fo...  10.8 us
    unnamed x30, local copies, waits for them, and re-layouts  9.52 us
    ppermute x6, waiting for transfers between devices, swap(): return lax.ppermute(value, axes, pairs + [(b, a) for a, b in pairs])  4.16 us
  transfers between devices with their start and end apart: 6, of which 2 were waited for; matrix products, arithmetic and copies ran while one was open for 0% of the time, Pallas kernels for 1%

profile of v2, /device:TPU:1, one launch (start us, length us, event | category | flops | bytes accessed | tf_op | source)
XLA Modules:
  0.0 101.7 jit_solution(7159946160594892252)
XLA Ops:
  0.6 0.0 copy-start.14
  0.7 0.1 pad_add_fusion.pos
  0.7 0.6 copy-done.14
  1.3 0.0 copy-start
  1.3 1.0 %copy-done = f32[8,16,1024]{2,1,0:T(8,128)S(1)} copy-done((f32[8,16,1024]{2,1,0:T(8,128)S(1)}, f32[8,16,1024]{2,1,0:T(8,128)}, u32[]{:S(2)}) %copy-start) | copy-done | bytes 524312
  2.3 0.0 copy-start.1
  2.3 1.0 %copy-done.1 = f32[8,16,1024]{2,1,0:T(8,128)S(1)} copy-done((f32[8,16,1024]{2,1,0:T(8,128)S(1)}, f32[8,16,1024]{2,1,0:T(8,128)}, u32[]{:S(2)}) %copy-start.1) | copy-done | bytes 524312
  3.4 0.0 copy-start.2
  3.4 1.0 %copy-done.2 = f32[8,16,1024]{2,1,0:T(8,128)S(1)} copy-done((f32[8,16,1024]{2,1,0:T(8,128)S(1)}, f32[8,16,1024]{2,1,0:T(8,128)}, u32[]{:S(2)}) %copy-start.2) | copy-done | bytes 524312
  4.4 0.0 copy-start.4
  4.4 1.0 %copy-done.4 = f32[8,16,1024]{2,1,0:T(8,128)S(1)} copy-done((f32[8,16,1024]{2,1,0:T(8,128)S(1)}, f32[8,16,1024]{2,1,0:T(8,128)}, u32[]{:S(2)}) %copy-start.4) | copy-done | bytes 524312
  5.5 0.0 copy-start.6
  5.5 1.0 %copy-done.6 = s32[8,16,1024]{2,1,0:T(8,128)S(1)} copy-done((s32[8,16,1024]{2,1,0:T(8,128)S(1)}, s32[8,16,1024]{2,1,0:T(8,128)}, u32[]{:S(2)}) %copy-start.6) | copy-done | bytes 524312
  6.5 0.0 copy-start.8
  6.5 1.0 copy-done.8
  7.5 0.0 copy-start.9
  7.5 1.0 copy-done.9
  8.5 0.0 copy-start.10
  8.5 0.8 copy-done.10
  9.4 0.0 copy-start.12
  9.4 0.8 copy-done.12
  10.2 1.0 shard_map.121
  11.2 3.9 %collective-permute-start = (f32[48,1024]{1,0:T(8,128)S(1)}, f32[48,1024]{1,0:T(8,128)S(1)}, u32[]{:S(2)}, u32[]{:S(2)}) collective-permute-start(f32[48,1024]{1,0:T(8,128)S(1)} %get-tuple-element.19), channel_id=1, source_target_pairs={{0,16},{32,48},{64,80},{96,112},{128,144},{160,176},{192,208},{224... | collective-permute-start | bytes 589832 | tf_op jit(solution)/shard_map/ppermute | solution.py:497
  15.2 0.7 collective-permute-start.1
  15.9 0.7 shard_map.122
  16.6 6.8 %collective-permute-start.2 = (f32[6,8,128]{2,1,0:T(8,128)S(1)}, f32[6,8,128]{2,1,0:T(8,128)S(1)}, u32[]{:S(2)}, u32[]{:S(2)}) collective-permute-start(f32[6,8,128]{2,1,0:T(8,128)S(1)} %get-tuple-element.22), channel_id=1, source_target_pairs={{0,1},{2,3},{4,5},{6,7},{8,9},{10,11},{12,13},{14,15},{1,0},{3,2},... | collective-permute-start | bytes 73736 | tf_op jit(solution)/shard_map/ppermute | solution.py:497
  23.3 11.4 %collective-permute-start.3 = (f32[6,8,128]{2,1,0:T(8,128)S(1)}, f32[6,8,128]{2,1,0:T(8,128)S(1)}, u32[]{:S(2)}, u32[]{:S(2)}) collective-permute-start(f32[6,8,128]{2,1,0:T(8,128)S(1)} %get-tuple-element.23), channel_id=1, source_target_pairs={{1,2},{3,4},{5,6},{7,8},{9,10},{11,12},{13,14},{2,1},{4,3},{6,5},{... | collective-permute-start | bytes 73736 | tf_op jit(solution)/shard_map/ppermute | solution.py:497
  34.8 0.0 collective-permute-done.2.gya
  34.8 2.4 %collective-permute-done.3.gyb = f32[6,8,128]{2,1,0:T(8,128)S(1)} collective-permute-done((f32[6,8,128]{2,1,0:T(8,128)S(1)}, f32[6,8,128]{2,1,0:T(8,128)S(1)}, u32[]{:S(2)}, u32[]{:S(2)}) %collective-permute-start.3) | collective-permute-done | bytes 24608 | tf_op jit(solution)/shard_map/ppermute | solution.py:497
  37.2 0.0 collective-permute-done.gxa
  37.2 0.0 collective-permute-done.1.gxb
  37.2 0.0 copy-start.3
  37.2 0.0 copy-start.5
  37.2 0.0 copy-start.7
  37.2 0.0 copy-start.11
  37.3 0.0 copy-start.13
  37.3 3.5 %shard_map.123 = (f32[8,16,1024]{2,1,0:T(8,128)S(1)}, f32[8,16,1024]{2,1,0:T(8,128)S(1)}, f32[7,16,1024]{2,1,0:T(8,128)S(1)}, f32[8,16,1024]{2,1,0:T(8,128)S(1)}...) custom-call(s32[8]{0:T(128)S(1)} %copy-done.14, ...), custom_call_target="tpu_custom_call" | custom-call | tf_op jit(solution)/shard_map/pallas_call | solution.py:483
  40.8 4.9 %collective-permute-start.4 = (f32[272,128]{1,0:T(8,128)S(1)}, f32[272,128]{1,0:T(8,128)S(1)}, u32[]{:S(2)}, u32[]{:S(2)}) collective-permute-start(f32[272,128]{1,0:T(8,128)S(1)} %get-tuple-element.30), channel_id=1, source_target_pairs={{0,16},{32,48},{64,80},{96,112},{128,144},{160,176},{192,208},{224... | collective-permute-start | bytes 417800 | tf_op jit(solution)/shard_map/ppermute | solution.py:497
  45.7 0.7 collective-permute-start.5
  46.3 1.8 %collective-permute-done.4.ma = f32[272,128]{1,0:T(8,128)S(1)} collective-permute-done((f32[272,128]{1,0:T(8,128)S(1)}, f32[272,128]{1,0:T(8,128)S(1)}, u32[]{:S(2)}, u32[]{:S(2)}) %collective-permute-start.4) | collective-permute-done | bytes 139296 | tf_op jit(solution)/shard_map/ppermute | solution.py:497
  48.1 0.0 collective-permute-done.5.mb
  48.1 0.0 copy-done.3
  48.1 0.0 copy-done.5
  48.1 0.0 copy-done.7
  48.1 0.0 copy-done.11
  48.1 0.0 copy-done.13
  48.1 5.6 %shard_map.124 = (f32[8,16,1024]{2,1,0:T(8,128)}, f32[8,16,1024]{2,1,0:T(8,128)}, f32[16,8,128]{2,1,0:T(8,128)S(1)}) custom-call(s32[8]{0:T(128)S(1)} %copy-done.14, s32[2]{0:T(128)S(1)} %pad_add_fusion.pos, f32[8,16,1024]{2,1,0:T(8,128)S(1)} %get-tuple-element.24.cond, f32[8,16,1024]{2,1,0:T(8,128)S(1)} %get-tuple-element.25.prior, ...), custom_call_target="tpu_custom_call" | custom-call | tf_op jit(solution)/shard_map/pallas_call | solution.py:483
  53.8 30.6 %all_to_all.10 = f32[16,8,128]{2,1,0:T(8,128)S(1)} all-to-all(f32[16,8,128]{2,1,0:T(8,128)S(1)} %get-tuple-element.34), channel_id=1, replica_groups=mesh['z_lo'=8,'x'=4,'y'=4,'z_hi'=2,'core'=2] {'z_hi','z_lo'}, dimensions={0} | all-to-all | bytes 131072 | tf_op jit(solution)/shard_map/all_to_all | solution.py:502
  84.4 14.9 %all_to_all.11 = f32[32,8,128]{2,1,0:T(8,128)S(1)} all-to-all(f32[32,8,128]{2,1,0:T(8,128)S(1)} %broadcast_in_dim.3), channel_id=1, replica_groups=mesh['z_lo'=8,'x'=4,'y'=4,'z_hi'=2,'core'=2] {'x','y','core'}, dimensions={0} | all-to-all | bytes 262144 | tf_op jit(solution)/shard_map/all_to_all | solution.py:502
  99.3 0.5 slice.3
  (3 shorter events, 0.1 us)
Async XLA Ops:
  0.6 0.7 copy-start.14
  1.3 1.0 %copy-start = (f32[8,16,1024]{2,1,0:T(8,128)S(1)}, f32[8,16,1024]{2,1,0:T(8,128)}, u32[]{:S(2)}) copy-start(f32[8,16,1024]{2,1,0:T(8,128)} %volts.3) | copy-start | bytes 1572868
  2.3 1.0 %copy-start.1 = (f32[8,16,1024]{2,1,0:T(8,128)S(1)}, f32[8,16,1024]{2,1,0:T(8,128)}, u32[]{:S(2)}) copy-start(f32[8,16,1024]{2,1,0:T(8,128)} %seg.3) | copy-start | bytes 1572868
  3.4 1.0 %copy-start.2 = (f32[8,16,1024]{2,1,0:T(8,128)S(1)}, f32[8,16,1024]{2,1,0:T(8,128)}, u32[]{:S(2)}) copy-start(f32[8,16,1024]{2,1,0:T(8,128)} %stress.3) | copy-start | bytes 1572868
  4.4 1.0 %copy-start.4 = (f32[8,16,1024]{2,1,0:T(8,128)S(1)}, f32[8,16,1024]{2,1,0:T(8,128)}, u32[]{:S(2)}) copy-start(f32[8,16,1024]{2,1,0:T(8,128)} %mob.3) | copy-start | bytes 1572868
  5.5 1.0 %copy-start.6 = (s32[8,16,1024]{2,1,0:T(8,128)S(1)}, s32[8,16,1024]{2,1,0:T(8,128)}, u32[]{:S(2)}) copy-start(s32[8,16,1024]{2,1,0:T(8,128)} %blk.3) | copy-start | bytes 1572868
  6.5 1.0 %copy-start.8 = (f32[7,16,1024]{2,1,0:T(8,128)S(1)}, f32[7,16,1024]{2,1,0:T(8,128)}, u32[]{:S(2)}) copy-start(f32[7,16,1024]{2,1,0:T(8,128)} %via_cond.3) | copy-start | bytes 1376260
  7.5 1.0 %copy-start.9 = (s32[7,16,1024]{2,1,0:T(8,128)S(1)}, s32[7,16,1024]{2,1,0:T(8,128)}, u32[]{:S(2)}) copy-start(s32[7,16,1024]{2,1,0:T(8,128)} %via_mask.3) | copy-start | bytes 1376260
  8.5 0.8 copy-start.10
  9.4 0.8 copy-start.12
  11.2 26.0 %collective-permute-start = (f32[48,1024]{1,0:T(8,128)S(1)}, f32[48,1024]{1,0:T(8,128)S(1)}, u32[]{:S(2)}, u32[]{:S(2)}) collective-permute-start(f32[48,1024]{1,0:T(8,128)S(1)} %get-tuple-element.19), channel_id=1, source_target_pairs={{0,16},{32,48},{64,80},{96,112},{128,144},{160,176},{192,208},{224... | collective-permute-start | bytes 589832 | tf_op jit(solution)/shard_map/ppermute | solution.py:497
  15.2 22.0 %collective-permute-start.1 = (f32[48,1024]{1,0:T(8,128)S(1)}, f32[48,1024]{1,0:T(8,128)S(1)}, u32[]{:S(2)}, u32[]{:S(2)}) collective-permute-start(f32[48,1024]{1,0:T(8,128)S(1)} %get-tuple-element.20), channel_id=1, source_target_pairs={{16,32},{48,64},{80,96},{112,128},{144,160},{176,192},{208,224},{2... | collective-permute-start | bytes 589832 | tf_op jit(solution)/shard_map/ppermute | solution.py:497
  16.6 18.2 %collective-permute-start.2 = (f32[6,8,128]{2,1,0:T(8,128)S(1)}, f32[6,8,128]{2,1,0:T(8,128)S(1)}, u32[]{:S(2)}, u32[]{:S(2)}) collective-permute-start(f32[6,8,128]{2,1,0:T(8,128)S(1)} %get-tuple-element.22), channel_id=1, source_target_pairs={{0,1},{2,3},{4,5},{6,7},{8,9},{10,11},{12,13},{14,15},{1,0},{3,2},... | collective-permute-start | bytes 73736 | tf_op jit(solution)/shard_map/ppermute | solution.py:497
  23.3 13.9 %collective-permute-start.3 = (f32[6,8,128]{2,1,0:T(8,128)S(1)}, f32[6,8,128]{2,1,0:T(8,128)S(1)}, u32[]{:S(2)}, u32[]{:S(2)}) collective-permute-start(f32[6,8,128]{2,1,0:T(8,128)S(1)} %get-tuple-element.23), channel_id=1, source_target_pairs={{1,2},{3,4},{5,6},{7,8},{9,10},{11,12},{13,14},{2,1},{4,3},{6,5},{... | collective-permute-start | bytes 73736 | tf_op jit(solution)/shard_map/ppermute | solution.py:497
  37.2 10.9 %copy-start.3 = (f32[8,16,1024]{2,1,0:T(8,128)S(1)}, f32[8,16,1024]{2,1,0:T(8,128)}, u32[]{:S(2)}) copy-start(f32[8,16,1024]{2,1,0:T(8,128)} %stress.3) | copy-start | bytes 1572868
  37.2 10.9 %copy-start.5 = (f32[8,16,1024]{2,1,0:T(8,128)S(1)}, f32[8,16,1024]{2,1,0:T(8,128)}, u32[]{:S(2)}) copy-start(f32[8,16,1024]{2,1,0:T(8,128)} %mob.3) | copy-start | bytes 1572868
  37.2 10.9 %copy-start.7 = (s32[8,16,1024]{2,1,0:T(8,128)S(1)}, s32[8,16,1024]{2,1,0:T(8,128)}, u32[]{:S(2)}) copy-start(s32[8,16,1024]{2,1,0:T(8,128)} %blk.3) | copy-start | bytes 1572868
  37.2 10.9 %copy-start.11 = (s32[16,1024]{1,0:T(8,128)S(1)}, s32[16,1024]{1,0:T(8,128)}, u32[]{:S(2)}) copy-start(s32[16,1024]{1,0:T(8,128)} %pad.9) | copy-start | bytes 196612
  37.3 10.9 %copy-start.13 = (f32[16,1024]{1,0:T(8,128)S(1)}, f32[16,1024]{1,0:T(8,128)}, u32[]{:S(2)}) copy-start(f32[16,1024]{1,0:T(8,128)} %load.5) | copy-start | bytes 196612
  40.8 7.3 %collective-permute-start.4 = (f32[272,128]{1,0:T(8,128)S(1)}, f32[272,128]{1,0:T(8,128)S(1)}, u32[]{:S(2)}, u32[]{:S(2)}) collective-permute-start(f32[272,128]{1,0:T(8,128)S(1)} %get-tuple-element.30), channel_id=1, source_target_pairs={{0,16},{32,48},{64,80},{96,112},{128,144},{160,176},{192,208},{224... | collective-permute-start | bytes 417800 | tf_op jit(solution)/shard_map/ppermute | solution.py:497
  45.7 2.4 %collective-permute-start.5 = (f32[272,128]{1,0:T(8,128)S(1)}, f32[272,128]{1,0:T(8,128)S(1)}, u32[]{:S(2)}, u32[]{:S(2)}) collective-permute-start(f32[272,128]{1,0:T(8,128)S(1)} %get-tuple-element.31), channel_id=1, source_target_pairs={{16,32},{48,64},{80,96},{112,128},{144,160},{176,192},{208,224},{2... | collective-permute-start | bytes 417800 | tf_op jit(solution)/shard_map/ppermute | solution.py:497

commit v3 on v2

--- a/solution.py
+++ b/solution.py
@@ -19,6 +19,10 @@
 EDGE = 12
 FIELDS = 6
 
+COST_ROWS = 2**20
+COST_STRIPS = 4000 * 2**20
+COST_EARLY = 1024
+
 damping = 0.8
 pad_conductance = 4.0
 supply_volts = 1.0
@@ -48,8 +52,21 @@
     return slot
 
 
+def fetch(sources, targets, sems):
+    copies = [pltpu.make_async_copy(a, b, sems.at[i]) for i, (a, b) in enumerate(zip(sources, targets))]
+    for copy in copies:
+        copy.start()
+    for copy in copies:
+        copy.wait()
+
+
 def pack_columns(total_x, total_y, width, dirs, pos, *refs):
-    ins, (own_ref, a_ref, b_ref) = refs[:18], refs[18:]
+    given, (own_ref, a_ref, b_ref), ins, sems = refs[:9], refs[9:12], refs[12:30], refs[30]
+    parts = []
+    for ref in given:
+        for lanes in (slice(0, LANES), slice(width - LANES, width)):
+            parts.append(ref.at[(slice(None),) * (len(ref.shape) - 1) + (lanes,)])
+    fetch(parts, ins, sems)
     gx, gy = pos[0], pos[1]
     col = iota((1, 1, LANES), 2)
 
@@ -92,7 +109,10 @@
     return (gy * shape[1] + iota(shape, 1) < total_y - 1).astype(jnp.float32)
 
 
-def pack_rows(total_x, dirs, pos, volts, seg, via_cond, via_mask, pad, load, stress, mob, blk, a_ref, b_ref):
+def pack_rows(total_x, dirs, pos, after, *refs):
+    given, (a_ref, b_ref), held_refs, sems = refs[:9], refs[9:11], refs[11:20], refs[20]
+    fetch(given, held_refs, sems)
+    volts, seg, via_cond, via_mask, pad, load, stress, mob, blk = held_refs
     gx = pos[0]
     even = gx % 2 == 0
     width = volts.shape[2]
@@ -184,7 +204,7 @@
 
 
 def early_sweeps(
-    total_x, total_y, dirs, pos, volts, seg, via_cond, via_mask, pad, load, gxa, gxb, own, gya, gyb,
+    total_x, total_y, dirs, pos, volts, seg, via_cond, via_mask, pad, load, gxa, gxb, strips_a, strips_b,
     cond_o, prior_o, via_o, diag_o, volts_o, edges_o, a_ref, b_ref, rate, one, two, halo, to_right, to_left,
 ):
     gx, gy = pos[0], pos[1]
@@ -270,6 +290,18 @@
                     if sweep == 2:
                         edges_o[:, l : l + 1, :] = jnp.zeros((2, 1, width), jnp.float32)
 
+    a_ref[: FIELDS * STRIP] = strips_a[...]
+    b_ref[: FIELDS * STRIP] = strips_b[...]
+    for j in range(width // LANES):
+        start = FIELDS * STRIP + j * ROWS
+        lanes = slice(j * LANES, (j + 1) * LANES)
+        a_ref[start : start + ROWS] = jnp.where(even, to_right[:, lanes], to_left[:, lanes])
+        b_ref[start : start + ROWS] = jnp.where(even, to_left[:, lanes], to_right[:, lanes])
+
+
+def pack_strips(pos, own, gyb, gya, a_ref, b_ref):
+    gx, gy = pos[0], pos[1]
+    even = gx % 2 == 0
     x = iota((STRIP, LANES), 1) % ROWS
     for f in range(FIELDS):
         left, right = strip_pair(gya, gyb, gy % 2 == 0, own, f)
@@ -277,28 +309,22 @@
         left_going = jnp.where(x < 8, left, pltpu.roll(right, 8, 1))
         a_ref[f * STRIP : (f + 1) * STRIP] = jnp.where(even, right_going, left_going)
         b_ref[f * STRIP : (f + 1) * STRIP] = jnp.where(even, left_going, right_going)
-    for j in range(width // LANES):
-        start = FIELDS * STRIP + j * ROWS
-        lanes = slice(j * LANES, (j + 1) * LANES)
-        a_ref[start : start + ROWS] = jnp.where(even, to_right[:, lanes], to_left[:, lanes])
-        b_ref[start : start + ROWS] = jnp.where(even, to_left[:, lanes], to_right[:, lanes])
-
-
-def strips(dirs, even_y, even_x, own, gya, gyb, ma, mb):
+
+
+def strip_field(f, even_y, even_x, own, gya, gyb, ma, mb):
+    x = iota((STRIP, LANES), 1) % ROWS
+    left, right = strip_pair(gya, gyb, even_y, own, f)
+    a, b = ma[f * STRIP : (f + 1) * STRIP], mb[f * STRIP : (f + 1) * STRIP]
+    from_right, from_left = jnp.where(even_x, a, b), jnp.where(even_x, b, a)
+    far_left = jnp.where(x >= 8, from_left, from_right)
+    far_right = jnp.where(x >= 8, pltpu.roll(from_left, 8, 1), pltpu.roll(from_right, LANES - 8, 1))
+    return jnp.concatenate([left, right], 0), jnp.concatenate([far_left, far_right], 0)
+
+
+def strip_shifts(dirs):
     tall = (2 * STRIP, LANES)
-    x = iota((STRIP, LANES), 1) % ROWS
-    own_f, far_f = [], []
-    for f in range(FIELDS):
-        left, right = strip_pair(gya, gyb, even_y, own, f)
-        a, b = ma[f * STRIP : (f + 1) * STRIP], mb[f * STRIP : (f + 1) * STRIP]
-        from_right, from_left = jnp.where(even_x, a, b), jnp.where(even_x, b, a)
-        far_left = jnp.where(x >= 8, from_left, from_right)
-        far_right = jnp.where(x >= 8, pltpu.roll(from_left, 8, 1), pltpu.roll(from_right, LANES - 8, 1))
-        own_f.append(jnp.concatenate([left, right], 0))
-        far_f.append(jnp.concatenate([far_left, far_right], 0))
-    fields = list(zip(own_f, far_f))
     along_y = lane_dirs(dirs, tall)
-    layer, x = iota(tall, 1) // ROWS, iota(tall, 1) % ROWS
+    x = iota(tall, 1) % ROWS
 
     def later(pair):
         o, h = pair
@@ -316,7 +342,16 @@
             out.append(jnp.where(along_y, pltpu.roll(this, 1, 0), across))
         return out
 
-    volts, cond, via, ends, stress, mobile = fields
+    return prior, later
+
+
+def strips(dirs, even_y, even_x, own, gya, gyb, ma, mb):
+    tall = (2 * STRIP, LANES)
+    layer = iota(tall, 1) // ROWS
+    prior, later = strip_shifts(dirs)
+    volts, cond, via, ends, mobile = (
+        strip_field(f, even_y, even_x, own, gya, gyb, ma, mb) for f in (0, 1, 2, 3, 5)
+    )
     via_below = [pltpu.roll(a, ROWS, 1) for a in via]
     top = [jnp.where(layer == LAYERS - 1, a, 0.0) for a in ends]
     load = [jnp.where(layer == 0, a, 0.0) for a in ends]
@@ -345,31 +380,37 @@
     squares = jnp.where(inside, resid * resid, 0.0)
     after = later(volts)
     wind = [mobile[i] * wind_factor * (cond[i] * (volts[i] - after[i])) for i in range(2)]
+    return turned(volts[0]), wind, squares
+
+
+def strip_stress(dirs, even_y, even_x, own, gya, gyb, ma, mb, wind):
+    stress, mobile = (strip_field(f, even_y, even_x, own, gya, gyb, ma, mb) for f in (4, 5))
+    prior, later = strip_shifts(dirs)
     for _ in range(STEPS):
         after = later(stress)
         flux = [mobile[i] * (after[i] - stress[i]) + wind[i] for i in range(2)]
         back = prior(flux)
         stress = [stress[i] + flux[i] - back[i] for i in range(2)]
-
-    def turned(value):
-        middle = jnp.zeros((LANES - 2 * OWN, LANES), jnp.float32)
-        whole = jnp.concatenate([value[REACH:STRIP], middle, value[STRIP : STRIP + OWN]], 0)
-        return whole.T.reshape(LAYERS, ROWS, LANES)
-
-    return turned(volts[0]), turned(stress[0]), squares
-
-
-def finish(
-    total_x, total_y, dirs, pos, cond, prior, via, diag, pad, load, early, edges, stress, mob, blk, gxa, gxb, own,
-    gya, gyb, ma, mb, volts_o, stress_o, sum_o, sums, near_left, near_right, ext_c, ext_m, ext_v, ext_s,
+    return turned(stress[0])
+
+
+def turned(value):
+    middle = jnp.zeros((LANES - 2 * OWN, LANES), jnp.float32)
+    whole = jnp.concatenate([value[REACH:STRIP], middle, value[STRIP : STRIP + OWN]], 0)
+    return whole.T.reshape(LAYERS, ROWS, LANES)
+
+
+def last_sweep(
+    dirs, pos, cond, prior, via, diag, pad, load, early, edges, gxa, gxb, own, gya, gyb, ma, mb,
+    volts_o, sum_o, sides_o, wind_o, sums, near_left, near_right,
 ):
     gx, gy = pos[0], pos[1]
     even = gx % 2 == 0
     width = early.shape[2]
     slot = slots_of(dirs)
 
-    def near(right, row, lanes=slice(None)):
-        a, b = gxa[pl.ds(row, 1), lanes], gxb[pl.ds(row, 1), lanes]
+    def near(right, row):
+        a, b = gxa[pl.ds(row, 1), :], gxb[pl.ds(row, 1), :]
         return jnp.where(even, a, b) if right else jnp.where(even, b, a)
 
     for j in range(width // LANES):
@@ -378,9 +419,6 @@
         a, b = ma[start : start + ROWS], mb[start : start + ROWS]
         near_right[:, lanes] = jnp.where(even, a, b)
         near_left[:, lanes] = jnp.where(even, b, a)
-    for ref in (ext_c, ext_m, ext_v, ext_s):
-        ref[0:8] = jnp.zeros((8, width), jnp.float32)
-        ref[24:32] = jnp.zeros((8, width), jnp.float32)
     sums[...] = jnp.zeros_like(sums)
 
     for l in range(LAYERS):
@@ -389,9 +427,20 @@
         def _(l=l):
             v = early[l]
             row = iota(v.shape, 0)
-            v2_left, v2_right = near_left[pl.ds(slot[l] * 4, 1), :], near_right[pl.ds(slot[l] * 4, 1), :]
+            base, low = slot[l] * EDGE, slot[l] * 4
+            v2_left, v2_right = near_left[pl.ds(low, 1), :], near_right[pl.ds(low, 1), :]
             extra = jnp.where(row == 0, prior[l] * v2_left, jnp.where(row == ROWS - 1, cond[l] * v2_right, 0.0))
             volts_o[l] = v + damping * extra / guarded(diag[l])
+            last = cond[l, ROWS - 1 :, :]
+            sides_o[0, pl.ds(low, 1), :] = (1.0 - damping) * v2_left + damping * (
+                near_left[pl.ds(low + 1, 1), :] + near(False, base + 2) * edges[0, l : l + 1, :]
+            ) / guarded(near(False, base + 11))
+            sides_o[1, pl.ds(low, 1), :] = (1.0 - damping) * v2_right + damping * (
+                near_right[pl.ds(low + 1, 1), :] + last * edges[1, l : l + 1, :]
+            ) / guarded(near(True, base + 11) + last)
+            for side, ref in enumerate((near_left, near_right)):
+                sides_o[side, pl.ds(low + 1, 1), :] = ref[pl.ds(low + 2, 1), :]
+                sides_o[side, pl.ds(low + 2, 1), :] = ref[pl.ds(low + 3, 1), :]
 
         @pl.when(dirs[l] == 1)
         def _(l=l):
@@ -418,27 +467,59 @@
 
         @pl.when(dirs[l] == 0)
         def _(l=l):
+            for at in blocks(width, False):
+                low = pl.ds(slot[l] * 4, 1)
+                add(at, sides_o[0, low, at[1]], sides_o[1, low, at[1]], 0)
+
+        @pl.when(dirs[l] == 1)
+        def _(l=l):
+            for at in blocks(width, True):
+                add(at, None, None, 1)
+
+    strip_v, wind, squares = strips(dirs, gy % 2 == 0, even, own, gya, gyb, ma, mb)
+    for i in range(2):
+        wind_o[i] = wind[i]
+    place(volts_o, strip_v)
+    total = jnp.sum(sums[...]) + jnp.sum(squares)
+    sum_o[...] = jnp.full(sum_o.shape, total, jnp.float32)
+
+
+def place(ref, strip):
+    width = ref.shape[2]
+    lane = iota((1, 1, LANES), 2)
+    ref[:, :, :LANES] = jnp.where(lane < REACH, strip, ref[:, :, :LANES])
+    ref[:, :, width - LANES :] = jnp.where(lane >= LANES - REACH, strip, ref[:, :, width - LANES :])
+
+
+def stress_steps(
+    total_x, total_y, dirs, pos, cond, volts, sides, stress, mob, blk, gxa, gxb, own, gya, gyb, ma, mb, wind_strip,
+    stress_o, ext_c, ext_m, ext_v, ext_s,
+):
+    gx, gy = pos[0], pos[1]
+    even = gx % 2 == 0
+    width = volts.shape[2]
+    slot = slots_of(dirs)
+
+    def near(right, row):
+        a, b = gxa[pl.ds(row, 1), :], gxb[pl.ds(row, 1), :]
+        return jnp.where(even, a, b) if right else jnp.where(even, b, a)
+
+    for ref in (ext_c, ext_m, ext_v, ext_s):
+        ref[0:8] = jnp.zeros((8, width), jnp.float32)
+        ref[24:32] = jnp.zeros((8, width), jnp.float32)
+
+    for l in range(LAYERS):
+
+        @pl.when(dirs[l] == 0)
+        def _(l=l):
             base, low = slot[l] * EDGE, slot[l] * 4
-            last = cond[l, ROWS - 1 :, :]
-            v_before = (1.0 - damping) * near_left[pl.ds(low, 1), :] + damping * (
-                near_left[pl.ds(low + 1, 1), :] + near(False, base + 2) * edges[0, l : l + 1, :]
-            ) / guarded(near(False, base + 11))
-            v_after = (1.0 - damping) * near_right[pl.ds(low, 1), :] + damping * (
-                near_right[pl.ds(low + 1, 1), :] + last * edges[1, l : l + 1, :]
-            ) / guarded(near(True, base + 11) + last)
-            ext_v[7:8] = v_before
-            ext_v[6:7] = near_left[pl.ds(low + 2, 1), :]
-            ext_v[5:6] = near_left[pl.ds(low + 3, 1), :]
-            ext_v[24:25] = v_after
-            ext_v[25:26] = near_right[pl.ds(low + 2, 1), :]
-            ext_v[26:27] = near_right[pl.ds(low + 3, 1), :]
-            ext_v[8:24] = volts_o[l]
-            for at in blocks(width, False):
-                add(at, ext_v[7:8, at[1]], ext_v[24:25, at[1]], 0)
-            for ref, first in ((ext_c, 0), (ext_m, 3), (ext_s, 6)):
-                for i in range(3):
+            for i in range(3):
+                ext_v[7 - i : 8 - i] = sides[0, pl.ds(low + i, 1), :]
+                ext_v[24 + i : 25 + i] = sides[1, pl.ds(low + i, 1), :]
+                for ref, first in ((ext_c, 0), (ext_m, 3), (ext_s, 6)):
                     ref[5 + i : 6 + i] = near(False, base + first + i)
                     ref[24 + i : 25 + i] = near(True, base + first + i)
+            ext_v[8:24] = volts[l]
             ext_c[8:24] = cond[l]
             ext_m[8:24] = mob[l] * (1.0 - blk[l].astype(jnp.float32)) * inner_x(gx, total_x, (ROWS, width))
             ext_s[8:24] = stress[l]
@@ -456,8 +537,7 @@
         @pl.when(dirs[l] == 1)
         def _(l=l):
             for at in blocks(width, True):
-                add(at, None, None, 1)
-                v, s = volts_o[(l, *at)], stress[(l, *at)]
+                v, s = volts[(l, *at)], stress[(l, *at)]
                 inner = inner_y(gy, total_y, (8, width))
                 m = mob[(l, *at)] * (1.0 - blk[(l, *at)].astype(jnp.float32)) * inner
                 wind = m * wind_factor * (cond[(l, *at)] * (v - pltpu.roll(v, width - 1, 1)))
@@ -466,28 +546,22 @@
                     s = s + flux - pltpu.roll(flux, 1, 1)
                 stress_o[(l, *at)] = s
 
-    strip_v, strip_s, squares = strips(dirs, gy % 2 == 0, even, own, gya, gyb, ma, mb)
-    lane = iota((1, 1, LANES), 2)
-    for ref, strip in ((volts_o, strip_v), (stress_o, strip_s)):
-        ref[:, :, :LANES] = jnp.where(lane < REACH, strip, ref[:, :, :LANES])
-        ref[:, :, width - LANES :] = jnp.where(lane >= LANES - REACH, strip, ref[:, :, width - LANES :])
-    total = jnp.sum(sums[...]) + jnp.sum(squares)
-    sum_o[...] = jnp.full(sum_o.shape, total, jnp.float32)
-
-
-def call(kernel, ins, outs, scratch=(), scalars=2, in_specs=None, grid=None):
-    smem = pl.BlockSpec(memory_space=pltpu.SMEM)
-    if in_specs is None:
-        in_specs = [pl.BlockSpec(memory_space=pltpu.VMEM)] * (len(ins) - scalars)
-    out_specs = [pl.BlockSpec(memory_space=pltpu.VMEM)] * len(outs)
+    wind = [wind_strip[0], wind_strip[1]]
+    place(stress_o, strip_stress(dirs, gy % 2 == 0, even, own, gya, gyb, ma, mb, wind))
+
+
+def call(kernel, ins, outs, scratch=(), scalars=2, copies=0, cost=0):
+    smem, vmem = pl.BlockSpec(memory_space=pltpu.SMEM), pl.BlockSpec(memory_space=pltpu.VMEM)
+    held = pl.BlockSpec(memory_space=pltpu.HBM) if copies else vmem
+    scratch = [pltpu.VMEM(*(s if isinstance(s[0], tuple) else (s, jnp.float32))) for s in scratch]
     return pl.pallas_call(
         kernel,
         out_shape=[jax.ShapeDtypeStruct(s, jnp.float32) for s in outs],
-        in_specs=[smem] * scalars + in_specs,
-        out_specs=out_specs,
-        scratch_shapes=[pltpu.VMEM(s, jnp.float32) for s in scratch],
-        compiler_params=pltpu.CompilerParams(vmem_limit_bytes=48 * 2**20),
-        **({"grid": grid} if grid else {}),
+        in_specs=[smem] * scalars + [held] * (len(ins) - scalars),
+        out_specs=[vmem] * len(outs),
+        scratch_shapes=scratch + ([pltpu.SemaphoreType.DMA((copies,))] if copies else []),
+        compiler_params=pltpu.CompilerParams(vmem_limit_bytes=(62 if copies else 16) * 2**20),
+        cost_estimate=pl.CostEstimate(flops=cost, bytes_accessed=cost, transcendentals=0),
     )(*ins)
 
 
@@ -510,38 +584,47 @@
     pos = jnp.stack([lax.axis_index(X), lax.axis_index(Y)]).astype(jnp.int32)
     shape = (layers, rows, width)
     fields = (volts_start, seg_cond, via_cond, via_mask, pad_mask, load_current, stress_start, mobility, blocked)
-    ends, specs = [], []
-    for a in fields:
-        for at in (0, width // LANES - 1):
-            ends.append(a)
-            index = (0,) * (a.ndim - 1) + (at,)
-            specs.append(pl.BlockSpec(a.shape[:-1] + (LANES,), lambda i, index=index: index))
     column = (FIELDS, REACH, LANES)
     own, gya, gyb = call(
         functools.partial(pack_columns, total_x, total_y, width),
-        (layer_dirs, pos, *ends),
+        (layer_dirs, pos, *fields),
         [(2, FIELDS, OWN, LANES), column, column],
-        in_specs=specs,
-        grid=(1,),
-    )
-    gyb = swap(gyb, Y, 1)
-    gya = swap(gya, Y, 0)
-    gxa, gxb = call(functools.partial(pack_rows, total_x), (layer_dirs, pos, *fields), [(SLOTS * EDGE, width)] * 2)
+        scratch=[(a.shape[:-1] + (LANES,), a.dtype) for a in fields for _ in range(2)],
+        copies=18,
+    )
+    gyb, gya = swap(gyb, Y, 1), swap(gya, Y, 0)
+    gxa, gxb = call(
+        functools.partial(pack_rows, total_x),
+        (layer_dirs, pos, own, *fields),
+        [(SLOTS * EDGE, width)] * 2,
+        scratch=[(a.shape, a.dtype) for a in fields],
+        copies=9,
+        cost=COST_ROWS,
+    )
     gxa, gxb = swap(gxa, X, 0), swap(gxb, X, 1)
+    side = (FIELDS * STRIP, LANES)
+    sa, sb = call(pack_strips, (pos, own, gyb, gya), [side, side], scalars=1, cost=COST_STRIPS)
     message = (FIELDS * STRIP + ROWS * (width // LANES), LANES)
     cond, prior, via, diag, early, edges, ma, mb = call(
         functools.partial(early_sweeps, total_x, total_y),
-        (layer_dirs, pos, *fields[:6], gxa, gxb, own, gya, gyb),
+        (layer_dirs, pos, *fields[:6], gxa, gxb, sa, sb),
         [shape, shape, (layers - 1, rows, width), shape, shape, (2, layers, width), message, message],
         scratch=[shape, shape, shape, (2, SLOTS, width), (ROWS, width), (ROWS, width)],
+        cost=COST_EARLY,
     )
     ma, mb = swap(ma, X, 0), swap(mb, X, 1)
-    volts, stress, held = call(
-        functools.partial(finish, total_x, total_y),
-        (layer_dirs, pos, cond, prior, via, diag, pad_mask, load_current, early, edges, *fields[6:], gxa, gxb, own,
-         gya, gyb, ma, mb),
-        [shape, shape, (lax.axis_size(("z_hi", "z_lo")), 8, LANES)],
-        scratch=[(8, LANES), (ROWS, width), (ROWS, width)] + [(32, width)] * 4,
+    volts, held, sides, wind = call(
+        last_sweep,
+        (layer_dirs, pos, cond, prior, via, diag, pad_mask, load_current, early, edges, gxa, gxb, own, gya, gyb, ma, mb),
+        [shape, (lax.axis_size(("z_hi", "z_lo")), 8, LANES), (2, ROWS, width), (2, 2 * STRIP, LANES)],
+        scratch=[(8, LANES), (ROWS, width), (ROWS, width)],
+    )
+    (stress,) = call(
+        functools.partial(stress_steps, total_x, total_y),
+        (layer_dirs, pos, cond, volts, sides, *fields[6:], gxa, gxb, own, gya, gyb, ma, mb, wind),
+        [shape],
+        scratch=[(32, width)] * 4,
+        cost=12 * 2**20,
     )
     resid_rms = jnp.sqrt(sum_all(held) / (layers * total_x * total_y))
     return volts, stress, resid_rms

time: 102 us -> 95.8 us (0.939)
  blocking collectives: 45.5 us -> 24 us
  starting transfers between devices: 28.4 us -> 39.2 us
  Pallas kernels: 10.8 us -> 18.6 us
  local copies, waits for them, and re-layouts: 10 us -> 2.87 us
  waiting for transfers between devices: 4.16 us -> 7.13 us
    all_to_all x2 -> x1, blocking collectives: 45.5 us -> 24 us  [sum_all(): total = jnp.sum(lax.all_to_all(held, axes, 0, 0), 0)]
    all_to_all x0 -> x1, starting transfers between devices: none -> 9.97 us  [sum_all(): total = jnp.sum(lax.all_to_all(held, axes, 0, 0), 0)]
    unnamed x30 -> x26, local copies, waits for them, and re-layouts: 9.52 us -> 1.7 us
    pallas_call x4 -> x6, Pallas kernels: 10.8 us -> 18.6 us  [call(): pl.pallas_call(kernel, out_shape=[jax.ShapeDtypeStruct(s, jnp.float32) fo...]
    all_to_all x0 -> x1, waiting for transfers between devices: none -> 2 us  [sum_all(): total = jnp.sum(lax.all_to_all(held, axes, 0, 0), 0)]
  transfers between devices with their start and end apart: 6 -> 7, of which waited for: 2 -> 3; matrix products, arithmetic and copies ran while one was open for 0% -> 0% of each run, Pallas kernels for 1% -> 10%
where the time goes in v3:
time: 95.8 us; the launch traced here: 95.2 us
  starting transfers between devices  39.2 us (41%)
  blocking collectives  24 us (25%)
  Pallas kernels  18.6 us (19%)
  waiting for transfers between devices  7.13 us (7%)
  local copies, waits for them, and re-layouts  2.87 us (3%)
  between operations  2.72 us (3%)
    ppermute x6, starting transfers between devices, swap(): return lax.ppermute(value, axes, pairs + [(b, a) for a, b in pairs])  29.3 us
    all_to_all x1, blocking collectives, sum_all(): total = jnp.sum(lax.all_to_all(held, axes, 0, 0), 0)  24 us
    pallas_call x6, Pallas kernels, call(): pl.pallas_call(kernel, out_shape=[jax.ShapeDtypeStruct(s, jnp.float32) fo...  18.6 us
    all_to_all x1, starting transfers between devices, sum_all(): total = jnp.sum(lax.all_to_all(held, axes, 0, 0), 0)  9.97 us
    ppermute x6, waiting for transfers between devices, swap(): return lax.ppermute(value, axes, pairs + [(b, a) for a, b in pairs])  5.13 us
    all_to_all x1, waiting for transfers between devices, sum_all(): total = jnp.sum(lax.all_to_all(held, axes, 0, 0), 0)  2 us
  transfers between devices with their start and end apart: 7, of which 3 were waited for; matrix products, arithmetic and copies ran while one was open for 0% of the time, Pallas kernels for 10%

profile of v3, /device:TPU:1, one launch (start us, length us, event | category | flops | bytes accessed | tf_op | source)
XLA Modules:
  0.0 95.2 jit_solution(12096208082623757456)
XLA Ops:
  0.6 0.6 pad_add_fusion.pos
  1.3 2.9 %shard_map.121 = (f32[2,6,16,128]{3,2,1,0:T(8,128)}, f32[6,8,128]{2,1,0:T(8,128)}, f32[6,8,128]{2,1,0:T(8,128)}) custom-call(s32[8]{0:T(128)} %dirs.9, s32[2]{0:T(128)} %pad_add_fusion.pos, f32[8,16,1024]{2,1,0:T(8,128)} %volts.1, f32[8,16,1024]{2,1,0:T(8,128)} %seg.1, f32[7,16,1024]{2,1,0:T(8,128)} %via_cond.1, s32[7,16,1024]{2,1,0:T(8,128)} %via_mask.1, ...), custom_call_target="tpu_custom_call" | custom-call | tf_op jit(solution)/shard_map/pallas_call | solution.py:557
  4.1 16.8 %collective-permute-start.2 = (f32[6,8,128]{2,1,0:T(8,128)}, f32[6,8,128]{2,1,0:T(8,128)S(1)}, u32[]{:S(2)}, u32[]{:S(2)}) collective-permute-start(f32[6,8,128]{2,1,0:T(8,128)} %get-tuple-element.25), channel_id=1, source_target_pairs={{1,2},{3,4},{5,6},{7,8},{9,10},{11,12},{13,14},{2,1},{4,3},{6,5},{... | collective-permute-start | bytes 73736 | tf_op jit(solution)/shard_map/ppermute | solution.py:571
  21.0 1.9 %collective-permute-start.3 = (f32[6,8,128]{2,1,0:T(8,128)}, f32[6,8,128]{2,1,0:T(8,128)S(1)}, u32[]{:S(2)}, u32[]{:S(2)}) collective-permute-start(f32[6,8,128]{2,1,0:T(8,128)} %get-tuple-element.26), channel_id=1, source_target_pairs={{0,1},{2,3},{4,5},{6,7},{8,9},{10,11},{12,13},{14,15},{1,0},{3,2},... | collective-permute-start | bytes 73736 | tf_op jit(solution)/shard_map/ppermute | solution.py:571
  22.9 0.0 copy-start.9
  22.9 4.0 %shard_map.122 = (f32[48,1024]{1,0:T(8,128)}, f32[48,1024]{1,0:T(8,128)}) custom-call(s32[8]{0:T(128)} %dirs.9, s32[2]{0:T(128)} %pad_add_fusion.pos, f32[2,6,16,128]{3,2,1,0:T(8,128)} %get-tuple-element.22.after.own, f32[8,16,1024]{2,1,0:T(8,128)} %volts.1, f32[8,16,1024]{2,1,0:T(8,128)} %seg.1, f32[7,16,1024]{2,1,0:T(8,128)} %via_cond.1, ...), custom_call_target="tpu_custom_call" | custom-call | flops 1048576 | bytes 1048576 | tf_op jit(solution)/shard_map/pallas_call | solution.py:557
  27.0 0.0 copy-start.12
  27.0 3.1 %collective-permute-start = (f32[48,1024]{1,0:T(8,128)}, f32[48,1024]{1,0:T(8,128)S(1)}, u32[]{:S(2)}, u32[]{:S(2)}) collective-permute-start(f32[48,1024]{1,0:T(8,128)} %get-tuple-element.23), channel_id=1, source_target_pairs={{0,16},{32,48},{64,80},{96,112},{128,144},{160,176},{192,208},{224... | collective-permute-start | bytes 589832 | tf_op jit(solution)/shard_map/ppermute | solution.py:571
  30.1 0.0 copy-start
  30.1 0.0 copy-start.1
  30.1 0.0 copy-start.5
  30.1 0.0 copy-start.6
  30.2 0.0 copy-start.7
  30.2 0.0 copy-start.8
  30.2 0.8 collective-permute-start.1
  31.0 0.0 collective-permute-done.2.gyb
  31.0 0.0 collective-permute-done.3.gya
  31.0 0.0 copy-done.9
  31.0 0.0 copy-done.12
  31.0 0.6 shard_map.123
  31.7 3.4 %collective-permute-done.gxa = f32[48,1024]{1,0:T(8,128)S(1)} collective-permute-done((f32[48,1024]{1,0:T(8,128)}, f32[48,1024]{1,0:T(8,128)S(1)}, u32[]{:S(2)}, u32[]{:S(2)}) %collective-permute-start) | collective-permute-done | bytes 196640 | tf_op jit(solution)/shard_map/ppermute | solution.py:571
  35.1 0.0 collective-permute-done.1.gxb
  35.1 0.0 copy-start.11
  35.1 0.0 copy-done
  35.1 0.0 copy-done.1
  35.1 0.0 copy-done.5
  35.1 0.0 copy-done.6
  35.1 0.0 copy-done.7
  35.1 0.0 copy-done.8
  35.1 0.6 copy-done.11
  35.7 3.4 %shard_map.124 = (f32[8,16,1024]{2,1,0:T(8,128)S(1)}, f32[8,16,1024]{2,1,0:T(8,128)S(1)}, f32[7,16,1024]{2,1,0:T(8,128)S(1)}, f32[8,16,1024]{2,1,0:T(8,128)S(1)}...) custom-call(s32[8]{0:T(128)S(1)} %copy-done.11, ...), custom_call_target="tpu_custom_call" | custom-call | flops 1024 | bytes 1024 | tf_op jit(solution)/shard_map/pallas_call | solution.py:557
  39.1 5.9 %collective-permute-start.4 = (f32[272,128]{1,0:T(8,128)S(1)}, f32[272,128]{1,0:T(8,128)S(1)}, u32[]{:S(2)}, u32[]{:S(2)}) collective-permute-start(f32[272,128]{1,0:T(8,128)S(1)} %get-tuple-element.35), channel_id=1, source_target_pairs={{0,16},{32,48},{64,80},{96,112},{128,144},{160,176},{192,208},{224... | collective-permute-start | bytes 417800 | tf_op jit(solution)/shard_map/ppermute | solution.py:571
  45.0 0.7 collective-permute-start.5
  45.7 1.8 %collective-permute-done.4.ma = f32[272,128]{1,0:T(8,128)S(1)} collective-permute-done((f32[272,128]{1,0:T(8,128)S(1)}, f32[272,128]{1,0:T(8,128)S(1)}, u32[]{:S(2)}, u32[]{:S(2)}) %collective-permute-start.4) | collective-permute-done | bytes 139296 | tf_op jit(solution)/shard_map/ppermute | solution.py:571
  47.5 0.0 collective-permute-done.5.mb
  47.5 0.0 copy-start.3
  47.5 0.0 copy-start.4
  47.5 3.1 %shard_map.125 = (f32[8,16,1024]{2,1,0:T(8,128)}, f32[16,8,128]{2,1,0:T(8,128)S(1)}, f32[2,16,1024]{2,1,0:T(8,128)S(1)}, f32[2,48,128]{2,1,0:T(8,128)S(1)}) custom-call(s32[8]{0:T(128)S(1)} %copy-done.11, s32[2]{0:T(128)S(1)} %copy-done.12, f32[8,16,1024]{2,1,0:T(8,128)S(1)} %get-tuple-element.29.cond, f32[8,16,1024]{2,1,0:T(8,128)S(1)} %get-tuple-element.30.prior, ...), custom_call_target="tpu_custom_call" | custom-call | tf_op jit(solution)/shard_map/pallas_call | solution.py:557
  50.5 0.0 copy-start.2
  50.5 24.0 %all_to_all.10 = f32[16,8,128]{2,1,0:T(8,128)S(1)} all-to-all(f32[16,8,128]{2,1,0:T(8,128)S(1)} %get-tuple-element.40), channel_id=1, replica_groups=mesh['z_lo'=8,'x'=4,'y'=4,'z_hi'=2,'core'=2] {'z_hi','z_lo'}, dimensions={0} | all-to-all | bytes 131072 | tf_op jit(solution)/shard_map/all_to_all | solution.py:576
  74.5 0.7 broadcast_in_dim.3
  75.2 10.0 %all-to-all-start.1 = ((f32[32,8,128]{2,1,0:T(8,128)}), f32[32,8,128]{2,1,0:T(8,128)S(1)}, u32[]{:S(2)}, u32[]{:S(2)}) async-start(f32[32,8,128]{2,1,0:T(8,128)} %broadcast_in_dim.3), calls=%async_computation.1 | async-start | bytes 262144 | tf_op jit(solution)/shard_map/all_to_all | solution.py:576
  85.2 0.0 copy-done.3
  85.2 0.0 copy-done.4
  85.2 0.0 copy-done.2
  85.2 0.0 copy-start.10
  85.2 1.0 %copy-done.10 = f32[8,16,1024]{2,1,0:T(8,128)S(1)} copy-done((f32[8,16,1024]{2,1,0:T(8,128)S(1)}, f32[8,16,1024]{2,1,0:T(8,128)}, u32[]{:S(2)}) %copy-start.10) | copy-done | bytes 524312
  86.2 4.6 %shard_map.126 = f32[8,16,1024]{2,1,0:T(8,128)} custom-call(s32[8]{0:T(128)S(1)} %copy-done.11, s32[2]{0:T(128)S(1)} %copy-done.12, f32[8,16,1024]{2,1,0:T(8,128)S(1)} %get-tuple-element.29.cond, f32[8,16,1024]{2,1,0:T(8,128)S(1)} %copy-done.10, f32[2,16,1024]{2,1,0:T(8,128)S(1)} %get-tuple-element.38.sides, f32[8,16,1024]{2,1,0:T(8,128)S(1)} %copy-done.2, ...), custom_call_target="tpu_custom_call" | custom-call | flops 12582912 | bytes 12582912 | tf_op jit(solution)/shard_map/pallas_call | solution.py:557
  90.9 2.0 %all-to-all-done.1 = f32[32,8,128]{2,1,0:T(8,128)S(1)} async-done(((f32[32,8,128]{2,1,0:T(8,128)}), f32[32,8,128]{2,1,0:T(8,128)S(1)}, u32[]{:S(2)}, u32[]{:S(2)}) %all-to-all-start.1) | async-done | bytes 131104 | tf_op jit(solution)/shard_map/all_to_all | solution.py:576
  92.9 0.5 slice.3
  (2 shorter events, 0.1 us)
Async XLA Ops:
  4.1 26.9 %collective-permute-start.2 = (f32[6,8,128]{2,1,0:T(8,128)}, f32[6,8,128]{2,1,0:T(8,128)S(1)}, u32[]{:S(2)}, u32[]{:S(2)}) collective-permute-start(f32[6,8,128]{2,1,0:T(8,128)} %get-tuple-element.25), channel_id=1, source_target_pairs={{1,2},{3,4},{5,6},{7,8},{9,10},{11,12},{13,14},{2,1},{4,3},{6,5},{... | collective-permute-start | bytes 73736 | tf_op jit(solution)/shard_map/ppermute | solution.py:571
  21.0 10.0 %collective-permute-start.3 = (f32[6,8,128]{2,1,0:T(8,128)}, f32[6,8,128]{2,1,0:T(8,128)S(1)}, u32[]{:S(2)}, u32[]{:S(2)}) collective-permute-start(f32[6,8,128]{2,1,0:T(8,128)} %get-tuple-element.26), channel_id=1, source_target_pairs={{0,1},{2,3},{4,5},{6,7},{8,9},{10,11},{12,13},{14,15},{1,0},{3,2},... | collective-permute-start | bytes 73736 | tf_op jit(solution)/shard_map/ppermute | solution.py:571
  22.9 8.1 %copy-start.9 = (f32[2,6,16,128]{3,2,1,0:T(8,128)S(1)}, f32[2,6,16,128]{3,2,1,0:T(8,128)}, u32[]{:S(2)}) copy-start(f32[2,6,16,128]{3,2,1,0:T(8,128)} %get-tuple-element.22.after.own) | copy-start | bytes 294916
  27.0 4.1 %copy-start.12 = (s32[2]{0:T(128)S(1)}, s32[2]{0:T(128)}, u32[]{:S(2)}) copy-start(s32[2]{0:T(128)} %pad_add_fusion.pos) | copy-start | bytes 28
  27.0 8.1 %collective-permute-start = (f32[48,1024]{1,0:T(8,128)}, f32[48,1024]{1,0:T(8,128)S(1)}, u32[]{:S(2)}, u32[]{:S(2)}) collective-permute-start(f32[48,1024]{1,0:T(8,128)} %get-tuple-element.23), channel_id=1, source_target_pairs={{0,16},{32,48},{64,80},{96,112},{128,144},{160,176},{192,208},{224... | collective-permute-start | bytes 589832 | tf_op jit(solution)/shard_map/ppermute | solution.py:571
  30.1 5.0 %copy-start = (f32[8,16,1024]{2,1,0:T(8,128)S(1)}, f32[8,16,1024]{2,1,0:T(8,128)}, u32[]{:S(2)}) copy-start(f32[8,16,1024]{2,1,0:T(8,128)} %volts.1) | copy-start | bytes 1572868
  30.1 4.9 %copy-start.1 = (f32[8,16,1024]{2,1,0:T(8,128)S(1)}, f32[8,16,1024]{2,1,0:T(8,128)}, u32[]{:S(2)}) copy-start(f32[8,16,1024]{2,1,0:T(8,128)} %seg.1) | copy-start | bytes 1572868
  30.1 4.9 %copy-start.5 = (f32[7,16,1024]{2,1,0:T(8,128)S(1)}, f32[7,16,1024]{2,1,0:T(8,128)}, u32[]{:S(2)}) copy-start(f32[7,16,1024]{2,1,0:T(8,128)} %via_cond.1) | copy-start | bytes 1376260
  30.1 4.9 %copy-start.6 = (s32[7,16,1024]{2,1,0:T(8,128)S(1)}, s32[7,16,1024]{2,1,0:T(8,128)}, u32[]{:S(2)}) copy-start(s32[7,16,1024]{2,1,0:T(8,128)} %via_mask.1) | copy-start | bytes 1376260
  30.2 4.9 %copy-start.7 = (s32[16,1024]{1,0:T(8,128)S(1)}, s32[16,1024]{1,0:T(8,128)}, u32[]{:S(2)}) copy-start(s32[16,1024]{1,0:T(8,128)} %pad.7) | copy-start | bytes 196612
  30.2 4.9 %copy-start.8 = (f32[16,1024]{1,0:T(8,128)S(1)}, f32[16,1024]{1,0:T(8,128)}, u32[]{:S(2)}) copy-start(f32[16,1024]{1,0:T(8,128)} %load.3) | copy-start | bytes 196612
  30.2 4.9 %collective-permute-start.1 = (f32[48,1024]{1,0:T(8,128)}, f32[48,1024]{1,0:T(8,128)S(1)}, u32[]{:S(2)}, u32[]{:S(2)}) collective-permute-start(f32[48,1024]{1,0:T(8,128)} %get-tuple-element.24), channel_id=1, source_target_pairs={{16,32},{48,64},{80,96},{112,128},{144,160},{176,192},{208,224},{2... | collective-permute-start | bytes 589832 | tf_op jit(solution)/shard_map/ppermute | solution.py:571
  35.1 0.7 copy-start.11
  39.1 8.3 %collective-permute-start.4 = (f32[272,128]{1,0:T(8,128)S(1)}, f32[272,128]{1,0:T(8,128)S(1)}, u32[]{:S(2)}, u32[]{:S(2)}) collective-permute-start(f32[272,128]{1,0:T(8,128)S(1)} %get-tuple-element.35), channel_id=1, source_target_pairs={{0,16},{32,48},{64,80},{96,112},{128,144},{160,176},{192,208},{224... | collective-permute-start | bytes 417800 | tf_op jit(solution)/shard_map/ppermute | solution.py:571
  45.0 2.4 %collective-permute-start.5 = (f32[272,128]{1,0:T(8,128)S(1)}, f32[272,128]{1,0:T(8,128)S(1)}, u32[]{:S(2)}, u32[]{:S(2)}) collective-permute-start(f32[272,128]{1,0:T(8,128)S(1)} %get-tuple-element.36), channel_id=1, source_target_pairs={{16,32},{48,64},{80,96},{112,128},{144,160},{176,192},{208,224},{2... | collective-permute-start | bytes 417800 | tf_op jit(solution)/shard_map/ppermute | solution.py:571
  47.5 37.7 %copy-start.3 = (f32[8,16,1024]{2,1,0:T(8,128)S(1)}, f32[8,16,1024]{2,1,0:T(8,128)}, u32[]{:S(2)}) copy-start(f32[8,16,1024]{2,1,0:T(8,128)} %mob.1) | copy-start | bytes 1572868
  47.5 37.7 %copy-start.4 = (s32[8,16,1024]{2,1,0:T(8,128)S(1)}, s32[8,16,1024]{2,1,0:T(8,128)}, u32[]{:S(2)}) copy-start(s32[8,16,1024]{2,1,0:T(8,128)} %blk.1) | copy-start | bytes 1572868
  50.5 34.7 %copy-start.2 = (f32[8,16,1024]{2,1,0:T(8,128)S(1)}, f32[8,16,1024]{2,1,0:T(8,128)}, u32[]{:S(2)}) copy-start(f32[8,16,1024]{2,1,0:T(8,128)} %stress.1) | copy-start | bytes 1572868
  75.2 17.7 %all-to-all-start.1 = ((f32[32,8,128]{2,1,0:T(8,128)}), f32[32,8,128]{2,1,0:T(8,128)S(1)}, u32[]{:S(2)}, u32[]{:S(2)}) async-start(f32[32,8,128]{2,1,0:T(8,128)} %broadcast_in_dim.3), calls=%async_computation.1 | async-start | bytes 262144 | tf_op jit(solution)/shard_map/all_to_all | solution.py:576
  85.2 1.0 %copy-start.10 = (f32[8,16,1024]{2,1,0:T(8,128)S(1)}, f32[8,16,1024]{2,1,0:T(8,128)}, u32[]{:S(2)}) copy-start(f32[8,16,1024]{2,1,0:T(8,128)} %get-tuple-element.19.volts) | copy-start | bytes 1572868

commit v4 on v3

--- a/solution.py
+++ b/solution.py
@@ -22,6 +22,7 @@
 COST_ROWS = 2**20
 COST_STRIPS = 4000 * 2**20
 COST_EARLY = 1024
+COST_SETUP = 4 * 2**20
 
 damping = 0.8
 pad_conductance = 4.0
@@ -30,6 +31,18 @@
 
 X = ("z_lo", "x")
 Y = ("y", "z_hi", "core")
+NEAR = ("x", "y", "core")
+FAR = ("z_hi", "z_lo")
+
+
+def position():
+    out = []
+    for axes in (X, Y):
+        at = lax.axis_index(axes[0])
+        for a in axes[1:]:
+            at = at * lax.axis_size(a) + lax.axis_index(a)
+        out.append(at)
+    return out
 
 
 def iota(shape, dim):
@@ -56,37 +69,44 @@
     copies = [pltpu.make_async_copy(a, b, sems.at[i]) for i, (a, b) in enumerate(zip(sources, targets))]
     for copy in copies:
         copy.start()
-    for copy in copies:
-        copy.wait()
-
-
-def pack_columns(total_x, total_y, width, dirs, pos, *refs):
+    return copies
+
+
+def pack_columns(total_x, total_y, width, dirs, *refs):
     given, (own_ref, a_ref, b_ref), ins, sems = refs[:9], refs[9:12], refs[12:30], refs[30]
     parts = []
     for ref in given:
         for lanes in (slice(0, LANES), slice(width - LANES, width)):
             parts.append(ref.at[(slice(None),) * (len(ref.shape) - 1) + (lanes,)])
-    fetch(parts, ins, sems)
-    gx, gy = pos[0], pos[1]
+    copies = fetch(parts, ins, sems)
+    gx, gy = position()
     col = iota((1, 1, LANES), 2)
 
     def pick(i):
+        for copy in copies[2 * i : 2 * i + 2]:
+            copy.wait()
         first, last = ins[2 * i][...], ins[2 * i + 1][...]
         return jnp.where(col.reshape((1,) * (first.ndim - 1) + (LANES,)) < LANES // 2, first, last)
 
-    volts, seg, via_cond, via_mask, pad, load, stress, mob, blk = (pick(i) for i in range(9))
+    def field(f):
+        if f < 2:
+            return pick(f)
+        if f == 2:
+            return jnp.concatenate([pick(2) * pick(3).astype(jnp.float32), none], 0)
+        if f == 3:
+            top, load = pad_conductance * pick(4).astype(jnp.float32), pick(5)
+            return jnp.concatenate([load[None]] + [none] * (LAYERS - 2) + [top[None]], 0)
+        if f == 4:
+            return pick(6)
+        return pick(7) * (1.0 - pick(8).astype(jnp.float32))
+
     none = jnp.zeros((1, ROWS, LANES), jnp.float32)
-    via = jnp.concatenate([via_cond * via_mask.astype(jnp.float32), none], 0)
-    ends = jnp.concatenate(
-        [load[None]] + [none] * (LAYERS - 2) + [pad_conductance * pad.astype(jnp.float32)[None]], 0
-    )
-    mobile = mob * (1.0 - blk.astype(jnp.float32))
     shape = (OWN, LANES)
     along_y = lane_dirs(dirs, shape)
     x = gx * ROWS + iota(shape, 1) % ROWS
     even = gy % 2 == 0
-    for f, field in enumerate((volts, seg, via, ends, stress, mobile)):
-        turned = field.reshape(LANES, LANES).T
+    for f in range(FIELDS):
+        turned = field(f).reshape(LANES, LANES).T
         pieces = []
         for side, start in enumerate((0, LANES - OWN)):
             piece = turned[start : start + OWN]
@@ -109,11 +129,8 @@
     return (gy * shape[1] + iota(shape, 1) < total_y - 1).astype(jnp.float32)
 
 
-def pack_rows(total_x, dirs, pos, after, *refs):
-    given, (a_ref, b_ref), held_refs, sems = refs[:9], refs[9:11], refs[11:20], refs[20]
-    fetch(given, held_refs, sems)
-    volts, seg, via_cond, via_mask, pad, load, stress, mob, blk = held_refs
-    gx = pos[0]
+def pack_rows(total_x, dirs, volts, seg, via_cond, via_mask, pad, load, stress, mob, blk, a_ref, b_ref):
+    gx, _ = position()
     even = gx % 2 == 0
     width = volts.shape[2]
     inner = inner_x(gx, total_x, (ROWS, width))
@@ -203,19 +220,11 @@
     )
 
 
-def early_sweeps(
-    total_x, total_y, dirs, pos, volts, seg, via_cond, via_mask, pad, load, gxa, gxb, strips_a, strips_b,
-    cond_o, prior_o, via_o, diag_o, volts_o, edges_o, a_ref, b_ref, rate, one, two, halo, to_right, to_left,
+def conductances(
+    total_x, total_y, dirs, after_a, after_b, seg, via_cond, via_mask, pad, cond_o, prior_o, via_o, diag_o, rate_o,
 ):
-    gx, gy = pos[0], pos[1]
-    even = gx % 2 == 0
-    width = volts.shape[2]
-    slot = slots_of(dirs)
-
-    def near(right, row, lanes=slice(None)):
-        a, b = gxa[pl.ds(row, 1), lanes], gxb[pl.ds(row, 1), lanes]
-        return jnp.where(even, a, b) if right else jnp.where(even, b, a)
-
+    gx, gy = position()
+    width = seg.shape[2]
     for l in range(LAYERS):
         if l < LAYERS - 1:
             via_o[l] = via_cond[l] * via_mask[l].astype(jnp.float32)
@@ -224,7 +233,7 @@
         def _(l=l):
             cond = seg[l] * inner_x(gx, total_x, (ROWS, width))
             cond_o[l] = cond
-            prior_o[l] = shifted(cond, 0, near(False, slot[l] * EDGE + 2), 0.0)[0]
+            prior_o[l] = shifted(cond, 0, 0.0, 0.0)[0]
 
         @pl.when(dirs[l] == 1)
         def _(l=l):
@@ -241,7 +250,30 @@
         else:
             diag = diag + pad_conductance * pad[...].astype(jnp.float32)
         diag_o[l] = diag
-        rate[l] = damping / guarded(diag)
+        rate_o[l] = damping / guarded(diag)
+
+
+def early_sweeps(
+    dirs, cond_o, prior_i, via_o, diag_i, rate_i, volts, pad, load, gxa, gxb, strips_a, strips_b,
+    prior_o, diag_o, rate_o, volts_o, edges_o, a_ref, b_ref, one, two, halo, to_right, to_left,
+):
+    gx, gy = position()
+    even = gx % 2 == 0
+    width = volts.shape[2]
+    slot = slots_of(dirs)
+
+    def near(right, row, lanes=slice(None)):
+        a, b = gxa[pl.ds(row, 1), lanes], gxb[pl.ds(row, 1), lanes]
+        return jnp.where(even, a, b) if right else jnp.where(even, b, a)
+
+    for l in range(LAYERS):
+
+        @pl.when(dirs[l] == 0)
+        def _(l=l):
+            first = near(False, slot[l] * EDGE + 2)
+            prior_o[l, :1] = first
+            diag_o[l, :1] = diag_i[l, :1] + first
+            rate_o[l, :1] = damping / guarded(diag_o[l, :1])
 
     for sweep, (old, new) in enumerate(((volts, one), (one, two), (two, volts_o))):
         for l in range(LAYERS):
@@ -268,7 +300,7 @@
                         before = after = 0.0
                     prior, later = shifted(v, 0, before, after)
                     num = prior_o[(l, *at)] * prior + cond_o[(l, *at)] * later + rest_of(l, at, old, via_o, pad, load)
-                    result = (1.0 - damping) * v + rate[(l, *at)] * num
+                    result = (1.0 - damping) * v + rate_o[(l, *at)] * num
                     new[(l, *at)] = result
                     if sweep == 2:
                         edges_o[0, l : l + 1, lanes] = v[:1]
@@ -286,7 +318,7 @@
                     v = old[(l, *at)]
                     prior, later = shifted(v, 1, None, None)
                     num = prior_o[(l, *at)] * prior + cond_o[(l, *at)] * later + rest_of(l, at, old, via_o, pad, load)
-                    new[(l, *at)] = (1.0 - damping) * v + rate[(l, *at)] * num
+                    new[(l, *at)] = (1.0 - damping) * v + rate_o[(l, *at)] * num
                     if sweep == 2:
                         edges_o[:, l : l + 1, :] = jnp.zeros((2, 1, width), jnp.float32)
 
@@ -299,8 +331,8 @@
         b_ref[start : start + ROWS] = jnp.where(even, to_left[:, lanes], to_right[:, lanes])
 
 
-def pack_strips(pos, own, gyb, gya, a_ref, b_ref):
-    gx, gy = pos[0], pos[1]
+def pack_strips(own, gyb, gya, a_ref, b_ref):
+    gx, gy = position()
     even = gx % 2 == 0
     x = iota((STRIP, LANES), 1) % ROWS
     for f in range(FIELDS):
@@ -401,10 +433,10 @@
 
 
 def last_sweep(
-    dirs, pos, cond, prior, via, diag, pad, load, early, edges, gxa, gxb, own, gya, gyb, ma, mb,
+    dirs, cond, prior, via, diag, pad, load, early, edges, gxa, gxb, own, gya, gyb, ma, mb,
     volts_o, sum_o, sides_o, wind_o, sums, near_left, near_right,
 ):
-    gx, gy = pos[0], pos[1]
+    gx, gy = position()
     even = gx % 2 == 0
     width = early.shape[2]
     slot = slots_of(dirs)
@@ -492,10 +524,10 @@
 
 
 def stress_steps(
-    total_x, total_y, dirs, pos, cond, volts, sides, stress, mob, blk, gxa, gxb, own, gya, gyb, ma, mb, wind_strip,
+    total_x, total_y, dirs, cond, volts, sides, stress, mob, blk, gxa, gxb, own, gya, gyb, ma, mb, wind_strip,
     stress_o, ext_c, ext_m, ext_v, ext_s,
 ):
-    gx, gy = pos[0], pos[1]
+    gx, gy = position()
     even = gx % 2 == 0
     width = volts.shape[2]
     slot = slots_of(dirs)
@@ -550,7 +582,7 @@
     place(stress_o, strip_stress(dirs, gy % 2 == 0, even, own, gya, gyb, ma, mb, wind))
 
 
-def call(kernel, ins, outs, scratch=(), scalars=2, copies=0, cost=0):
+def call(kernel, ins, outs, scratch=(), scalars=1, copies=0, cost=0, aliases={}):
     smem, vmem = pl.BlockSpec(memory_space=pltpu.SMEM), pl.BlockSpec(memory_space=pltpu.VMEM)
     held = pl.BlockSpec(memory_space=pltpu.HBM) if copies else vmem
     scratch = [pltpu.VMEM(*(s if isinstance(s[0], tuple) else (s, jnp.float32))) for s in scratch]
@@ -559,8 +591,9 @@
         out_shape=[jax.ShapeDtypeStruct(s, jnp.float32) for s in outs],
         in_specs=[smem] * scalars + [held] * (len(ins) - scalars),
         out_specs=[vmem] * len(outs),
+        input_output_aliases=aliases,
         scratch_shapes=scratch + ([pltpu.SemaphoreType.DMA((copies,))] if copies else []),
-        compiler_params=pltpu.CompilerParams(vmem_limit_bytes=(62 if copies else 16) * 2**20),
+        compiler_params=pltpu.CompilerParams(vmem_limit_bytes=(57 if copies else 16) * 2**20),
         cost_estimate=pl.CostEstimate(flops=cost, bytes_accessed=cost, transcendentals=0),
     )(*ins)
 
@@ -571,62 +604,82 @@
     return lax.ppermute(value, axes, pairs + [(b, a) for a, b in pairs])
 
 
-def sum_all(held):
-    for axes, then in ((("z_hi", "z_lo"), ("x", "y", "core")), (("x", "y", "core"), ())):
-        total = jnp.sum(lax.all_to_all(held, axes, 0, 0), 0)
-        held = jnp.broadcast_to(total, (lax.axis_size(then), 8, LANES)) if then else total
-    return held[0, 0]
+def partial_sum(held, out):
+    total = held[0]
+    for i in range(1, held.shape[0]):
+        total = total + held[i]
+    for i in range(out.shape[0]):
+        out[i] = total
+
+
+def root_mean(count, held, out):
+    total = jnp.sum(held[...][:, :1, :1])
+    out[...] = jnp.sqrt(jnp.full((1, LANES), total / count, jnp.float32))
+
+
+def rms_all(held, count):
+    got = lax.all_to_all(held, NEAR, 0, 0)
+    (held,) = call(partial_sum, (got,), [(lax.axis_size(FAR), 1, LANES)], scalars=0)
+    got = lax.all_to_all(held, FAR, 0, 0)
+    (out,) = call(functools.partial(root_mean, count), (got,), [(1, LANES)], scalars=0)
+    return out[0, 0]
 
 
 def body(volts_start, seg_cond, via_cond, via_mask, pad_mask, load_current, stress_start, mobility, blocked, layer_dirs):
     layers, rows, width = seg_cond.shape
     total_x, total_y = rows * lax.axis_size(X), width * lax.axis_size(Y)
-    pos = jnp.stack([lax.axis_index(X), lax.axis_index(Y)]).astype(jnp.int32)
     shape = (layers, rows, width)
     fields = (volts_start, seg_cond, via_cond, via_mask, pad_mask, load_current, stress_start, mobility, blocked)
     column = (FIELDS, REACH, LANES)
     own, gya, gyb = call(
         functools.partial(pack_columns, total_x, total_y, width),
-        (layer_dirs, pos, *fields),
+        (layer_dirs, *fields),
         [(2, FIELDS, OWN, LANES), column, column],
         scratch=[(a.shape[:-1] + (LANES,), a.dtype) for a in fields for _ in range(2)],
         copies=18,
     )
     gyb, gya = swap(gyb, Y, 1), swap(gya, Y, 0)
+    own, fields = lax.optimization_barrier((own, fields))
     gxa, gxb = call(
         functools.partial(pack_rows, total_x),
-        (layer_dirs, pos, own, *fields),
+        (layer_dirs, *fields),
         [(SLOTS * EDGE, width)] * 2,
-        scratch=[(a.shape, a.dtype) for a in fields],
-        copies=9,
         cost=COST_ROWS,
     )
+    sent_a, sent_b = gxa, gxb
     gxa, gxb = swap(gxa, X, 0), swap(gxb, X, 1)
     side = (FIELDS * STRIP, LANES)
-    sa, sb = call(pack_strips, (pos, own, gyb, gya), [side, side], scalars=1, cost=COST_STRIPS)
+    sa, sb = call(pack_strips, (own, gyb, gya), [side, side], scalars=0, cost=COST_STRIPS)
     message = (FIELDS * STRIP + ROWS * (width // LANES), LANES)
-    cond, prior, via, diag, early, edges, ma, mb = call(
-        functools.partial(early_sweeps, total_x, total_y),
-        (layer_dirs, pos, *fields[:6], gxa, gxb, sa, sb),
-        [shape, shape, (layers - 1, rows, width), shape, shape, (2, layers, width), message, message],
-        scratch=[shape, shape, shape, (2, SLOTS, width), (ROWS, width), (ROWS, width)],
+    cond, prior, via, diag, rate = call(
+        functools.partial(conductances, total_x, total_y),
+        (layer_dirs, sent_a, sent_b, *fields[1:5]),
+        [shape, shape, (layers - 1, rows, width), shape, shape],
+        cost=COST_SETUP,
+    )
+    prior, diag, _, early, edges, ma, mb = call(
+        early_sweeps,
+        (layer_dirs, cond, prior, via, diag, rate, fields[0], *fields[4:6], gxa, gxb, sa, sb),
+        [shape, shape, shape, shape, (2, layers, width), message, message],
+        scratch=[shape, shape, (2, SLOTS, width), (ROWS, width), (ROWS, width)],
         cost=COST_EARLY,
+        aliases={2: 0, 4: 1, 5: 2},
     )
     ma, mb = swap(ma, X, 0), swap(mb, X, 1)
     volts, held, sides, wind = call(
         last_sweep,
-        (layer_dirs, pos, cond, prior, via, diag, pad_mask, load_current, early, edges, gxa, gxb, own, gya, gyb, ma, mb),
-        [shape, (lax.axis_size(("z_hi", "z_lo")), 8, LANES), (2, ROWS, width), (2, 2 * STRIP, LANES)],
+        (layer_dirs, cond, prior, via, diag, *fields[4:6], early, edges, gxa, gxb, own, gya, gyb, ma, mb),
+        [shape, (lax.axis_size(NEAR), 1, LANES), (2, ROWS, width), (2, 2 * STRIP, LANES)],
         scratch=[(8, LANES), (ROWS, width), (ROWS, width)],
     )
     (stress,) = call(
         functools.partial(stress_steps, total_x, total_y),
-        (layer_dirs, pos, cond, volts, sides, *fields[6:], gxa, gxb, own, gya, gyb, ma, mb, wind),
+        (layer_dirs, cond, volts, sides, *fields[6:], gxa, gxb, own, gya, gyb, ma, mb, wind),
         [shape],
         scratch=[(32, width)] * 4,
         cost=12 * 2**20,
     )
-    resid_rms = jnp.sqrt(sum_all(held) / (layers * total_x * total_y))
+    resid_rms = rms_all(held, layers * total_x * total_y)
     return volts, stress, resid_rms
 
 

time: 95.8 us -> 86.7 us (0.905)
  starting transfers between devices: 39.2 us -> 34.6 us
  waiting for transfers between devices: 7.13 us -> 9.96 us
  between operations: 2.72 us -> 0.93 us
  local copies, waits for them, and re-layouts: 2.87 us -> 1.09 us
  blocking collectives: 24 us -> 22.3 us
  Pallas kernels: 18.6 us -> 17.3 us
    all_to_all x1, starting transfers between devices: 9.97 us -> 5.45 us  [rms_all(): got = lax.all_to_all(held, FAR, 0, 0)]
    all_to_all x1, waiting for transfers between devices: 2 us -> 5.63 us  [rms_all(): got = lax.all_to_all(held, FAR, 0, 0)]
    all_to_all x1, blocking collectives: 24 us -> 22.3 us  [rms_all(): got = lax.all_to_all(held, NEAR, 0, 0)]
    pallas_call x6 -> x9, Pallas kernels: 18.6 us -> 17.3 us  [call(): pl.pallas_call(kernel, out_shape=[jax.ShapeDtypeStruct(s, jnp.float32) fo...]
  transfers between devices with their start and end apart: 7 -> 7, of which waited for: 3 -> 3; matrix products, arithmetic and copies ran while one was open for 0% -> 0% of each run, Pallas kernels for 10% -> 8%
where the time goes in v4:
time: 86.7 us; the launch traced here: 86.2 us
  starting transfers between devices  34.6 us (40%)
  blocking collectives  22.3 us (26%)
  Pallas kernels  17.3 us (20%)
  waiting for transfers between devices  9.96 us (11%)
  local copies, waits for them, and re-layouts  1.09 us (1%)
  between operations  0.93 us (1%)
    ppermute x6, starting transfers between devices, swap(): return lax.ppermute(value, axes, pairs + [(b, a) for a, b in pairs])  29.2 us
    all_to_all x1, blocking collectives, rms_all(): got = lax.all_to_all(held, NEAR, 0, 0)  22.3 us
    pallas_call x9, Pallas kernels, call(): pl.pallas_call(kernel, out_shape=[jax.ShapeDtypeStruct(s, jnp.float32) fo...  17.3 us
    all_to_all x1, waiting for transfers between devices, rms_all(): got = lax.all_to_all(held, FAR, 0, 0)  5.63 us
    all_to_all x1, starting transfers between devices, rms_all(): got = lax.all_to_all(held, FAR, 0, 0)  5.45 us
    ppermute x6, waiting for transfers between devices, swap(): return lax.ppermute(value, axes, pairs + [(b, a) for a, b in pairs])  4.33 us
  transfers between devices with their start and end apart: 7, of which 3 were waited for; matrix products, arithmetic and copies ran while one was open for 0% of the time, Pallas kernels for 8%

profile of v4, /device:TPU:1, one launch (start us, length us, event | category | flops | bytes accessed | tf_op | source)
XLA Modules:
  0.0 86.2 jit_solution(8112186324568505425)
XLA Ops:
  0.6 0.0 copy-start.2
  0.6 0.0 copy-start.1
  0.7 0.0 copy-start
  0.7 0.0 copy-start.8
  0.7 0.0 copy-start.7
  0.7 0.0 copy-start.6
  0.7 0.0 copy-start.5
  0.7 0.0 copy-start.3
  0.7 0.0 copy-start.4
  0.7 3.3 %shard_map.121 = (f32[2,6,16,128]{3,2,1,0:T(8,128)}, f32[6,8,128]{2,1,0:T(8,128)}, f32[6,8,128]{2,1,0:T(8,128)}) custom-call(s32[8]{0:T(128)} %dirs.11, f32[8,16,1024]{2,1,0:T(8,128)} %volts.1, f32[8,16,1024]{2,1,0:T(8,128)} %seg.1, f32[7,16,1024]{2,1,0:T(8,128)} %via_cond.1, s32[7,16,1024]{2,1,0:T(8,128)} %via_mask.1, s32[16,1024]{1,0:T(8,128)} %pad.3, ...), custom_call_target="tpu_custom_call" | custom-call | tf_op jit(solution)/shard_map/pallas_call | solution.py:589
  4.1 16.8 %collective-permute-start.2 = (f32[6,8,128]{2,1,0:T(8,128)}, f32[6,8,128]{2,1,0:T(8,128)S(1)}, u32[]{:S(2)}, u32[]{:S(2)}) collective-permute-start(f32[6,8,128]{2,1,0:T(8,128)} %get-tuple-element.53), channel_id=1, source_target_pairs={{1,2},{3,4},{5,6},{7,8},{9,10},{11,12},{13,14},{2,1},{4,3},{6,5},{... | collective-permute-start | bytes 73736 | tf_op jit(solution)/shard_map/ppermute | solution.py:604
  20.9 0.0 copy-start.11
  20.9 1.9 %collective-permute-start.3 = (f32[6,8,128]{2,1,0:T(8,128)}, f32[6,8,128]{2,1,0:T(8,128)S(1)}, u32[]{:S(2)}, u32[]{:S(2)}) collective-permute-start(f32[6,8,128]{2,1,0:T(8,128)} %get-tuple-element.54), channel_id=1, source_target_pairs={{0,1},{2,3},{4,5},{6,7},{8,9},{10,11},{12,13},{14,15},{1,0},{3,2},... | collective-permute-start | bytes 73736 | tf_op jit(solution)/shard_map/ppermute | solution.py:604
  22.8 0.0 copy-done.2
  22.9 0.0 copy-done.1
  22.9 0.0 copy-done
  22.9 0.0 copy-done.8
  22.9 0.0 copy-done.7
  22.9 0.0 copy-done.6
  22.9 0.0 copy-done.5
  22.9 0.0 copy-done.3
  22.9 0.0 copy-done.4
  22.9 0.0 copy-done.11
  22.9 1.0 %shard_map.122 = (f32[48,1024]{1,0:T(8,128)S(1)}, f32[48,1024]{1,0:T(8,128)S(1)}) custom-call(s32[8]{0:T(128)S(1)} %copy-done.11, f32[8,16,1024]{2,1,0:T(8,128)S(1)} %copy-done.4, f32[8,16,1024]{2,1,0:T(8,128)S(1)} %copy-done.3, f32[7,16,1024]{2,1,0:T(8,128)S(1)} %copy-done.5, s32[7,16,1024]{2,1,0:T(8,128)S(1)} %copy-done.6, s32[16,1024]{1,0:T(8,128)S(1)} %copy-done.7, ...), custom_call_target="tpu_custom_call" | custom-call | flops 1048576 | bytes 1048576 | tf_op jit(solution)/shard_map/pallas_call | solution.py:589
  23.9 3.1 %collective-permute-start = (f32[48,1024]{1,0:T(8,128)S(1)}, f32[48,1024]{1,0:T(8,128)S(1)}, u32[]{:S(2)}, u32[]{:S(2)}) collective-permute-start(f32[48,1024]{1,0:T(8,128)S(1)} %get-tuple-element.45.after_a), channel_id=1, source_target_pairs={{0,16},{32,48},{64,80},{96,112},{128,144},{160,176},{192,208},{224... | collective-permute-start | bytes 589832 | tf_op jit(solution)/shard_map/ppermute | solution.py:604
  27.1 0.0 copy-start.10
  27.1 0.8 collective-permute-start.1
  27.9 1.2 %shard_map.123 = (f32[8,16,1024]{2,1,0:T(8,128)S(1)}, f32[8,16,1024]{2,1,0:T(8,128)S(1)}, f32[7,16,1024]{2,1,0:T(8,128)S(1)}, f32[8,16,1024]{2,1,0:T(8,128)S(1)}, f32[8,16,1024]{2,1,0:T(8,128)S(1)}) custom-call(s32[8]{0:T(128)S(1)} %copy-done.11, f32[48,1024]{1,0:T(8,128)S(1)} %get-tuple-element.45.after_a, f32[48,1024]{1,0:T(8,128)S(1)} %get-tuple-element.46.after_b, ...), custom_call_target="tpu_custom_call" | custom-call | flops 4194304 | bytes 4194304 | tf_op jit(solution)/shard_map/pallas_call | solution.py:589
  29.1 0.0 collective-permute-done.2.gyb
  29.1 0.0 collective-permute-done.3.gya
  29.1 0.0 copy-done.10
  29.1 0.1 shard_map.124
  29.2 2.6 %collective-permute-done.gxa = f32[48,1024]{1,0:T(8,128)S(1)} collective-permute-done((f32[48,1024]{1,0:T(8,128)S(1)}, f32[48,1024]{1,0:T(8,128)S(1)}, u32[]{:S(2)}, u32[]{:S(2)}) %collective-permute-start) | collective-permute-done | bytes 196640 | tf_op jit(solution)/shard_map/ppermute | solution.py:604
  31.8 0.0 collective-permute-done.1.gxb
  31.8 2.7 %shard_map.125 = (f32[8,16,1024]{2,1,0:T(8,128)S(1)}, f32[8,16,1024]{2,1,0:T(8,128)S(1)}, f32[8,16,1024]{2,1,0:T(8,128)S(1)}, f32[8,16,1024]{2,1,0:T(8,128)S(1)}...) custom-call(s32[8]{0:T(128)S(1)} %copy-done.11, ...), custom_call_target="tpu_custom_call", output_to_operand_aliasing={{0}: (2, {}), {1}: (4, {}), {2}: (5, {})} | custom-call | flops 1024 | bytes 1024 | tf_op jit(solution)/shard_map/pallas_call | solution.py:589
  34.6 5.8 %collective-permute-start.4 = (f32[272,128]{1,0:T(8,128)S(1)}, f32[272,128]{1,0:T(8,128)S(1)}, u32[]{:S(2)}, u32[]{:S(2)}) collective-permute-start(f32[272,128]{1,0:T(8,128)S(1)} %get-tuple-element.61), channel_id=1, source_target_pairs={{0,16},{32,48},{64,80},{96,112},{128,144},{160,176},{192,208},{224... | collective-permute-start | bytes 417800 | tf_op jit(solution)/shard_map/ppermute | solution.py:604
  40.4 0.7 collective-permute-start.5
  41.1 1.8 %collective-permute-done.4.ma = f32[272,128]{1,0:T(8,128)S(1)} collective-permute-done((f32[272,128]{1,0:T(8,128)S(1)}, f32[272,128]{1,0:T(8,128)S(1)}, u32[]{:S(2)}, u32[]{:S(2)}) %collective-permute-start.4) | collective-permute-done | bytes 139296 | tf_op jit(solution)/shard_map/ppermute | solution.py:604
  42.8 0.0 collective-permute-done.5.mb
  42.8 3.0 %shard_map.126 = (f32[8,16,1024]{2,1,0:T(8,128)}, f32[32,1,128]{2,1,0:T(1,128)S(1)}, f32[2,16,1024]{2,1,0:T(8,128)S(1)}, f32[2,48,128]{2,1,0:T(8,128)S(1)}) custom-call(s32[8]{0:T(128)S(1)} %copy-done.11, f32[8,16,1024]{2,1,0:T(8,128)S(1)} %get-tuple-element.47.cond_o.cond, f32[8,16,1024]{2,1,0:T(8,128)S(1)} %get-tuple-element.57.prior, ...), custom_call_target="tpu_custom_call" | custom-call | tf_op jit(solution)/shard_map/pallas_call | solution.py:589
  45.9 22.3 %all_to_all.10.held = f32[32,1,128]{2,1,0:T(1,128)S(1)} all-to-all(f32[32,1,128]{2,1,0:T(1,128)S(1)} %get-tuple-element.66), channel_id=1, replica_groups=mesh['z_lo'=8,'x'=4,'y'=4,'z_hi'=2,'core'=2] {'x','y','core'}, dimensions={0} | all-to-all | bytes 32768 | tf_op jit(solution)/shard_map/all_to_all | solution.py:621
  68.2 0.6 shard_map.128
  68.8 5.4 %all-to-all-start.1 = ((f32[16,1,128]{2,1,0:T(1,128)}), f32[16,1,128]{2,1,0:T(1,128)S(1)}, u32[]{:S(2)}, u32[]{:S(2)}) async-start(f32[16,1,128]{2,1,0:T(1,128)} %shard_map.128), calls=%async_computation.1 | async-start | bytes 16384 | tf_op jit(solution)/shard_map/all_to_all | solution.py:623
  74.3 0.0 copy-start.9
  74.3 1.0 %copy-done.9 = f32[8,16,1024]{2,1,0:T(8,128)S(1)} copy-done((f32[8,16,1024]{2,1,0:T(8,128)S(1)}, f32[8,16,1024]{2,1,0:T(8,128)}, u32[]{:S(2)}) %copy-start.9) | copy-done | bytes 524312
  75.3 4.6 %shard_map.127 = f32[8,16,1024]{2,1,0:T(8,128)} custom-call(s32[8]{0:T(128)S(1)} %copy-done.11, f32[8,16,1024]{2,1,0:T(8,128)S(1)} %get-tuple-element.47.cond_o.cond, f32[8,16,1024]{2,1,0:T(8,128)S(1)} %copy-done.9, f32[2,16,1024]{2,1,0:T(8,128)S(1)} %get-tuple-element.64.sides, f32[8,16,1024]{2,1,0:T(8,128)S(1)} %copy-done, f32[8,16,1024]{2,1,0:T(8,128)S(1)} %copy-done.1, ...), custom_call_target="tpu_custom_call" | custom-call | flops 12582912 | bytes 12582912 | tf_op jit(solution)/shard_map/pallas_call | solution.py:589
  80.0 5.6 %all-to-all-done.1.held = f32[16,1,128]{2,1,0:T(1,128)S(1)} async-done(((f32[16,1,128]{2,1,0:T(1,128)}), f32[16,1,128]{2,1,0:T(1,128)S(1)}, u32[]{:S(2)}, u32[]{:S(2)}) %all-to-all-start.1) | async-done | bytes 8224 | tf_op jit(solution)/shard_map/all_to_all | solution.py:623
  85.6 0.7 shard_map.129
Async XLA Ops:
  0.6 22.2 %copy-start.2 = (s32[8,16,1024]{2,1,0:T(8,128)S(1)}, s32[8,16,1024]{2,1,0:T(8,128)}, u32[]{:S(2)}) copy-start(s32[8,16,1024]{2,1,0:T(8,128)} %blk.1) | copy-start | bytes 1572868
  0.6 22.2 %copy-start.1 = (f32[8,16,1024]{2,1,0:T(8,128)S(1)}, f32[8,16,1024]{2,1,0:T(8,128)}, u32[]{:S(2)}) copy-start(f32[8,16,1024]{2,1,0:T(8,128)} %mob.1) | copy-start | bytes 1572868
  0.7 22.2 %copy-start = (f32[8,16,1024]{2,1,0:T(8,128)S(1)}, f32[8,16,1024]{2,1,0:T(8,128)}, u32[]{:S(2)}) copy-start(f32[8,16,1024]{2,1,0:T(8,128)} %stress.1) | copy-start | bytes 1572868
  0.7 22.2 %copy-start.8 = (f32[16,1024]{1,0:T(8,128)S(1)}, f32[16,1024]{1,0:T(8,128)}, u32[]{:S(2)}) copy-start(f32[16,1024]{1,0:T(8,128)} %load.2) | copy-start | bytes 196612
  0.7 22.2 %copy-start.7 = (s32[16,1024]{1,0:T(8,128)S(1)}, s32[16,1024]{1,0:T(8,128)}, u32[]{:S(2)}) copy-start(s32[16,1024]{1,0:T(8,128)} %pad.3) | copy-start | bytes 196612
  0.7 22.2 %copy-start.6 = (s32[7,16,1024]{2,1,0:T(8,128)S(1)}, s32[7,16,1024]{2,1,0:T(8,128)}, u32[]{:S(2)}) copy-start(s32[7,16,1024]{2,1,0:T(8,128)} %via_mask.1) | copy-start | bytes 1376260
  0.7 22.2 %copy-start.5 = (f32[7,16,1024]{2,1,0:T(8,128)S(1)}, f32[7,16,1024]{2,1,0:T(8,128)}, u32[]{:S(2)}) copy-start(f32[7,16,1024]{2,1,0:T(8,128)} %via_cond.1) | copy-start | bytes 1376260
  0.7 22.2 %copy-start.3 = (f32[8,16,1024]{2,1,0:T(8,128)S(1)}, f32[8,16,1024]{2,1,0:T(8,128)}, u32[]{:S(2)}) copy-start(f32[8,16,1024]{2,1,0:T(8,128)} %seg.1) | copy-start | bytes 1572868
  0.7 22.2 %copy-start.4 = (f32[8,16,1024]{2,1,0:T(8,128)S(1)}, f32[8,16,1024]{2,1,0:T(8,128)}, u32[]{:S(2)}) copy-start(f32[8,16,1024]{2,1,0:T(8,128)} %volts.1) | copy-start | bytes 1572868
  4.1 25.0 %collective-permute-start.2 = (f32[6,8,128]{2,1,0:T(8,128)}, f32[6,8,128]{2,1,0:T(8,128)S(1)}, u32[]{:S(2)}, u32[]{:S(2)}) collective-permute-start(f32[6,8,128]{2,1,0:T(8,128)} %get-tuple-element.53), channel_id=1, source_target_pairs={{1,2},{3,4},{5,6},{7,8},{9,10},{11,12},{13,14},{2,1},{4,3},{6,5},{... | collective-permute-start | bytes 73736 | tf_op jit(solution)/shard_map/ppermute | solution.py:604
  20.9 2.0 %copy-start.11 = (s32[8]{0:T(128)S(1)}, s32[8]{0:T(128)}, u32[]{:S(2)}) copy-start(s32[8]{0:T(128)} %dirs.11) | copy-start | bytes 100
  20.9 8.2 %collective-permute-start.3 = (f32[6,8,128]{2,1,0:T(8,128)}, f32[6,8,128]{2,1,0:T(8,128)S(1)}, u32[]{:S(2)}, u32[]{:S(2)}) collective-permute-start(f32[6,8,128]{2,1,0:T(8,128)} %get-tuple-element.54), channel_id=1, source_target_pairs={{0,1},{2,3},{4,5},{6,7},{8,9},{10,11},{12,13},{14,15},{1,0},{3,2},... | collective-permute-start | bytes 73736 | tf_op jit(solution)/shard_map/ppermute | solution.py:604
  23.9 7.9 %collective-permute-start = (f32[48,1024]{1,0:T(8,128)S(1)}, f32[48,1024]{1,0:T(8,128)S(1)}, u32[]{:S(2)}, u32[]{:S(2)}) collective-permute-start(f32[48,1024]{1,0:T(8,128)S(1)} %get-tuple-element.45.after_a), channel_id=1, source_target_pairs={{0,16},{32,48},{64,80},{96,112},{128,144},{160,176},{192,208},{224... | collective-permute-start | bytes 589832 | tf_op jit(solution)/shard_map/ppermute | solution.py:604
  27.1 2.0 %copy-start.10 = (f32[2,6,16,128]{3,2,1,0:T(8,128)S(1)}, f32[2,6,16,128]{3,2,1,0:T(8,128)}, u32[]{:S(2)}) copy-start(f32[2,6,16,128]{3,2,1,0:T(8,128)} %get-tuple-element.52.own) | copy-start | bytes 294916
  27.1 4.7 %collective-permute-start.1 = (f32[48,1024]{1,0:T(8,128)S(1)}, f32[48,1024]{1,0:T(8,128)S(1)}, u32[]{:S(2)}, u32[]{:S(2)}) collective-permute-start(f32[48,1024]{1,0:T(8,128)S(1)} %get-tuple-element.46.after_b), channel_id=1, source_target_pairs={{16,32},{48,64},{80,96},{112,128},{144,160},{176,192},{208,224},{2... | collective-permute-start | bytes 589832 | tf_op jit(solution)/shard_map/ppermute | solution.py:604
  34.6 8.3 %collective-permute-start.4 = (f32[272,128]{1,0:T(8,128)S(1)}, f32[272,128]{1,0:T(8,128)S(1)}, u32[]{:S(2)}, u32[]{:S(2)}) collective-permute-start(f32[272,128]{1,0:T(8,128)S(1)} %get-tuple-element.61), channel_id=1, source_target_pairs={{0,16},{32,48},{64,80},{96,112},{128,144},{160,176},{192,208},{224... | collective-permute-start | bytes 417800 | tf_op jit(solution)/shard_map/ppermute | solution.py:604
  40.4 2.4 %collective-permute-start.5 = (f32[272,128]{1,0:T(8,128)S(1)}, f32[272,128]{1,0:T(8,128)S(1)}, u32[]{:S(2)}, u32[]{:S(2)}) collective-permute-start(f32[272,128]{1,0:T(8,128)S(1)} %get-tuple-element.62), channel_id=1, source_target_pairs={{16,32},{48,64},{80,96},{112,128},{144,160},{176,192},{208,224},{2... | collective-permute-start | bytes 417800 | tf_op jit(solution)/shard_map/ppermute | solution.py:604
  68.8 16.8 %all-to-all-start.1 = ((f32[16,1,128]{2,1,0:T(1,128)}), f32[16,1,128]{2,1,0:T(1,128)S(1)}, u32[]{:S(2)}, u32[]{:S(2)}) async-start(f32[16,1,128]{2,1,0:T(1,128)} %shard_map.128), calls=%async_computation.1 | async-start | bytes 16384 | tf_op jit(solution)/shard_map/all_to_all | solution.py:623
  74.3 1.0 %copy-start.9 = (f32[8,16,1024]{2,1,0:T(8,128)S(1)}, f32[8,16,1024]{2,1,0:T(8,128)}, u32[]{:S(2)}) copy-start(f32[8,16,1024]{2,1,0:T(8,128)} %get-tuple-element.32.volts) | copy-start | bytes 1572868

commit v5 on v4

--- a/solution.py
+++ b/solution.py
@@ -221,7 +221,8 @@
 
 
 def conductances(
-    total_x, total_y, dirs, after_a, after_b, seg, via_cond, via_mask, pad, cond_o, prior_o, via_o, diag_o, rate_o,
+    total_x, total_y, dirs, after_a, after_b, volts, seg, via_cond, via_mask, pad, load,
+    cond_o, prior_o, via_o, diag_o, rate_o, volts_o,
 ):
     gx, gy = position()
     width = seg.shape[2]
@@ -252,10 +253,21 @@
         diag_o[l] = diag
         rate_o[l] = damping / guarded(diag)
 
+    for l in range(LAYERS):
+        for along_y in (False, True):
+
+            @pl.when(dirs[l] == int(along_y))
+            def _(l=l, along_y=along_y):
+                for at in blocks(width, along_y):
+                    v = volts[(l, *at)]
+                    prior, later = shifted(v, int(along_y), 0.0, 0.0)
+                    num = prior_o[(l, *at)] * prior + cond_o[(l, *at)] * later + rest_of(l, at, volts, via_o, pad, load)
+                    volts_o[(l, *at)] = (1.0 - damping) * v + rate_o[(l, *at)] * num
+
 
 def early_sweeps(
-    dirs, cond_o, prior_i, via_o, diag_i, rate_i, volts, pad, load, gxa, gxb, strips_a, strips_b,
-    prior_o, diag_o, rate_o, volts_o, edges_o, a_ref, b_ref, one, two, halo, to_right, to_left,
+    dirs, cond_o, prior_i, via_o, diag_i, rate_i, first_v, volts, pad, load, gxa, gxb, strips_a, strips_b,
+    prior_o, diag_o, volts_o, edges_o, a_ref, b_ref, rate_o, one, two, halo, to_right, to_left,
 ):
     gx, gy = position()
     even = gx % 2 == 0
@@ -268,33 +280,39 @@
 
     for l in range(LAYERS):
 
+        one[l] = first_v[l]
+
         @pl.when(dirs[l] == 0)
         def _(l=l):
-            first = near(False, slot[l] * EDGE + 2)
-            prior_o[l, :1] = first
-            diag_o[l, :1] = diag_i[l, :1] + first
-            rate_o[l, :1] = damping / guarded(diag_o[l, :1])
-
-    for sweep, (old, new) in enumerate(((volts, one), (one, two), (two, volts_o))):
+            base = slot[l] * EDGE
+            before, after, cond_left = near(False, base + 9), near(True, base + 9), near(False, base + 2)
+            v, last = volts[l], cond_o[l, ROWS - 1 :]
+            prior_o[l], diag_o[l], rate_o[l] = prior_i[l], diag_i[l], rate_i[l]
+            prior_o[l, :1] = cond_left
+            diag = diag_i[l, :1] + cond_left
+            diag_o[l, :1] = diag
+            rate = damping / guarded(diag)
+            rate_o[l, :1] = rate
+            end = (slice(0, 1), slice(None))
+            num = cond_left * before + cond_o[l, :1] * v[1:2] + rest_of(l, end, volts, via_o, pad, load)
+            one[l, :1] = (1.0 - damping) * v[:1] + rate * num
+            one[l, ROWS - 1 :] = first_v[l, ROWS - 1 :] + rate_i[l, ROWS - 1 :] * last * after
+            halo[0, pl.ds(slot[l], 1), :] = (1.0 - damping) * before + damping * (
+                near(False, base + 10) + cond_left * v[:1]
+            ) / guarded(near(False, base + 11))
+            halo[1, pl.ds(slot[l], 1), :] = (1.0 - damping) * after + damping * (
+                near(True, base + 10) + last * v[ROWS - 1 :]
+            ) / guarded(near(True, base + 11) + last)
+
+    for sweep, (old, new) in ((1, (one, two)), (2, (two, volts_o))):
         for l in range(LAYERS):
 
             @pl.when(dirs[l] == 0)
             def _(l=l):
-                base = slot[l] * EDGE
                 for at in blocks(width, False):
                     lanes = at[1]
                     v = old[(l, *at)]
-                    if sweep == 0:
-                        before, after = near(False, base + 9, lanes), near(True, base + 9, lanes)
-                        cond_left = near(False, base + 2, lanes)
-                        last = cond_o[l, ROWS - 1 :, lanes]
-                        halo[0, pl.ds(slot[l], 1), lanes] = (1.0 - damping) * before + damping * (
-                            near(False, base + 10, lanes) + cond_left * v[:1]
-                        ) / guarded(near(False, base + 11, lanes))
-                        halo[1, pl.ds(slot[l], 1), lanes] = (1.0 - damping) * after + damping * (
-                            near(True, base + 10, lanes) + last * v[ROWS - 1 :]
-                        ) / guarded(near(True, base + 11, lanes) + last)
-                    elif sweep == 1:
+                    if sweep == 1:
                         before, after = halo[0, pl.ds(slot[l], 1), lanes], halo[1, pl.ds(slot[l], 1), lanes]
                     else:
                         before = after = 0.0
@@ -317,8 +335,8 @@
                 for at in blocks(width, True):
                     v = old[(l, *at)]
                     prior, later = shifted(v, 1, None, None)
-                    num = prior_o[(l, *at)] * prior + cond_o[(l, *at)] * later + rest_of(l, at, old, via_o, pad, load)
-                    new[(l, *at)] = (1.0 - damping) * v + rate_o[(l, *at)] * num
+                    num = prior_i[(l, *at)] * prior + cond_o[(l, *at)] * later + rest_of(l, at, old, via_o, pad, load)
+                    new[(l, *at)] = (1.0 - damping) * v + rate_i[(l, *at)] * num
                     if sweep == 2:
                         edges_o[:, l : l + 1, :] = jnp.zeros((2, 1, width), jnp.float32)
 
@@ -412,7 +430,7 @@
     squares = jnp.where(inside, resid * resid, 0.0)
     after = later(volts)
     wind = [mobile[i] * wind_factor * (cond[i] * (volts[i] - after[i])) for i in range(2)]
-    return turned(volts[0]), wind, squares
+    return volts[0], wind, squares
 
 
 def strip_stress(dirs, even_y, even_x, own, gya, gyb, ma, mb, wind):
@@ -432,13 +450,63 @@
     return whole.T.reshape(LAYERS, ROWS, LANES)
 
 
+def inner_residuals(
+    dirs, cond, prior_x, prior_y, via, diag_x, diag_y, pad, load, early, sum_o, ends_o,
+):
+    width = early.shape[2]
+    sum_o[...] = jnp.zeros_like(sum_o)
+    for l in range(LAYERS):
+
+        def add(along_y, prior, diag, l=l):
+            for at in blocks(width, along_y):
+                v = early[(l, *at)]
+                first, second = shifted(v, int(along_y), 0.0, 0.0)
+                resid = (
+                    prior[(l, *at)] * first
+                    + cond[(l, *at)] * second
+                    + rest_of(l, at, early, via, pad, load)
+                    - diag[(l, *at)] * v
+                )
+                row, col = at[0].start + iota(v.shape, 0), at[1].start + iota(v.shape, 1)
+                inside = (col >= REACH) & (col < width - REACH) & (row >= 2) & (row < ROWS - 2)
+                squares = jnp.where(inside, resid * resid, 0.0)
+                total = jnp.zeros((8, LANES), jnp.float32)
+                for r in range(0, v.shape[0], 8):
+                    for c in range(0, v.shape[1], LANES):
+                        total = total + squares[r : r + 8, c : c + LANES]
+                sum_o[...] += total
+                for i, r in enumerate((0, 1, ROWS - 2, ROWS - 1)):
+                    if at[0].start <= r < at[0].stop:
+                        ends_o[i, l : l + 1, at[1]] = resid[r - at[0].start : r - at[0].start + 1]
+
+        here = slice(l, l + 1)
+        if l < LAYERS - 1:
+            ends_o[10, here], ends_o[11, here] = via[l, :1], via[l, ROWS - 1 :]
+        else:
+            ends_o[10, here] = ends_o[11, here] = jnp.zeros((1, width), jnp.float32)
+
+        @pl.when(dirs[l] == 0)
+        def _(l=l, add=add, here=here):
+            add(False, prior_x, diag_x)
+            ends_o[4, here], ends_o[5, here] = diag_x[l, :1], diag_x[l, ROWS - 1 :]
+            ends_o[6, here], ends_o[7, here] = prior_x[l, :1], cond[l, ROWS - 1 :]
+            ends_o[8, here], ends_o[9, here] = cond[l, :1], cond[l, ROWS - 2 : ROWS - 1]
+
+        @pl.when(dirs[l] == 1)
+        def _(l=l, add=add, here=here):
+            add(True, prior_y, diag_y)
+            ends_o[4, here], ends_o[5, here] = diag_y[l, :1], diag_y[l, ROWS - 1 :]
+            for i in range(6, 10):
+                ends_o[i, here] = jnp.zeros((1, width), jnp.float32)
+
+
 def last_sweep(
-    dirs, cond, prior, via, diag, pad, load, early, edges, gxa, gxb, own, gya, gyb, ma, mb,
-    volts_o, sum_o, sides_o, wind_o, sums, near_left, near_right,
+    dirs, inner, ends, edges, gxa, gxb, own, gya, gyb, ma, mb,
+    sum_o, sides_o, strip_o, near_left, near_right, second, third,
 ):
     gx, gy = position()
     even = gx % 2 == 0
-    width = early.shape[2]
+    width = ends.shape[2]
     slot = slots_of(dirs)
 
     def near(right, row):
@@ -451,69 +519,60 @@
         a, b = ma[start : start + ROWS], mb[start : start + ROWS]
         near_right[:, lanes] = jnp.where(even, a, b)
         near_left[:, lanes] = jnp.where(even, b, a)
-    sums[...] = jnp.zeros_like(sums)
-
+    second[...] = jnp.zeros_like(second)
+    third[...] = jnp.zeros_like(third)
     for l in range(LAYERS):
 
         @pl.when(dirs[l] == 0)
         def _(l=l):
-            v = early[l]
-            row = iota(v.shape, 0)
             base, low = slot[l] * EDGE, slot[l] * 4
-            v2_left, v2_right = near_left[pl.ds(low, 1), :], near_right[pl.ds(low, 1), :]
-            extra = jnp.where(row == 0, prior[l] * v2_left, jnp.where(row == ROWS - 1, cond[l] * v2_right, 0.0))
-            volts_o[l] = v + damping * extra / guarded(diag[l])
-            last = cond[l, ROWS - 1 :, :]
-            sides_o[0, pl.ds(low, 1), :] = (1.0 - damping) * v2_left + damping * (
-                near_left[pl.ds(low + 1, 1), :] + near(False, base + 2) * edges[0, l : l + 1, :]
-            ) / guarded(near(False, base + 11))
-            sides_o[1, pl.ds(low, 1), :] = (1.0 - damping) * v2_right + damping * (
-                near_right[pl.ds(low + 1, 1), :] + last * edges[1, l : l + 1, :]
-            ) / guarded(near(True, base + 11) + last)
             for side, ref in enumerate((near_left, near_right)):
-                sides_o[side, pl.ds(low + 1, 1), :] = ref[pl.ds(low + 2, 1), :]
-                sides_o[side, pl.ds(low + 2, 1), :] = ref[pl.ds(low + 3, 1), :]
-
-        @pl.when(dirs[l] == 1)
-        def _(l=l):
-            volts_o[l] = early[l]
-
-    for l in range(LAYERS):
-
-        def add(at, before, after, dim, l=l):
-            v = volts_o[(l, *at)]
-            first, second = shifted(v, dim, before, after)
-            resid = (
-                prior[(l, *at)] * first
-                + cond[(l, *at)] * second
-                + rest_of(l, at, volts_o, via, pad, load)
-                - diag[(l, *at)] * v
-            )
-            col = at[1].start + iota(v.shape, 1)
-            squares = jnp.where((col >= REACH) & (col < width - REACH), resid * resid, 0.0)
-            total = jnp.zeros((8, LANES), jnp.float32)
-            for r in range(0, v.shape[0], 8):
-                for c in range(0, v.shape[1], LANES):
-                    total = total + squares[r : r + 8, c : c + LANES]
-            sums[...] += total
+                here = slice(l, l + 1)
+                v2 = ref[pl.ds(low, 1), :]
+                cond = ends[6 + side, here]
+                diag = near(bool(side), base + 11)
+                if side:
+                    diag = diag + cond
+                v3 = (1.0 - damping) * v2 + damping * (
+                    ref[pl.ds(low + 1, 1), :] + cond * edges[side, here]
+                ) / guarded(diag)
+                second[side, here] = v2
+                third[side, here] = v3
+                sides_o[pl.ds(low + ROWS * side, 1), :] = v3
+                sides_o[pl.ds(low + ROWS * side + 1, 1), :] = ref[pl.ds(low + 2, 1), :]
+                sides_o[pl.ds(low + ROWS * side + 2, 1), :] = ref[pl.ds(low + 3, 1), :]
+
+    total = inner[...]
+    col = iota((LAYERS, width), 1)
+    inside = (col >= REACH) & (col < width - REACH)
+    for side in range(2):
+        diag, cond, via = ends[4 + side], ends[6 + side], ends[10 + side]
+        change = damping * cond * second[side] / guarded(diag)
+        second[side] = change
+        outer = (
+            ends[3 * side]
+            - diag * change
+            + cond * third[side]
+            + pltpu.roll(via, 1, 0) * pltpu.roll(change, 1, 0)
+            + via * pltpu.roll(change, LAYERS - 1, 0)
+        )
+        next_in = ends[1 + side] + ends[8 + side] * change
+        squares = jnp.where(inside, outer * outer + next_in * next_in, 0.0)
+        for c in range(0, width, LANES):
+            total = total + squares[:, c : c + LANES]
+    for l in range(LAYERS):
 
         @pl.when(dirs[l] == 0)
         def _(l=l):
-            for at in blocks(width, False):
-                low = pl.ds(slot[l] * 4, 1)
-                add(at, sides_o[0, low, at[1]], sides_o[1, low, at[1]], 0)
-
-        @pl.when(dirs[l] == 1)
-        def _(l=l):
-            for at in blocks(width, True):
-                add(at, None, None, 1)
+            for side in range(2):
+                sides_o[pl.ds(slot[l] * 4 + ROWS * side + 3, 1), :] = second[side, l : l + 1]
 
     strip_v, wind, squares = strips(dirs, gy % 2 == 0, even, own, gya, gyb, ma, mb)
-    for i in range(2):
-        wind_o[i] = wind[i]
-    place(volts_o, strip_v)
-    total = jnp.sum(sums[...]) + jnp.sum(squares)
-    sum_o[...] = jnp.full(sum_o.shape, total, jnp.float32)
+    for i, value in enumerate([strip_v] + wind):
+        strip_o[2 * STRIP * i : 2 * STRIP * (i + 1)] = value
+    for r in range(0, 2 * STRIP, 8):
+        total = total + squares[r : r + 8]
+    sum_o[...] = jnp.full(sum_o.shape, jnp.sum(total), jnp.float32)
 
 
 def place(ref, strip):
@@ -524,12 +583,12 @@
 
 
 def stress_steps(
-    total_x, total_y, dirs, cond, volts, sides, stress, mob, blk, gxa, gxb, own, gya, gyb, ma, mb, wind_strip,
-    stress_o, ext_c, ext_m, ext_v, ext_s,
+    total_x, total_y, dirs, cond, early, sides, stress, mob, blk, gxa, gxb, own, gya, gyb, ma, mb, strip,
+    volts_o, stress_o, ext_c, ext_m, ext_v, ext_s,
 ):
     gx, gy = position()
     even = gx % 2 == 0
-    width = volts.shape[2]
+    width = early.shape[2]
     slot = slots_of(dirs)
 
     def near(right, row):
@@ -546,12 +605,15 @@
         def _(l=l):
             base, low = slot[l] * EDGE, slot[l] * 4
             for i in range(3):
-                ext_v[7 - i : 8 - i] = sides[0, pl.ds(low + i, 1), :]
-                ext_v[24 + i : 25 + i] = sides[1, pl.ds(low + i, 1), :]
+                ext_v[7 - i : 8 - i] = sides[pl.ds(low + i, 1), :]
+                ext_v[24 + i : 25 + i] = sides[pl.ds(low + ROWS + i, 1), :]
                 for ref, first in ((ext_c, 0), (ext_m, 3), (ext_s, 6)):
                     ref[5 + i : 6 + i] = near(False, base + first + i)
                     ref[24 + i : 25 + i] = near(True, base + first + i)
-            ext_v[8:24] = volts[l]
+            ext_v[8:24] = early[l]
+            ext_v[8:9] = early[l, :1] + sides[pl.ds(low + 3, 1), :]
+            ext_v[23:24] = early[l, ROWS - 1 :] + sides[pl.ds(low + ROWS + 3, 1), :]
+            volts_o[l] = ext_v[8:24]
             ext_c[8:24] = cond[l]
             ext_m[8:24] = mob[l] * (1.0 - blk[l].astype(jnp.float32)) * inner_x(gx, total_x, (ROWS, width))
             ext_s[8:24] = stress[l]
@@ -569,7 +631,8 @@
         @pl.when(dirs[l] == 1)
         def _(l=l):
             for at in blocks(width, True):
-                v, s = volts[(l, *at)], stress[(l, *at)]
+                v, s = early[(l, *at)], stress[(l, *at)]
+                volts_o[(l, *at)] = v
                 inner = inner_y(gy, total_y, (8, width))
                 m = mob[(l, *at)] * (1.0 - blk[(l, *at)].astype(jnp.float32)) * inner
                 wind = m * wind_factor * (cond[(l, *at)] * (v - pltpu.roll(v, width - 1, 1)))
@@ -578,11 +641,12 @@
                     s = s + flux - pltpu.roll(flux, 1, 1)
                 stress_o[(l, *at)] = s
 
-    wind = [wind_strip[0], wind_strip[1]]
+    strip_v, *wind = (strip[2 * STRIP * i : 2 * STRIP * (i + 1)] for i in range(3))
+    place(volts_o, turned(strip_v))
     place(stress_o, strip_stress(dirs, gy % 2 == 0, even, own, gya, gyb, ma, mb, wind))
 
 
-def call(kernel, ins, outs, scratch=(), scalars=1, copies=0, cost=0, aliases={}):
+def call(kernel, ins, outs, scratch=(), scalars=1, copies=0, cost=0):
     smem, vmem = pl.BlockSpec(memory_space=pltpu.SMEM), pl.BlockSpec(memory_space=pltpu.VMEM)
     held = pl.BlockSpec(memory_space=pltpu.HBM) if copies else vmem
     scratch = [pltpu.VMEM(*(s if isinstance(s[0], tuple) else (s, jnp.float32))) for s in scratch]
@@ -591,7 +655,6 @@
         out_shape=[jax.ShapeDtypeStruct(s, jnp.float32) for s in outs],
         in_specs=[smem] * scalars + [held] * (len(ins) - scalars),
         out_specs=[vmem] * len(outs),
-        input_output_aliases=aliases,
         scratch_shapes=scratch + ([pltpu.SemaphoreType.DMA((copies,))] if copies else []),
         compiler_params=pltpu.CompilerParams(vmem_limit_bytes=(57 if copies else 16) * 2**20),
         cost_estimate=pl.CostEstimate(flops=cost, bytes_accessed=cost, transcendentals=0),
@@ -651,31 +714,36 @@
     side = (FIELDS * STRIP, LANES)
     sa, sb = call(pack_strips, (own, gyb, gya), [side, side], scalars=0, cost=COST_STRIPS)
     message = (FIELDS * STRIP + ROWS * (width // LANES), LANES)
-    cond, prior, via, diag, rate = call(
+    cond, prior_y, via, diag_y, rate, first = call(
         functools.partial(conductances, total_x, total_y),
-        (layer_dirs, sent_a, sent_b, *fields[1:5]),
-        [shape, shape, (layers - 1, rows, width), shape, shape],
+        (layer_dirs, sent_a, sent_b, *fields[:6]),
+        [shape, shape, (layers - 1, rows, width), shape, shape, shape],
         cost=COST_SETUP,
     )
-    prior, diag, _, early, edges, ma, mb = call(
+    prior_x, diag_x, early, edges, ma, mb = call(
         early_sweeps,
-        (layer_dirs, cond, prior, via, diag, rate, fields[0], *fields[4:6], gxa, gxb, sa, sb),
-        [shape, shape, shape, shape, (2, layers, width), message, message],
-        scratch=[shape, shape, (2, SLOTS, width), (ROWS, width), (ROWS, width)],
+        (layer_dirs, cond, prior_y, via, diag_y, rate, first, fields[0], *fields[4:6], gxa, gxb, sa, sb),
+        [shape, shape, shape, (2, layers, width), message, message],
+        scratch=[shape, shape, shape, (2, SLOTS, width), (ROWS, width), (ROWS, width)],
         cost=COST_EARLY,
-        aliases={2: 0, 4: 1, 5: 2},
     )
     ma, mb = swap(ma, X, 0), swap(mb, X, 1)
-    volts, held, sides, wind = call(
+    inner, ends = call(
+        inner_residuals,
+        (layer_dirs, cond, prior_x, prior_y, via, diag_x, diag_y, *fields[4:6], early),
+        [(8, LANES), (12, layers, width)],
+        cost=COST_SETUP,
+    )
+    held, sides, strip = call(
         last_sweep,
-        (layer_dirs, cond, prior, via, diag, *fields[4:6], early, edges, gxa, gxb, own, gya, gyb, ma, mb),
-        [shape, (lax.axis_size(NEAR), 1, LANES), (2, ROWS, width), (2, 2 * STRIP, LANES)],
-        scratch=[(8, LANES), (ROWS, width), (ROWS, width)],
-    )
-    (stress,) = call(
+        (layer_dirs, inner, ends, edges, gxa, gxb, own, gya, gyb, ma, mb),
+        [(lax.axis_size(NEAR), 1, LANES), (2 * ROWS, width), (6 * STRIP, LANES)],
+        scratch=[(ROWS, width), (ROWS, width), (2, layers, width), (2, layers, width)],
+    )
+    volts, stress = call(
         functools.partial(stress_steps, total_x, total_y),
-        (layer_dirs, cond, volts, sides, *fields[6:], gxa, gxb, own, gya, gyb, ma, mb, wind),
-        [shape],
+        (layer_dirs, cond, early, sides, *fields[6:], gxa, gxb, own, gya, gyb, ma, mb, strip),
+        [shape, shape],
         scratch=[(32, width)] * 4,
         cost=12 * 2**20,
     )

time: 86.7 us -> 85.2 us (0.983)
  waiting for transfers between devices: 9.96 us -> 6.59 us
  local copies, waits for them, and re-layouts: 1.09 us -> 2.96 us
    ppermute x6, waiting for transfers between devices: 4.33 us -> 2.38 us  [swap(): return lax.ppermute(value, axes, pairs + [(b, a) for a, b in pairs])]
    unnamed x24 -> x32, local copies, waits for them, and re-layouts: 1.09 us -> 2.96 us
    all_to_all x1, waiting for transfers between devices: 5.63 us -> 4.21 us  [rms_all(): got = lax.all_to_all(held, FAR, 0, 0)]
    pallas_call x9 -> x10, Pallas kernels: 17.3 us -> 17.2 us  [call(): pl.pallas_call(kernel, out_shape=[jax.ShapeDtypeStruct(s, jnp.float32) fo...]
  transfers between devices with their start and end apart: 7 -> 7, of which waited for: 3 -> 3; matrix products, arithmetic and copies ran while one was open for 0% -> 0% of each run, Pallas kernels for 8% -> 11%
where the time goes in v5:
time: 85.2 us; the launch traced here: 84.7 us
  starting transfers between devices  34.6 us (41%)
  blocking collectives  22.3 us (26%)
  Pallas kernels  17.2 us (20%)
  waiting for transfers between devices  6.59 us (8%)
  local copies, waits for them, and re-layouts  2.96 us (3%)
  between operations  0.96 us (1%)
    ppermute x6, starting transfers between devices, swap(): return lax.ppermute(value, axes, pairs + [(b, a) for a, b in pairs])  29.2 us
    all_to_all x1, blocking collectives, rms_all(): got = lax.all_to_all(held, NEAR, 0, 0)  22.3 us
    pallas_call x10, Pallas kernels, call(): pl.pallas_call(kernel, out_shape=[jax.ShapeDtypeStruct(s, jnp.float32) fo...  17.2 us
    all_to_all x1, starting transfers between devices, rms_all(): got = lax.all_to_all(held, FAR, 0, 0)  5.45 us
    all_to_all x1, waiting for transfers between devices, rms_all(): got = lax.all_to_all(held, FAR, 0, 0)  4.21 us
    unnamed x32, local copies, waits for them, and re-layouts  2.96 us
    ppermute x6, waiting for transfers between devices, swap(): return lax.ppermute(value, axes, pairs + [(b, a) for a, b in pairs])  2.38 us
  transfers between devices with their start and end apart: 7, of which 3 were waited for; matrix products, arithmetic and copies ran while one was open for 0% of the time, Pallas kernels for 11%

profile of v5, /device:TPU:1, one launch (start us, length us, event | category | flops | bytes accessed | tf_op | source)
XLA Modules:
  0.0 84.7 jit_solution(17307051228665825243)
XLA Ops:
  0.6 0.0 copy-start.4
  0.6 0.0 copy-start.3
  0.7 0.0 copy-start.2
  0.7 0.0 copy-start.8
  0.7 0.0 copy-start.7
  0.7 0.0 copy-start.6
  0.7 0.0 copy-start.5
  0.7 0.0 copy-start.1
  0.7 0.0 copy-start
  0.7 3.3 %shard_map.121 = (f32[2,6,16,128]{3,2,1,0:T(8,128)}, f32[6,8,128]{2,1,0:T(8,128)}, f32[6,8,128]{2,1,0:T(8,128)}) custom-call(s32[8]{0:T(128)} %dirs.13, f32[8,16,1024]{2,1,0:T(8,128)} %volts.2, f32[8,16,1024]{2,1,0:T(8,128)} %seg.1, f32[7,16,1024]{2,1,0:T(8,128)} %via_cond.1, s32[7,16,1024]{2,1,0:T(8,128)} %via_mask.1, s32[16,1024]{1,0:T(8,128)} %pad.3, ...), custom_call_target="tpu_custom_call" | custom-call | tf_op jit(solution)/shard_map/pallas_call | solution.py:653
  4.1 16.8 %collective-permute-start.2 = (f32[6,8,128]{2,1,0:T(8,128)}, f32[6,8,128]{2,1,0:T(8,128)S(1)}, u32[]{:S(2)}, u32[]{:S(2)}) collective-permute-start(f32[6,8,128]{2,1,0:T(8,128)} %get-tuple-element.58), channel_id=1, source_target_pairs={{1,2},{3,4},{5,6},{7,8},{9,10},{11,12},{13,14},{2,1},{4,3},{6,5},{... | collective-permute-start | bytes 73736 | tf_op jit(solution)/shard_map/ppermute | solution.py:667
  20.9 0.0 copy-start.14
  20.9 1.9 %collective-permute-start.3 = (f32[6,8,128]{2,1,0:T(8,128)}, f32[6,8,128]{2,1,0:T(8,128)S(1)}, u32[]{:S(2)}, u32[]{:S(2)}) collective-permute-start(f32[6,8,128]{2,1,0:T(8,128)} %get-tuple-element.59), channel_id=1, source_target_pairs={{0,1},{2,3},{4,5},{6,7},{8,9},{10,11},{12,13},{14,15},{1,0},{3,2},... | collective-permute-start | bytes 73736 | tf_op jit(solution)/shard_map/ppermute | solution.py:667
  22.8 0.0 copy-done.4
  22.9 0.0 copy-done.3
  22.9 0.0 copy-done.2
  22.9 0.0 copy-done.8
  22.9 0.0 copy-done.7
  22.9 0.0 copy-done.6
  22.9 0.0 copy-done.5
  22.9 0.0 copy-done.1
  22.9 0.0 copy-done
  22.9 0.0 copy-done.14
  22.9 1.0 %shard_map.122 = (f32[48,1024]{1,0:T(8,128)S(1)}, f32[48,1024]{1,0:T(8,128)S(1)}) custom-call(s32[8]{0:T(128)S(1)} %copy-done.14, f32[8,16,1024]{2,1,0:T(8,128)S(1)} %copy-done, f32[8,16,1024]{2,1,0:T(8,128)S(1)} %copy-done.1, f32[7,16,1024]{2,1,0:T(8,128)S(1)} %copy-done.5, s32[7,16,1024]{2,1,0:T(8,128)S(1)} %copy-done.6, s32[16,1024]{1,0:T(8,128)S(1)} %copy-done.7, ...), custom_call_target="tpu_custom_call" | custom-call | flops 1048576 | bytes 1048576 | tf_op jit(solution)/shard_map/pallas_call | solution.py:653
  23.9 3.1 %collective-permute-start = (f32[48,1024]{1,0:T(8,128)S(1)}, f32[48,1024]{1,0:T(8,128)S(1)}, u32[]{:S(2)}, u32[]{:S(2)}) collective-permute-start(f32[48,1024]{1,0:T(8,128)S(1)} %get-tuple-element.49.after_a), channel_id=1, source_target_pairs={{0,16},{32,48},{64,80},{96,112},{128,144},{160,176},{192,208},{224... | collective-permute-start | bytes 589832 | tf_op jit(solution)/shard_map/ppermute | solution.py:667
  27.1 0.0 copy-start.9
  27.1 0.8 collective-permute-start.1
  27.9 1.8 %shard_map.123 = (f32[8,16,1024]{2,1,0:T(8,128)S(1)}, f32[8,16,1024]{2,1,0:T(8,128)S(1)}, f32[7,16,1024]{2,1,0:T(8,128)S(1)}, f32[8,16,1024]{2,1,0:T(8,128)S(1)}...) custom-call(s32[8]{0:T(128)S(1)} %copy-done.14, f32[48,1024]{1,0:T(8,128)S(1)} %get-tuple-element.49.after_a, ...), custom_call_target="tpu_custom_call" | custom-call | flops 4194304 | bytes 4194304 | tf_op jit(solution)/shard_map/pallas_call | solution.py:653
  29.7 0.0 collective-permute-done.2.gyb
  29.7 0.0 collective-permute-done.3.gya
  29.8 0.0 copy-done.9
  29.8 0.0 copy-start.10
  29.8 0.1 shard_map.124
  29.9 1.9 %collective-permute-done.gxa = f32[48,1024]{1,0:T(8,128)S(1)} collective-permute-done((f32[48,1024]{1,0:T(8,128)S(1)}, f32[48,1024]{1,0:T(8,128)S(1)}, u32[]{:S(2)}, u32[]{:S(2)}) %collective-permute-start) | collective-permute-done | bytes 196640 | tf_op jit(solution)/shard_map/ppermute | solution.py:667
  31.8 0.0 collective-permute-done.1.gxb
  31.8 2.2 %shard_map.125 = (f32[8,16,1024]{2,1,0:T(8,128)S(1)}, f32[8,16,1024]{2,1,0:T(8,128)S(1)}, f32[8,16,1024]{2,1,0:T(8,128)S(1)}, f32[2,8,1024]{2,1,0:T(8,128)S(1)},...) custom-call(s32[8]{0:T(128)S(1)} %copy-done.14, f32[8,16,1024]{2,1,0:T(8,128)S(1)} %get-tuple-element.51.cond_o.cond, ...), custom_call_target="tpu_custom_call" | custom-call | flops 1024 | bytes 1024 | tf_op jit(solution)/shard_map/pallas_call | solution.py:653
  34.0 5.8 %collective-permute-start.4 = (f32[272,128]{1,0:T(8,128)S(1)}, f32[272,128]{1,0:T(8,128)S(1)}, u32[]{:S(2)}, u32[]{:S(2)}) collective-permute-start(f32[272,128]{1,0:T(8,128)S(1)} %get-tuple-element.68), channel_id=1, source_target_pairs={{0,16},{32,48},{64,80},{96,112},{128,144},{160,176},{192,208},{224... | collective-permute-start | bytes 417800 | tf_op jit(solution)/shard_map/ppermute | solution.py:667
  39.8 0.7 collective-permute-start.5
  40.5 1.3 %shard_map.126 = (f32[8,128]{1,0:T(8,128)S(1)}, f32[12,8,1024]{2,1,0:T(8,128)S(1)}) custom-call(s32[8]{0:T(128)S(1)} %copy-done.14, f32[8,16,1024]{2,1,0:T(8,128)S(1)} %get-tuple-element.51.cond_o.cond, f32[8,16,1024]{2,1,0:T(8,128)S(1)} %get-tuple-element.63.prior_x, f32[8,16,1024]{2,1,0:T(8,128)S(1)} %get-tuple-element.52.prior_i.prior_y, ...), custom_call_target="tpu_custom_call" | custom-call | flops 4194304 | bytes 4194304 | tf_op jit(solution)/shard_map/pallas_call | solution.py:653
  41.8 0.5 collective-permute-done.4.ma
  42.3 0.0 collective-permute-done.5.mb
  42.3 0.0 copy-done.10
  42.3 1.4 %shard_map.127 = (f32[32,1,128]{2,1,0:T(1,128)S(1)}, f32[32,1024]{1,0:T(8,128)S(1)}, f32[144,128]{1,0:T(8,128)S(1)}) custom-call(s32[8]{0:T(128)S(1)} %copy-done.14, f32[8,128]{1,0:T(8,128)S(1)} %get-tuple-element.65.inner, f32[12,8,1024]{2,1,0:T(8,128)S(1)} %get-tuple-element.66.ends, f32[2,8,1024]{2,1,0:T(8,128)S(1)} %get-tuple-element.67.edges, ...), custom_call_target="tpu_custom_call" | custom-call | tf_op jit(solution)/shard_map/pallas_call | solution.py:653
  43.7 0.0 copy-start.12
  43.7 0.6 copy-done.12
  44.3 22.3 %all_to_all.10.held = f32[32,1,128]{2,1,0:T(1,128)S(1)} all-to-all(f32[32,1,128]{2,1,0:T(1,128)S(1)} %get-tuple-element.74), channel_id=1, replica_groups=mesh['z_lo'=8,'x'=4,'y'=4,'z_hi'=2,'core'=2] {'x','y','core'}, dimensions={0} | all-to-all | bytes 32768 | tf_op jit(solution)/shard_map/all_to_all | solution.py:684
  66.6 0.6 shard_map.129
  67.3 5.4 %all-to-all-start.1 = ((f32[16,1,128]{2,1,0:T(1,128)}), f32[16,1,128]{2,1,0:T(1,128)S(1)}, u32[]{:S(2)}, u32[]{:S(2)}) async-start(f32[16,1,128]{2,1,0:T(1,128)} %shard_map.129), calls=%async_computation.1 | async-start | bytes 16384 | tf_op jit(solution)/shard_map/all_to_all | solution.py:686
  72.7 0.0 copy-start.15
  72.7 0.6 copy-done.15
  73.4 0.0 copy-start.11
  73.4 0.7 copy-done.11
  74.1 0.0 copy-start.13
  74.1 0.9 %copy-done.13 = f32[144,128]{1,0:T(8,128)S(1)} copy-done((f32[144,128]{1,0:T(8,128)S(1)}, f32[144,128]{1,0:T(8,128)}, u32[]{:S(2)}) %copy-start.13) | copy-done | bytes 73752
  75.0 4.8 %shard_map.128 = (f32[8,16,1024]{2,1,0:T(8,128)}, f32[8,16,1024]{2,1,0:T(8,128)}) custom-call(s32[8]{0:T(128)S(1)} %copy-done.15, f32[8,16,1024]{2,1,0:T(8,128)S(1)} %get-tuple-element.51.cond_o.cond, f32[8,16,1024]{2,1,0:T(8,128)S(1)} %get-tuple-element.62.early, f32[32,1024]{1,0:T(8,128)S(1)} %get-tuple-element.70.sides, f32[8,16,1024]{2,1,0:T(8,128)S(1)} %copy-done.2, ...), custom_call_target="tpu_custom_call" | custom-call | flops 12582912 | bytes 12582912 | tf_op jit(solution)/shard_map/pallas_call | solution.py:653
  79.8 4.2 %all-to-all-done.1.held = f32[16,1,128]{2,1,0:T(1,128)S(1)} async-done(((f32[16,1,128]{2,1,0:T(1,128)}), f32[16,1,128]{2,1,0:T(1,128)S(1)}, u32[]{:S(2)}, u32[]{:S(2)}) %all-to-all-start.1) | async-done | bytes 8224 | tf_op jit(solution)/shard_map/all_to_all | solution.py:686
  84.0 0.7 shard_map.130
Async XLA Ops:
  0.6 22.2 %copy-start.4 = (s32[8,16,1024]{2,1,0:T(8,128)S(1)}, s32[8,16,1024]{2,1,0:T(8,128)}, u32[]{:S(2)}) copy-start(s32[8,16,1024]{2,1,0:T(8,128)} %blk.1) | copy-start | bytes 1572868
  0.6 22.2 %copy-start.3 = (f32[8,16,1024]{2,1,0:T(8,128)S(1)}, f32[8,16,1024]{2,1,0:T(8,128)}, u32[]{:S(2)}) copy-start(f32[8,16,1024]{2,1,0:T(8,128)} %mob.1) | copy-start | bytes 1572868
  0.7 22.2 %copy-start.2 = (f32[8,16,1024]{2,1,0:T(8,128)S(1)}, f32[8,16,1024]{2,1,0:T(8,128)}, u32[]{:S(2)}) copy-start(f32[8,16,1024]{2,1,0:T(8,128)} %stress.1) | copy-start | bytes 1572868
  0.7 22.2 %copy-start.8 = (f32[16,1024]{1,0:T(8,128)S(1)}, f32[16,1024]{1,0:T(8,128)}, u32[]{:S(2)}) copy-start(f32[16,1024]{1,0:T(8,128)} %load.3) | copy-start | bytes 196612
  0.7 22.2 %copy-start.7 = (s32[16,1024]{1,0:T(8,128)S(1)}, s32[16,1024]{1,0:T(8,128)}, u32[]{:S(2)}) copy-start(s32[16,1024]{1,0:T(8,128)} %pad.3) | copy-start | bytes 196612
  0.7 22.2 %copy-start.6 = (s32[7,16,1024]{2,1,0:T(8,128)S(1)}, s32[7,16,1024]{2,1,0:T(8,128)}, u32[]{:S(2)}) copy-start(s32[7,16,1024]{2,1,0:T(8,128)} %via_mask.1) | copy-start | bytes 1376260
  0.7 22.2 %copy-start.5 = (f32[7,16,1024]{2,1,0:T(8,128)S(1)}, f32[7,16,1024]{2,1,0:T(8,128)}, u32[]{:S(2)}) copy-start(f32[7,16,1024]{2,1,0:T(8,128)} %via_cond.1) | copy-start | bytes 1376260
  0.7 22.2 %copy-start.1 = (f32[8,16,1024]{2,1,0:T(8,128)S(1)}, f32[8,16,1024]{2,1,0:T(8,128)}, u32[]{:S(2)}) copy-start(f32[8,16,1024]{2,1,0:T(8,128)} %seg.1) | copy-start | bytes 1572868
  0.7 22.2 %copy-start = (f32[8,16,1024]{2,1,0:T(8,128)S(1)}, f32[8,16,1024]{2,1,0:T(8,128)}, u32[]{:S(2)}) copy-start(f32[8,16,1024]{2,1,0:T(8,128)} %volts.2) | copy-start | bytes 1572868
  4.1 25.7 %collective-permute-start.2 = (f32[6,8,128]{2,1,0:T(8,128)}, f32[6,8,128]{2,1,0:T(8,128)S(1)}, u32[]{:S(2)}, u32[]{:S(2)}) collective-permute-start(f32[6,8,128]{2,1,0:T(8,128)} %get-tuple-element.58), channel_id=1, source_target_pairs={{1,2},{3,4},{5,6},{7,8},{9,10},{11,12},{13,14},{2,1},{4,3},{6,5},{... | collective-permute-start | bytes 73736 | tf_op jit(solution)/shard_map/ppermute | solution.py:667
  20.9 2.0 %copy-start.14 = (s32[8]{0:T(128)S(1)}, s32[8]{0:T(128)}, u32[]{:S(2)}) copy-start(s32[8]{0:T(128)} %dirs.13) | copy-start | bytes 100
  20.9 8.8 %collective-permute-start.3 = (f32[6,8,128]{2,1,0:T(8,128)}, f32[6,8,128]{2,1,0:T(8,128)S(1)}, u32[]{:S(2)}, u32[]{:S(2)}) collective-permute-start(f32[6,8,128]{2,1,0:T(8,128)} %get-tuple-element.59), channel_id=1, source_target_pairs={{0,1},{2,3},{4,5},{6,7},{8,9},{10,11},{12,13},{14,15},{1,0},{3,2},... | collective-permute-start | bytes 73736 | tf_op jit(solution)/shard_map/ppermute | solution.py:667
  23.9 7.9 %collective-permute-start = (f32[48,1024]{1,0:T(8,128)S(1)}, f32[48,1024]{1,0:T(8,128)S(1)}, u32[]{:S(2)}, u32[]{:S(2)}) collective-permute-start(f32[48,1024]{1,0:T(8,128)S(1)} %get-tuple-element.49.after_a), channel_id=1, source_target_pairs={{0,16},{32,48},{64,80},{96,112},{128,144},{160,176},{192,208},{224... | collective-permute-start | bytes 589832 | tf_op jit(solution)/shard_map/ppermute | solution.py:667
  27.1 2.7 %copy-start.9 = (f32[2,6,16,128]{3,2,1,0:T(8,128)S(1)}, f32[2,6,16,128]{3,2,1,0:T(8,128)}, u32[]{:S(2)}) copy-start(f32[2,6,16,128]{3,2,1,0:T(8,128)} %get-tuple-element.57.own) | copy-start | bytes 294916
  27.1 4.7 %collective-permute-start.1 = (f32[48,1024]{1,0:T(8,128)S(1)}, f32[48,1024]{1,0:T(8,128)S(1)}, u32[]{:S(2)}, u32[]{:S(2)}) collective-permute-start(f32[48,1024]{1,0:T(8,128)S(1)} %get-tuple-element.50.after_b), channel_id=1, source_target_pairs={{16,32},{48,64},{80,96},{112,128},{144,160},{176,192},{208,224},{2... | collective-permute-start | bytes 589832 | tf_op jit(solution)/shard_map/ppermute | solution.py:667
  29.8 12.5 %copy-start.10 = (f32[6,8,128]{2,1,0:T(8,128)}, f32[6,8,128]{2,1,0:T(8,128)S(1)}, u32[]{:S(2)}) copy-start(f32[6,8,128]{2,1,0:T(8,128)S(1)} %collective-permute-done.3.gya) | copy-start | bytes 73732
  34.0 8.3 %collective-permute-start.4 = (f32[272,128]{1,0:T(8,128)S(1)}, f32[272,128]{1,0:T(8,128)S(1)}, u32[]{:S(2)}, u32[]{:S(2)}) collective-permute-start(f32[272,128]{1,0:T(8,128)S(1)} %get-tuple-element.68), channel_id=1, source_target_pairs={{0,16},{32,48},{64,80},{96,112},{128,144},{160,176},{192,208},{224... | collective-permute-start | bytes 417800 | tf_op jit(solution)/shard_map/ppermute | solution.py:667
  39.8 2.4 %collective-permute-start.5 = (f32[272,128]{1,0:T(8,128)S(1)}, f32[272,128]{1,0:T(8,128)S(1)}, u32[]{:S(2)}, u32[]{:S(2)}) collective-permute-start(f32[272,128]{1,0:T(8,128)S(1)} %get-tuple-element.69), channel_id=1, source_target_pairs={{16,32},{48,64},{80,96},{112,128},{144,160},{176,192},{208,224},{2... | collective-permute-start | bytes 417800 | tf_op jit(solution)/shard_map/ppermute | solution.py:667
  43.7 0.6 copy-start.12
  67.3 16.8 %all-to-all-start.1 = ((f32[16,1,128]{2,1,0:T(1,128)}), f32[16,1,128]{2,1,0:T(1,128)S(1)}, u32[]{:S(2)}, u32[]{:S(2)}) async-start(f32[16,1,128]{2,1,0:T(1,128)} %shard_map.129), calls=%async_computation.1 | async-start | bytes 16384 | tf_op jit(solution)/shard_map/all_to_all | solution.py:686
  72.7 0.7 copy-start.15
  73.4 0.7 copy-start.11
  74.1 0.9 %copy-start.13 = (f32[144,128]{1,0:T(8,128)S(1)}, f32[144,128]{1,0:T(8,128)}, u32[]{:S(2)}) copy-start(f32[144,128]{1,0:T(8,128)} %copy-done.12) | copy-start | bytes 221188

commit v6 on v5

--- a/solution.py
+++ b/solution.py
@@ -340,13 +340,23 @@
                     if sweep == 2:
                         edges_o[:, l : l + 1, :] = jnp.zeros((2, 1, width), jnp.float32)
 
-    a_ref[: FIELDS * STRIP] = strips_a[...]
-    b_ref[: FIELDS * STRIP] = strips_b[...]
+    a_ref[: SENT] = strips_a[...]
+    b_ref[: SENT] = strips_b[...]
     for j in range(width // LANES):
-        start = FIELDS * STRIP + j * ROWS
+        start = SENT + j * ROWS
         lanes = slice(j * LANES, (j + 1) * LANES)
         a_ref[start : start + ROWS] = jnp.where(even, to_right[:, lanes], to_left[:, lanes])
         b_ref[start : start + ROWS] = jnp.where(even, to_left[:, lanes], to_right[:, lanes])
+
+
+def strip_rows(f):
+    if f < 4:
+        return slice(f * STRIP, (f + 1) * STRIP), slice(0, STRIP)
+    start = 4 * STRIP + (f - 4) * REACH
+    return slice(start, start + REACH), slice(REACH, 2 * REACH)
+
+
+SENT = strip_rows(FIELDS - 1)[0].stop
 
 
 def pack_strips(own, gyb, gya, a_ref, b_ref):
@@ -357,14 +367,19 @@
         left, right = strip_pair(gya, gyb, gy % 2 == 0, own, f)
         right_going = jnp.where(x >= 8, left, pltpu.roll(right, LANES - 8, 1))
         left_going = jnp.where(x < 8, left, pltpu.roll(right, 8, 1))
-        a_ref[f * STRIP : (f + 1) * STRIP] = jnp.where(even, right_going, left_going)
-        b_ref[f * STRIP : (f + 1) * STRIP] = jnp.where(even, left_going, right_going)
+        to, rows = strip_rows(f)
+        a_ref[to] = jnp.where(even, right_going, left_going)[rows]
+        b_ref[to] = jnp.where(even, left_going, right_going)[rows]
 
 
 def strip_field(f, even_y, even_x, own, gya, gyb, ma, mb):
     x = iota((STRIP, LANES), 1) % ROWS
     left, right = strip_pair(gya, gyb, even_y, own, f)
-    a, b = ma[f * STRIP : (f + 1) * STRIP], mb[f * STRIP : (f + 1) * STRIP]
+    at, rows = strip_rows(f)
+    a, b = ma[at], mb[at]
+    if rows.start:
+        none = jnp.zeros((REACH, LANES), jnp.float32)
+        a, b = jnp.concatenate([none, a, none], 0), jnp.concatenate([none, b, none], 0)
     from_right, from_left = jnp.where(even_x, a, b), jnp.where(even_x, b, a)
     far_left = jnp.where(x >= 8, from_left, from_right)
     far_right = jnp.where(x >= 8, pltpu.roll(from_left, 8, 1), pltpu.roll(from_right, LANES - 8, 1))
@@ -502,7 +517,7 @@
 
 def last_sweep(
     dirs, inner, ends, edges, gxa, gxb, own, gya, gyb, ma, mb,
-    sum_o, sides_o, strip_o, near_left, near_right, second, third,
+    sum_o, sides_o, near_left, near_right, second, third,
 ):
     gx, gy = position()
     even = gx % 2 == 0
@@ -514,7 +529,7 @@
         return jnp.where(even, a, b) if right else jnp.where(even, b, a)
 
     for j in range(width // LANES):
-        start = FIELDS * STRIP + j * ROWS
+        start = SENT + j * ROWS
         lanes = slice(j * LANES, (j + 1) * LANES)
         a, b = ma[start : start + ROWS], mb[start : start + ROWS]
         near_right[:, lanes] = jnp.where(even, a, b)
@@ -567,9 +582,7 @@
             for side in range(2):
                 sides_o[pl.ds(slot[l] * 4 + ROWS * side + 3, 1), :] = second[side, l : l + 1]
 
-    strip_v, wind, squares = strips(dirs, gy % 2 == 0, even, own, gya, gyb, ma, mb)
-    for i, value in enumerate([strip_v] + wind):
-        strip_o[2 * STRIP * i : 2 * STRIP * (i + 1)] = value
+    _, _, squares = strips(dirs, gy % 2 == 0, even, own, gya, gyb, ma, mb)
     for r in range(0, 2 * STRIP, 8):
         total = total + squares[r : r + 8]
     sum_o[...] = jnp.full(sum_o.shape, jnp.sum(total), jnp.float32)
@@ -583,7 +596,7 @@
 
 
 def stress_steps(
-    total_x, total_y, dirs, cond, early, sides, stress, mob, blk, gxa, gxb, own, gya, gyb, ma, mb, strip,
+    total_x, total_y, dirs, cond, early, sides, stress, mob, blk, gxa, gxb, own, gya, gyb, ma, mb,
     volts_o, stress_o, ext_c, ext_m, ext_v, ext_s,
 ):
     gx, gy = position()
@@ -641,7 +654,7 @@
                     s = s + flux - pltpu.roll(flux, 1, 1)
                 stress_o[(l, *at)] = s
 
-    strip_v, *wind = (strip[2 * STRIP * i : 2 * STRIP * (i + 1)] for i in range(3))
+    strip_v, wind, _ = strips(dirs, gy % 2 == 0, even, own, gya, gyb, ma, mb)
     place(volts_o, turned(strip_v))
     place(stress_o, strip_stress(dirs, gy % 2 == 0, even, own, gya, gyb, ma, mb, wind))
 
@@ -711,9 +724,9 @@
     )
     sent_a, sent_b = gxa, gxb
     gxa, gxb = swap(gxa, X, 0), swap(gxb, X, 1)
-    side = (FIELDS * STRIP, LANES)
+    side = (SENT, LANES)
     sa, sb = call(pack_strips, (own, gyb, gya), [side, side], scalars=0, cost=COST_STRIPS)
-    message = (FIELDS * STRIP + ROWS * (width // LANES), LANES)
+    message = (SENT + ROWS * (width // LANES), LANES)
     cond, prior_y, via, diag_y, rate, first = call(
         functools.partial(conductances, total_x, total_y),
         (layer_dirs, sent_a, sent_b, *fields[:6]),
@@ -734,15 +747,15 @@
         [(8, LANES), (12, layers, width)],
         cost=COST_SETUP,
     )
-    held, sides, strip = call(
+    held, sides = call(
         last_sweep,
         (layer_dirs, inner, ends, edges, gxa, gxb, own, gya, gyb, ma, mb),
-        [(lax.axis_size(NEAR), 1, LANES), (2 * ROWS, width), (6 * STRIP, LANES)],
+        [(lax.axis_size(NEAR), 1, LANES), (2 * ROWS, width)],
         scratch=[(ROWS, width), (ROWS, width), (2, layers, width), (2, layers, width)],
     )
     volts, stress = call(
         functools.partial(stress_steps, total_x, total_y),
-        (layer_dirs, cond, early, sides, *fields[6:], gxa, gxb, own, gya, gyb, ma, mb, strip),
+        (layer_dirs, cond, early, sides, *fields[6:], gxa, gxb, own, gya, gyb, ma, mb),
         [shape, shape],
         scratch=[(32, width)] * 4,
         cost=12 * 2**20,

time: 85.2 us -> 84.2 us (0.988)
  local copies, waits for them, and re-layouts: 2.96 us -> 0.05 us
  waiting for transfers between devices: 6.59 us -> 8.22 us
    unnamed x32 -> x22, local copies, waits for them, and re-layouts: 2.96 us -> 0.05 us
    all_to_all x1, waiting for transfers between devices: 4.21 us -> 6.01 us  [rms_all(): got = lax.all_to_all(held, FAR, 0, 0)]
where the time goes in v6:
time: 84.2 us; the launch traced here: 83.8 us
  starting transfers between devices  34.6 us (41%)
  blocking collectives  22.3 us (26%)
  Pallas kernels  17.6 us (21%)
  waiting for transfers between devices  8.22 us (10%)
  between operations  0.94 us (1%)
    ppermute x6, starting transfers between devices, swap(): return lax.ppermute(value, axes, pairs + [(b, a) for a, b in pairs])  29.2 us
    all_to_all x1, blocking collectives, rms_all(): got = lax.all_to_all(held, NEAR, 0, 0)  22.3 us
    pallas_call x10, Pallas kernels, call(): pl.pallas_call(kernel, out_shape=[jax.ShapeDtypeStruct(s, jnp.float32) fo...  17.6 us
    all_to_all x1, waiting for transfers between devices, rms_all(): got = lax.all_to_all(held, FAR, 0, 0)  6.01 us
    all_to_all x1, starting transfers between devices, rms_all(): got = lax.all_to_all(held, FAR, 0, 0)  5.45 us
    ppermute x6, waiting for transfers between devices, swap(): return lax.ppermute(value, axes, pairs + [(b, a) for a, b in pairs])  2.21 us
  transfers between devices with their start and end apart: 7, of which 3 were waited for; matrix products, arithmetic and copies ran while one was open for 0% of the time, Pallas kernels for 11%

profile of v6, /device:TPU:1, one launch (start us, length us, event | category | flops | bytes accessed | tf_op | source)
XLA Modules:
  0.0 83.8 jit_solution(4503326268018644001)
XLA Ops:
  0.6 0.0 copy-start.4
  0.6 0.0 copy-start.3
  0.7 0.0 copy-start.2
  0.7 0.0 copy-start.8
  0.7 0.0 copy-start.7
  0.7 0.0 copy-start.6
  0.7 0.0 copy-start.5
  0.7 0.0 copy-start.1
  0.7 0.0 copy-start
  0.7 3.3 %shard_map.121 = (f32[2,6,16,128]{3,2,1,0:T(8,128)}, f32[6,8,128]{2,1,0:T(8,128)}, f32[6,8,128]{2,1,0:T(8,128)}) custom-call(s32[8]{0:T(128)} %dirs.13, f32[8,16,1024]{2,1,0:T(8,128)} %volts.2, f32[8,16,1024]{2,1,0:T(8,128)} %seg.1, f32[7,16,1024]{2,1,0:T(8,128)} %via_cond.1, s32[7,16,1024]{2,1,0:T(8,128)} %via_mask.1, s32[16,1024]{1,0:T(8,128)} %pad.3, ...), custom_call_target="tpu_custom_call" | custom-call | tf_op jit(solution)/shard_map/pallas_call | solution.py:666
  4.1 16.8 %collective-permute-start.2 = (f32[6,8,128]{2,1,0:T(8,128)}, f32[6,8,128]{2,1,0:T(8,128)S(1)}, u32[]{:S(2)}, u32[]{:S(2)}) collective-permute-start(f32[6,8,128]{2,1,0:T(8,128)} %get-tuple-element.57), channel_id=1, source_target_pairs={{1,2},{3,4},{5,6},{7,8},{9,10},{11,12},{13,14},{2,1},{4,3},{6,5},{... | collective-permute-start | bytes 73736 | tf_op jit(solution)/shard_map/ppermute | solution.py:680
  20.9 0.0 copy-start.10
  20.9 1.9 %collective-permute-start.3 = (f32[6,8,128]{2,1,0:T(8,128)}, f32[6,8,128]{2,1,0:T(8,128)S(1)}, u32[]{:S(2)}, u32[]{:S(2)}) collective-permute-start(f32[6,8,128]{2,1,0:T(8,128)} %get-tuple-element.58), channel_id=1, source_target_pairs={{0,1},{2,3},{4,5},{6,7},{8,9},{10,11},{12,13},{14,15},{1,0},{3,2},... | collective-permute-start | bytes 73736 | tf_op jit(solution)/shard_map/ppermute | solution.py:680
  22.9 0.0 copy-done.4
  22.9 0.0 copy-done.3
  22.9 0.0 copy-done.2
  22.9 0.0 copy-done.8
  22.9 0.0 copy-done.7
  22.9 0.0 copy-done.6
  22.9 0.0 copy-done.5
  22.9 0.0 copy-done.1
  22.9 0.0 copy-done
  22.9 0.0 copy-done.10
  23.0 1.0 %shard_map.122 = (f32[48,1024]{1,0:T(8,128)S(1)}, f32[48,1024]{1,0:T(8,128)S(1)}) custom-call(s32[8]{0:T(128)S(1)} %copy-done.10, f32[8,16,1024]{2,1,0:T(8,128)S(1)} %copy-done, f32[8,16,1024]{2,1,0:T(8,128)S(1)} %copy-done.1, f32[7,16,1024]{2,1,0:T(8,128)S(1)} %copy-done.5, s32[7,16,1024]{2,1,0:T(8,128)S(1)} %copy-done.6, s32[16,1024]{1,0:T(8,128)S(1)} %copy-done.7, ...), custom_call_target="tpu_custom_call" | custom-call | flops 1048576 | bytes 1048576 | tf_op jit(solution)/shard_map/pallas_call | solution.py:666
  24.0 3.1 %collective-permute-start = (f32[48,1024]{1,0:T(8,128)S(1)}, f32[48,1024]{1,0:T(8,128)S(1)}, u32[]{:S(2)}, u32[]{:S(2)}) collective-permute-start(f32[48,1024]{1,0:T(8,128)S(1)} %get-tuple-element.48.after_a), channel_id=1, source_target_pairs={{0,16},{32,48},{64,80},{96,112},{128,144},{160,176},{192,208},{224... | collective-permute-start | bytes 589832 | tf_op jit(solution)/shard_map/ppermute | solution.py:680
  27.1 0.0 copy-start.9
  27.1 0.8 collective-permute-start.1
  27.9 1.8 %shard_map.123 = (f32[8,16,1024]{2,1,0:T(8,128)S(1)}, f32[8,16,1024]{2,1,0:T(8,128)S(1)}, f32[7,16,1024]{2,1,0:T(8,128)S(1)}, f32[8,16,1024]{2,1,0:T(8,128)S(1)}...) custom-call(s32[8]{0:T(128)S(1)} %copy-done.10, f32[48,1024]{1,0:T(8,128)S(1)} %get-tuple-element.48.after_a, ...), custom_call_target="tpu_custom_call" | custom-call | flops 4194304 | bytes 4194304 | tf_op jit(solution)/shard_map/pallas_call | solution.py:666
  29.8 0.0 collective-permute-done.2.gyb
  29.8 0.0 collective-permute-done.3.gya
  29.8 0.0 copy-done.9
  29.8 0.1 shard_map.124
  29.9 1.9 %collective-permute-done.gxa = f32[48,1024]{1,0:T(8,128)S(1)} collective-permute-done((f32[48,1024]{1,0:T(8,128)S(1)}, f32[48,1024]{1,0:T(8,128)S(1)}, u32[]{:S(2)}, u32[]{:S(2)}) %collective-permute-start) | collective-permute-done | bytes 196640 | tf_op jit(solution)/shard_map/ppermute | solution.py:680
  31.8 0.0 collective-permute-done.1.gxb
  31.8 2.2 %shard_map.125 = (f32[8,16,1024]{2,1,0:T(8,128)S(1)}, f32[8,16,1024]{2,1,0:T(8,128)S(1)}, f32[8,16,1024]{2,1,0:T(8,128)S(1)}, f32[2,8,1024]{2,1,0:T(8,128)S(1)},...) custom-call(s32[8]{0:T(128)S(1)} %copy-done.10, f32[8,16,1024]{2,1,0:T(8,128)S(1)} %get-tuple-element.50.cond_o.cond, ...), custom_call_target="tpu_custom_call" | custom-call | flops 1024 | bytes 1024 | tf_op jit(solution)/shard_map/pallas_call | solution.py:666
  34.0 5.8 %collective-permute-start.4 = (f32[240,128]{1,0:T(8,128)S(1)}, f32[240,128]{1,0:T(8,128)S(1)}, u32[]{:S(2)}, u32[]{:S(2)}) collective-permute-start(f32[240,128]{1,0:T(8,128)S(1)} %get-tuple-element.67), channel_id=1, source_target_pairs={{0,16},{32,48},{64,80},{96,112},{128,144},{160,176},{192,208},{224... | collective-permute-start | bytes 368648 | tf_op jit(solution)/shard_map/ppermute | solution.py:680
  39.9 0.7 collective-permute-start.5
  40.5 1.3 %shard_map.126 = (f32[8,128]{1,0:T(8,128)S(1)}, f32[12,8,1024]{2,1,0:T(8,128)S(1)}) custom-call(s32[8]{0:T(128)S(1)} %copy-done.10, f32[8,16,1024]{2,1,0:T(8,128)S(1)} %get-tuple-element.50.cond_o.cond, f32[8,16,1024]{2,1,0:T(8,128)S(1)} %get-tuple-element.62.prior_x, f32[8,16,1024]{2,1,0:T(8,128)S(1)} %get-tuple-element.51.prior_i.prior_y, ...), custom_call_target="tpu_custom_call" | custom-call | flops 4194304 | bytes 4194304 | tf_op jit(solution)/shard_map/pallas_call | solution.py:666
  41.8 0.3 collective-permute-done.4.ma
  42.1 0.0 collective-permute-done.5.mb
  42.1 1.4 %shard_map.127 = (f32[32,1,128]{2,1,0:T(1,128)S(1)}, f32[32,1024]{1,0:T(8,128)S(1)}) custom-call(s32[8]{0:T(128)S(1)} %copy-done.10, f32[8,128]{1,0:T(8,128)S(1)} %get-tuple-element.64.inner, f32[12,8,1024]{2,1,0:T(8,128)S(1)} %get-tuple-element.65.ends, f32[2,8,1024]{2,1,0:T(8,128)S(1)} %get-tuple-element.66.edges, ...), custom_call_target="tpu_custom_call" | custom-call | tf_op jit(solution)/shard_map/pallas_call | solution.py:666
  43.5 22.3 %all_to_all.10.held = f32[32,1,128]{2,1,0:T(1,128)S(1)} all-to-all(f32[32,1,128]{2,1,0:T(1,128)S(1)} %get-tuple-element.72), channel_id=1, replica_groups=mesh['z_lo'=8,'x'=4,'y'=4,'z_hi'=2,'core'=2] {'x','y','core'}, dimensions={0} | all-to-all | bytes 32768 | tf_op jit(solution)/shard_map/all_to_all | solution.py:697
  65.9 0.6 shard_map.129
  66.5 5.4 %all-to-all-start.1 = ((f32[16,1,128]{2,1,0:T(1,128)}), f32[16,1,128]{2,1,0:T(1,128)S(1)}, u32[]{:S(2)}, u32[]{:S(2)}) async-start(f32[16,1,128]{2,1,0:T(1,128)} %shard_map.129), calls=%async_computation.1 | async-start | bytes 16384 | tf_op jit(solution)/shard_map/all_to_all | solution.py:699
  71.9 5.2 %shard_map.128 = (f32[8,16,1024]{2,1,0:T(8,128)}, f32[8,16,1024]{2,1,0:T(8,128)}) custom-call(s32[8]{0:T(128)S(1)} %copy-done.10, f32[8,16,1024]{2,1,0:T(8,128)S(1)} %get-tuple-element.50.cond_o.cond, f32[8,16,1024]{2,1,0:T(8,128)S(1)} %get-tuple-element.61.early, f32[32,1024]{1,0:T(8,128)S(1)} %get-tuple-element.69.sides, f32[8,16,1024]{2,1,0:T(8,128)S(1)} %copy-done.2, ...), custom_call_target="tpu_custom_call" | custom-call | flops 12582912 | bytes 12582912 | tf_op jit(solution)/shard_map/pallas_call | solution.py:666
  77.2 6.0 %all-to-all-done.1.held = f32[16,1,128]{2,1,0:T(1,128)S(1)} async-done(((f32[16,1,128]{2,1,0:T(1,128)}), f32[16,1,128]{2,1,0:T(1,128)S(1)}, u32[]{:S(2)}, u32[]{:S(2)}) %all-to-all-start.1) | async-done | bytes 8224 | tf_op jit(solution)/shard_map/all_to_all | solution.py:699
  83.2 0.7 shard_map.130
Async XLA Ops:
  0.6 22.2 %copy-start.4 = (s32[8,16,1024]{2,1,0:T(8,128)S(1)}, s32[8,16,1024]{2,1,0:T(8,128)}, u32[]{:S(2)}) copy-start(s32[8,16,1024]{2,1,0:T(8,128)} %blk.1) | copy-start | bytes 1572868
  0.6 22.2 %copy-start.3 = (f32[8,16,1024]{2,1,0:T(8,128)S(1)}, f32[8,16,1024]{2,1,0:T(8,128)}, u32[]{:S(2)}) copy-start(f32[8,16,1024]{2,1,0:T(8,128)} %mob.1) | copy-start | bytes 1572868
  0.7 22.2 %copy-start.2 = (f32[8,16,1024]{2,1,0:T(8,128)S(1)}, f32[8,16,1024]{2,1,0:T(8,128)}, u32[]{:S(2)}) copy-start(f32[8,16,1024]{2,1,0:T(8,128)} %stress.1) | copy-start | bytes 1572868
  0.7 22.2 %copy-start.8 = (f32[16,1024]{1,0:T(8,128)S(1)}, f32[16,1024]{1,0:T(8,128)}, u32[]{:S(2)}) copy-start(f32[16,1024]{1,0:T(8,128)} %load.3) | copy-start | bytes 196612
  0.7 22.2 %copy-start.7 = (s32[16,1024]{1,0:T(8,128)S(1)}, s32[16,1024]{1,0:T(8,128)}, u32[]{:S(2)}) copy-start(s32[16,1024]{1,0:T(8,128)} %pad.3) | copy-start | bytes 196612
  0.7 22.2 %copy-start.6 = (s32[7,16,1024]{2,1,0:T(8,128)S(1)}, s32[7,16,1024]{2,1,0:T(8,128)}, u32[]{:S(2)}) copy-start(s32[7,16,1024]{2,1,0:T(8,128)} %via_mask.1) | copy-start | bytes 1376260
  0.7 22.2 %copy-start.5 = (f32[7,16,1024]{2,1,0:T(8,128)S(1)}, f32[7,16,1024]{2,1,0:T(8,128)}, u32[]{:S(2)}) copy-start(f32[7,16,1024]{2,1,0:T(8,128)} %via_cond.1) | copy-start | bytes 1376260
  0.7 22.2 %copy-start.1 = (f32[8,16,1024]{2,1,0:T(8,128)S(1)}, f32[8,16,1024]{2,1,0:T(8,128)}, u32[]{:S(2)}) copy-start(f32[8,16,1024]{2,1,0:T(8,128)} %seg.1) | copy-start | bytes 1572868
  0.7 22.2 %copy-start = (f32[8,16,1024]{2,1,0:T(8,128)S(1)}, f32[8,16,1024]{2,1,0:T(8,128)}, u32[]{:S(2)}) copy-start(f32[8,16,1024]{2,1,0:T(8,128)} %volts.2) | copy-start | bytes 1572868
  4.1 25.7 %collective-permute-start.2 = (f32[6,8,128]{2,1,0:T(8,128)}, f32[6,8,128]{2,1,0:T(8,128)S(1)}, u32[]{:S(2)}, u32[]{:S(2)}) collective-permute-start(f32[6,8,128]{2,1,0:T(8,128)} %get-tuple-element.57), channel_id=1, source_target_pairs={{1,2},{3,4},{5,6},{7,8},{9,10},{11,12},{13,14},{2,1},{4,3},{6,5},{... | collective-permute-start | bytes 73736 | tf_op jit(solution)/shard_map/ppermute | solution.py:680
  20.9 2.0 %copy-start.10 = (s32[8]{0:T(128)S(1)}, s32[8]{0:T(128)}, u32[]{:S(2)}) copy-start(s32[8]{0:T(128)} %dirs.13) | copy-start | bytes 100
  20.9 8.8 %collective-permute-start.3 = (f32[6,8,128]{2,1,0:T(8,128)}, f32[6,8,128]{2,1,0:T(8,128)S(1)}, u32[]{:S(2)}, u32[]{:S(2)}) collective-permute-start(f32[6,8,128]{2,1,0:T(8,128)} %get-tuple-element.58), channel_id=1, source_target_pairs={{0,1},{2,3},{4,5},{6,7},{8,9},{10,11},{12,13},{14,15},{1,0},{3,2},... | collective-permute-start | bytes 73736 | tf_op jit(solution)/shard_map/ppermute | solution.py:680
  24.0 7.9 %collective-permute-start = (f32[48,1024]{1,0:T(8,128)S(1)}, f32[48,1024]{1,0:T(8,128)S(1)}, u32[]{:S(2)}, u32[]{:S(2)}) collective-permute-start(f32[48,1024]{1,0:T(8,128)S(1)} %get-tuple-element.48.after_a), channel_id=1, source_target_pairs={{0,16},{32,48},{64,80},{96,112},{128,144},{160,176},{192,208},{224... | collective-permute-start | bytes 589832 | tf_op jit(solution)/shard_map/ppermute | solution.py:680
  27.1 2.7 %copy-start.9 = (f32[2,6,16,128]{3,2,1,0:T(8,128)S(1)}, f32[2,6,16,128]{3,2,1,0:T(8,128)}, u32[]{:S(2)}) copy-start(f32[2,6,16,128]{3,2,1,0:T(8,128)} %get-tuple-element.56.own) | copy-start | bytes 294916
  27.1 4.7 %collective-permute-start.1 = (f32[48,1024]{1,0:T(8,128)S(1)}, f32[48,1024]{1,0:T(8,128)S(1)}, u32[]{:S(2)}, u32[]{:S(2)}) collective-permute-start(f32[48,1024]{1,0:T(8,128)S(1)} %get-tuple-element.49.after_b), channel_id=1, source_target_pairs={{16,32},{48,64},{80,96},{112,128},{144,160},{176,192},{208,224},{2... | collective-permute-start | bytes 589832 | tf_op jit(solution)/shard_map/ppermute | solution.py:680
  34.0 8.1 %collective-permute-start.4 = (f32[240,128]{1,0:T(8,128)S(1)}, f32[240,128]{1,0:T(8,128)S(1)}, u32[]{:S(2)}, u32[]{:S(2)}) collective-permute-start(f32[240,128]{1,0:T(8,128)S(1)} %get-tuple-element.67), channel_id=1, source_target_pairs={{0,16},{32,48},{64,80},{96,112},{128,144},{160,176},{192,208},{224... | collective-permute-start | bytes 368648 | tf_op jit(solution)/shard_map/ppermute | solution.py:680
  39.9 2.3 %collective-permute-start.5 = (f32[240,128]{1,0:T(8,128)S(1)}, f32[240,128]{1,0:T(8,128)S(1)}, u32[]{:S(2)}, u32[]{:S(2)}) collective-permute-start(f32[240,128]{1,0:T(8,128)S(1)} %get-tuple-element.68), channel_id=1, source_target_pairs={{16,32},{48,64},{80,96},{112,128},{144,160},{176,192},{208,224},{2... | collective-permute-start | bytes 368648 | tf_op jit(solution)/shard_map/ppermute | solution.py:680
  66.5 16.7 %all-to-all-start.1 = ((f32[16,1,128]{2,1,0:T(1,128)}), f32[16,1,128]{2,1,0:T(1,128)S(1)}, u32[]{:S(2)}, u32[]{:S(2)}) async-start(f32[16,1,128]{2,1,0:T(1,128)} %shard_map.129), calls=%async_computation.1 | async-start | bytes 16384 | tf_op jit(solution)/shard_map/all_to_all | solution.py:699

commit v7 on v6

--- a/solution.py
+++ b/solution.py
@@ -68,7 +68,7 @@
 def fetch(sources, targets, sems):
     copies = [pltpu.make_async_copy(a, b, sems.at[i]) for i, (a, b) in enumerate(zip(sources, targets))]
     for copy in copies:
-        copy.start()
+        copy.start(priority=1)
     return copies
 
 

time: 84.2 us -> 84.2 us (level)
  no operation moved by 1% of the time
where the time goes in v7:
time: 84.2 us; the launch traced here: 83.8 us
  starting transfers between devices  34.6 us (41%)
  blocking collectives  22.3 us (26%)
  Pallas kernels  17.6 us (21%)
  waiting for transfers between devices  8.24 us (10%)
  between operations  0.94 us (1%)
    ppermute x6, starting transfers between devices, swap(): return lax.ppermute(value, axes, pairs + [(b, a) for a, b in pairs])  29.2 us
    all_to_all x1, blocking collectives, rms_all(): got = lax.all_to_all(held, NEAR, 0, 0)  22.3 us
    pallas_call x10, Pallas kernels, call(): pl.pallas_call(kernel, out_shape=[jax.ShapeDtypeStruct(s, jnp.float32) fo...  17.6 us
    all_to_all x1, waiting for transfers between devices, rms_all(): got = lax.all_to_all(held, FAR, 0, 0)  6.02 us
    all_to_all x1, starting transfers between devices, rms_all(): got = lax.all_to_all(held, FAR, 0, 0)  5.45 us
    ppermute x6, waiting for transfers between devices, swap(): return lax.ppermute(value, axes, pairs + [(b, a) for a, b in pairs])  2.22 us
  transfers between devices with their start and end apart: 7, of which 3 were waited for; matrix products, arithmetic and copies ran while one was open for 0% of the time, Pallas kernels for 11%

profile of v7, /device:TPU:1, one launch (start us, length us, event | category | flops | bytes accessed | tf_op | source)
XLA Modules:
  0.0 83.8 jit_solution(15853616199973587131)
XLA Ops:
  0.6 0.0 copy-start.4
  0.6 0.0 copy-start.3
  0.7 0.0 copy-start.2
  0.7 0.0 copy-start.8
  0.7 0.0 copy-start.7
  0.7 0.0 copy-start.6
  0.7 0.0 copy-start.5
  0.7 0.0 copy-start.1
  0.7 0.0 copy-start
  0.7 3.3 %shard_map.121 = (f32[2,6,16,128]{3,2,1,0:T(8,128)}, f32[6,8,128]{2,1,0:T(8,128)}, f32[6,8,128]{2,1,0:T(8,128)}) custom-call(s32[8]{0:T(128)} %dirs.13, f32[8,16,1024]{2,1,0:T(8,128)} %volts.2, f32[8,16,1024]{2,1,0:T(8,128)} %seg.1, f32[7,16,1024]{2,1,0:T(8,128)} %via_cond.1, s32[7,16,1024]{2,1,0:T(8,128)} %via_mask.1, s32[16,1024]{1,0:T(8,128)} %pad.3, ...), custom_call_target="tpu_custom_call" | custom-call | tf_op jit(solution)/shard_map/pallas_call | solution.py:666
  4.1 16.8 %collective-permute-start.2 = (f32[6,8,128]{2,1,0:T(8,128)}, f32[6,8,128]{2,1,0:T(8,128)S(1)}, u32[]{:S(2)}, u32[]{:S(2)}) collective-permute-start(f32[6,8,128]{2,1,0:T(8,128)} %get-tuple-element.57), channel_id=1, source_target_pairs={{1,2},{3,4},{5,6},{7,8},{9,10},{11,12},{13,14},{2,1},{4,3},{6,5},{... | collective-permute-start | bytes 73736 | tf_op jit(solution)/shard_map/ppermute | solution.py:680
  20.9 0.0 copy-start.10
  20.9 1.9 %collective-permute-start.3 = (f32[6,8,128]{2,1,0:T(8,128)}, f32[6,8,128]{2,1,0:T(8,128)S(1)}, u32[]{:S(2)}, u32[]{:S(2)}) collective-permute-start(f32[6,8,128]{2,1,0:T(8,128)} %get-tuple-element.58), channel_id=1, source_target_pairs={{0,1},{2,3},{4,5},{6,7},{8,9},{10,11},{12,13},{14,15},{1,0},{3,2},... | collective-permute-start | bytes 73736 | tf_op jit(solution)/shard_map/ppermute | solution.py:680
  22.9 0.0 copy-done.4
  22.9 0.0 copy-done.3
  22.9 0.0 copy-done.2
  22.9 0.0 copy-done.8
  22.9 0.0 copy-done.7
  22.9 0.0 copy-done.6
  22.9 0.0 copy-done.5
  22.9 0.0 copy-done.1
  22.9 0.0 copy-done
  22.9 0.0 copy-done.10
  23.0 1.0 %shard_map.122 = (f32[48,1024]{1,0:T(8,128)S(1)}, f32[48,1024]{1,0:T(8,128)S(1)}) custom-call(s32[8]{0:T(128)S(1)} %copy-done.10, f32[8,16,1024]{2,1,0:T(8,128)S(1)} %copy-done, f32[8,16,1024]{2,1,0:T(8,128)S(1)} %copy-done.1, f32[7,16,1024]{2,1,0:T(8,128)S(1)} %copy-done.5, s32[7,16,1024]{2,1,0:T(8,128)S(1)} %copy-done.6, s32[16,1024]{1,0:T(8,128)S(1)} %copy-done.7, ...), custom_call_target="tpu_custom_call" | custom-call | flops 1048576 | bytes 1048576 | tf_op jit(solution)/shard_map/pallas_call | solution.py:666
  24.0 3.1 %collective-permute-start = (f32[48,1024]{1,0:T(8,128)S(1)}, f32[48,1024]{1,0:T(8,128)S(1)}, u32[]{:S(2)}, u32[]{:S(2)}) collective-permute-start(f32[48,1024]{1,0:T(8,128)S(1)} %get-tuple-element.48.after_a), channel_id=1, source_target_pairs={{0,16},{32,48},{64,80},{96,112},{128,144},{160,176},{192,208},{224... | collective-permute-start | bytes 589832 | tf_op jit(solution)/shard_map/ppermute | solution.py:680
  27.1 0.0 copy-start.9
  27.1 0.8 collective-permute-start.1
  27.9 1.8 %shard_map.123 = (f32[8,16,1024]{2,1,0:T(8,128)S(1)}, f32[8,16,1024]{2,1,0:T(8,128)S(1)}, f32[7,16,1024]{2,1,0:T(8,128)S(1)}, f32[8,16,1024]{2,1,0:T(8,128)S(1)}...) custom-call(s32[8]{0:T(128)S(1)} %copy-done.10, f32[48,1024]{1,0:T(8,128)S(1)} %get-tuple-element.48.after_a, ...), custom_call_target="tpu_custom_call" | custom-call | flops 4194304 | bytes 4194304 | tf_op jit(solution)/shard_map/pallas_call | solution.py:666
  29.7 0.0 collective-permute-done.2.gyb
  29.8 0.0 collective-permute-done.3.gya
  29.8 0.0 copy-done.9
  29.8 0.1 shard_map.124
  29.9 1.9 %collective-permute-done.gxa = f32[48,1024]{1,0:T(8,128)S(1)} collective-permute-done((f32[48,1024]{1,0:T(8,128)S(1)}, f32[48,1024]{1,0:T(8,128)S(1)}, u32[]{:S(2)}, u32[]{:S(2)}) %collective-permute-start) | collective-permute-done | bytes 196640 | tf_op jit(solution)/shard_map/ppermute | solution.py:680
  31.8 0.0 collective-permute-done.1.gxb
  31.8 2.2 %shard_map.125 = (f32[8,16,1024]{2,1,0:T(8,128)S(1)}, f32[8,16,1024]{2,1,0:T(8,128)S(1)}, f32[8,16,1024]{2,1,0:T(8,128)S(1)}, f32[2,8,1024]{2,1,0:T(8,128)S(1)},...) custom-call(s32[8]{0:T(128)S(1)} %copy-done.10, f32[8,16,1024]{2,1,0:T(8,128)S(1)} %get-tuple-element.50.cond_o.cond, ...), custom_call_target="tpu_custom_call" | custom-call | flops 1024 | bytes 1024 | tf_op jit(solution)/shard_map/pallas_call | solution.py:666
  34.0 5.8 %collective-permute-start.4 = (f32[240,128]{1,0:T(8,128)S(1)}, f32[240,128]{1,0:T(8,128)S(1)}, u32[]{:S(2)}, u32[]{:S(2)}) collective-permute-start(f32[240,128]{1,0:T(8,128)S(1)} %get-tuple-element.67), channel_id=1, source_target_pairs={{0,16},{32,48},{64,80},{96,112},{128,144},{160,176},{192,208},{224... | collective-permute-start | bytes 368648 | tf_op jit(solution)/shard_map/ppermute | solution.py:680
  39.8 0.7 collective-permute-start.5
  40.5 1.3 %shard_map.126 = (f32[8,128]{1,0:T(8,128)S(1)}, f32[12,8,1024]{2,1,0:T(8,128)S(1)}) custom-call(s32[8]{0:T(128)S(1)} %copy-done.10, f32[8,16,1024]{2,1,0:T(8,128)S(1)} %get-tuple-element.50.cond_o.cond, f32[8,16,1024]{2,1,0:T(8,128)S(1)} %get-tuple-element.62.prior_x, f32[8,16,1024]{2,1,0:T(8,128)S(1)} %get-tuple-element.51.prior_i.prior_y, ...), custom_call_target="tpu_custom_call" | custom-call | flops 4194304 | bytes 4194304 | tf_op jit(solution)/shard_map/pallas_call | solution.py:666
  41.8 0.3 collective-permute-done.4.ma
  42.1 0.0 collective-permute-done.5.mb
  42.1 1.4 %shard_map.127 = (f32[32,1,128]{2,1,0:T(1,128)S(1)}, f32[32,1024]{1,0:T(8,128)S(1)}) custom-call(s32[8]{0:T(128)S(1)} %copy-done.10, f32[8,128]{1,0:T(8,128)S(1)} %get-tuple-element.64.inner, f32[12,8,1024]{2,1,0:T(8,128)S(1)} %get-tuple-element.65.ends, f32[2,8,1024]{2,1,0:T(8,128)S(1)} %get-tuple-element.66.edges, ...), custom_call_target="tpu_custom_call" | custom-call | tf_op jit(solution)/shard_map/pallas_call | solution.py:666
  43.5 22.3 %all_to_all.10.held = f32[32,1,128]{2,1,0:T(1,128)S(1)} all-to-all(f32[32,1,128]{2,1,0:T(1,128)S(1)} %get-tuple-element.72), channel_id=1, replica_groups=mesh['z_lo'=8,'x'=4,'y'=4,'z_hi'=2,'core'=2] {'x','y','core'}, dimensions={0} | all-to-all | bytes 32768 | tf_op jit(solution)/shard_map/all_to_all | solution.py:697
  65.8 0.6 shard_map.129
  66.5 5.4 %all-to-all-start.1 = ((f32[16,1,128]{2,1,0:T(1,128)}), f32[16,1,128]{2,1,0:T(1,128)S(1)}, u32[]{:S(2)}, u32[]{:S(2)}) async-start(f32[16,1,128]{2,1,0:T(1,128)} %shard_map.129), calls=%async_computation.1 | async-start | bytes 16384 | tf_op jit(solution)/shard_map/all_to_all | solution.py:699
  71.9 5.2 %shard_map.128 = (f32[8,16,1024]{2,1,0:T(8,128)}, f32[8,16,1024]{2,1,0:T(8,128)}) custom-call(s32[8]{0:T(128)S(1)} %copy-done.10, f32[8,16,1024]{2,1,0:T(8,128)S(1)} %get-tuple-element.50.cond_o.cond, f32[8,16,1024]{2,1,0:T(8,128)S(1)} %get-tuple-element.61.early, f32[32,1024]{1,0:T(8,128)S(1)} %get-tuple-element.69.sides, f32[8,16,1024]{2,1,0:T(8,128)S(1)} %copy-done.2, ...), custom_call_target="tpu_custom_call" | custom-call | flops 12582912 | bytes 12582912 | tf_op jit(solution)/shard_map/pallas_call | solution.py:666
  77.1 6.0 %all-to-all-done.1.held = f32[16,1,128]{2,1,0:T(1,128)S(1)} async-done(((f32[16,1,128]{2,1,0:T(1,128)}), f32[16,1,128]{2,1,0:T(1,128)S(1)}, u32[]{:S(2)}, u32[]{:S(2)}) %all-to-all-start.1) | async-done | bytes 8224 | tf_op jit(solution)/shard_map/all_to_all | solution.py:699
  83.1 0.7 shard_map.130
Async XLA Ops:
  0.6 22.2 %copy-start.4 = (s32[8,16,1024]{2,1,0:T(8,128)S(1)}, s32[8,16,1024]{2,1,0:T(8,128)}, u32[]{:S(2)}) copy-start(s32[8,16,1024]{2,1,0:T(8,128)} %blk.1) | copy-start | bytes 1572868
  0.6 22.2 %copy-start.3 = (f32[8,16,1024]{2,1,0:T(8,128)S(1)}, f32[8,16,1024]{2,1,0:T(8,128)}, u32[]{:S(2)}) copy-start(f32[8,16,1024]{2,1,0:T(8,128)} %mob.1) | copy-start | bytes 1572868
  0.7 22.2 %copy-start.2 = (f32[8,16,1024]{2,1,0:T(8,128)S(1)}, f32[8,16,1024]{2,1,0:T(8,128)}, u32[]{:S(2)}) copy-start(f32[8,16,1024]{2,1,0:T(8,128)} %stress.1) | copy-start | bytes 1572868
  0.7 22.2 %copy-start.8 = (f32[16,1024]{1,0:T(8,128)S(1)}, f32[16,1024]{1,0:T(8,128)}, u32[]{:S(2)}) copy-start(f32[16,1024]{1,0:T(8,128)} %load.3) | copy-start | bytes 196612
  0.7 22.2 %copy-start.7 = (s32[16,1024]{1,0:T(8,128)S(1)}, s32[16,1024]{1,0:T(8,128)}, u32[]{:S(2)}) copy-start(s32[16,1024]{1,0:T(8,128)} %pad.3) | copy-start | bytes 196612
  0.7 22.2 %copy-start.6 = (s32[7,16,1024]{2,1,0:T(8,128)S(1)}, s32[7,16,1024]{2,1,0:T(8,128)}, u32[]{:S(2)}) copy-start(s32[7,16,1024]{2,1,0:T(8,128)} %via_mask.1) | copy-start | bytes 1376260
  0.7 22.2 %copy-start.5 = (f32[7,16,1024]{2,1,0:T(8,128)S(1)}, f32[7,16,1024]{2,1,0:T(8,128)}, u32[]{:S(2)}) copy-start(f32[7,16,1024]{2,1,0:T(8,128)} %via_cond.1) | copy-start | bytes 1376260
  0.7 22.2 %copy-start.1 = (f32[8,16,1024]{2,1,0:T(8,128)S(1)}, f32[8,16,1024]{2,1,0:T(8,128)}, u32[]{:S(2)}) copy-start(f32[8,16,1024]{2,1,0:T(8,128)} %seg.1) | copy-start | bytes 1572868
  0.7 22.2 %copy-start = (f32[8,16,1024]{2,1,0:T(8,128)S(1)}, f32[8,16,1024]{2,1,0:T(8,128)}, u32[]{:S(2)}) copy-start(f32[8,16,1024]{2,1,0:T(8,128)} %volts.2) | copy-start | bytes 1572868
  4.1 25.7 %collective-permute-start.2 = (f32[6,8,128]{2,1,0:T(8,128)}, f32[6,8,128]{2,1,0:T(8,128)S(1)}, u32[]{:S(2)}, u32[]{:S(2)}) collective-permute-start(f32[6,8,128]{2,1,0:T(8,128)} %get-tuple-element.57), channel_id=1, source_target_pairs={{1,2},{3,4},{5,6},{7,8},{9,10},{11,12},{13,14},{2,1},{4,3},{6,5},{... | collective-permute-start | bytes 73736 | tf_op jit(solution)/shard_map/ppermute | solution.py:680
  20.9 2.0 %copy-start.10 = (s32[8]{0:T(128)S(1)}, s32[8]{0:T(128)}, u32[]{:S(2)}) copy-start(s32[8]{0:T(128)} %dirs.13) | copy-start | bytes 100
  20.9 8.8 %collective-permute-start.3 = (f32[6,8,128]{2,1,0:T(8,128)}, f32[6,8,128]{2,1,0:T(8,128)S(1)}, u32[]{:S(2)}, u32[]{:S(2)}) collective-permute-start(f32[6,8,128]{2,1,0:T(8,128)} %get-tuple-element.58), channel_id=1, source_target_pairs={{0,1},{2,3},{4,5},{6,7},{8,9},{10,11},{12,13},{14,15},{1,0},{3,2},... | collective-permute-start | bytes 73736 | tf_op jit(solution)/shard_map/ppermute | solution.py:680
  24.0 7.9 %collective-permute-start = (f32[48,1024]{1,0:T(8,128)S(1)}, f32[48,1024]{1,0:T(8,128)S(1)}, u32[]{:S(2)}, u32[]{:S(2)}) collective-permute-start(f32[48,1024]{1,0:T(8,128)S(1)} %get-tuple-element.48.after_a), channel_id=1, source_target_pairs={{0,16},{32,48},{64,80},{96,112},{128,144},{160,176},{192,208},{224... | collective-permute-start | bytes 589832 | tf_op jit(solution)/shard_map/ppermute | solution.py:680
  27.1 2.7 %copy-start.9 = (f32[2,6,16,128]{3,2,1,0:T(8,128)S(1)}, f32[2,6,16,128]{3,2,1,0:T(8,128)}, u32[]{:S(2)}) copy-start(f32[2,6,16,128]{3,2,1,0:T(8,128)} %get-tuple-element.56.own) | copy-start | bytes 294916
  27.1 4.7 %collective-permute-start.1 = (f32[48,1024]{1,0:T(8,128)S(1)}, f32[48,1024]{1,0:T(8,128)S(1)}, u32[]{:S(2)}, u32[]{:S(2)}) collective-permute-start(f32[48,1024]{1,0:T(8,128)S(1)} %get-tuple-element.49.after_b), channel_id=1, source_target_pairs={{16,32},{48,64},{80,96},{112,128},{144,160},{176,192},{208,224},{2... | collective-permute-start | bytes 589832 | tf_op jit(solution)/shard_map/ppermute | solution.py:680
  34.0 8.1 %collective-permute-start.4 = (f32[240,128]{1,0:T(8,128)S(1)}, f32[240,128]{1,0:T(8,128)S(1)}, u32[]{:S(2)}, u32[]{:S(2)}) collective-permute-start(f32[240,128]{1,0:T(8,128)S(1)} %get-tuple-element.67), channel_id=1, source_target_pairs={{0,16},{32,48},{64,80},{96,112},{128,144},{160,176},{192,208},{224... | collective-permute-start | bytes 368648 | tf_op jit(solution)/shard_map/ppermute | solution.py:680
  39.8 2.3 %collective-permute-start.5 = (f32[240,128]{1,0:T(8,128)S(1)}, f32[240,128]{1,0:T(8,128)S(1)}, u32[]{:S(2)}, u32[]{:S(2)}) collective-permute-start(f32[240,128]{1,0:T(8,128)S(1)} %get-tuple-element.68), channel_id=1, source_target_pairs={{16,32},{48,64},{80,96},{112,128},{144,160},{176,192},{208,224},{2... | collective-permute-start | bytes 368648 | tf_op jit(solution)/shard_map/ppermute | solution.py:680
  66.5 16.7 %all-to-all-start.1 = ((f32[16,1,128]{2,1,0:T(1,128)}), f32[16,1,128]{2,1,0:T(1,128)S(1)}, u32[]{:S(2)}, u32[]{:S(2)}) async-start(f32[16,1,128]{2,1,0:T(1,128)} %shard_map.129), calls=%async_computation.1 | async-start | bytes 16384 | tf_op jit(solution)/shard_map/all_to_all | solution.py:699

commit v8 on v7

--- a/solution.py
+++ b/solution.py
@@ -32,7 +32,7 @@
 X = ("z_lo", "x")
 Y = ("y", "z_hi", "core")
 NEAR = ("x", "y", "core")
-FAR = ("z_hi", "z_lo")
+FAR = ("z_lo", "z_hi")
 
 
 def position():

time: 84.2 us -> 84.2 us (level)
  no operation moved by 1% of the time
where the time goes in v8:
time: 84.2 us; the launch traced here: 83.8 us
  starting transfers between devices  34.6 us (41%)
  blocking collectives  22.3 us (26%)
  Pallas kernels  17.6 us (21%)
  waiting for transfers between devices  8.25 us (10%)
  between operations  0.94 us (1%)
    ppermute x6, starting transfers between devices, swap(): return lax.ppermute(value, axes, pairs + [(b, a) for a, b in pairs])  29.2 us
    all_to_all x1, blocking collectives, rms_all(): got = lax.all_to_all(held, NEAR, 0, 0)  22.3 us
    pallas_call x10, Pallas kernels, call(): pl.pallas_call(kernel, out_shape=[jax.ShapeDtypeStruct(s, jnp.float32) fo...  17.6 us
    all_to_all x1, waiting for transfers between devices, rms_all(): got = lax.all_to_all(held, FAR, 0, 0)  6.03 us
    all_to_all x1, starting transfers between devices, rms_all(): got = lax.all_to_all(held, FAR, 0, 0)  5.45 us
    ppermute x6, waiting for transfers between devices, swap(): return lax.ppermute(value, axes, pairs + [(b, a) for a, b in pairs])  2.21 us
  transfers between devices with their start and end apart: 7, of which 3 were waited for; matrix products, arithmetic and copies ran while one was open for 0% of the time, Pallas kernels for 11%

profile of v8, /device:TPU:1, one launch (start us, length us, event | category | flops | bytes accessed | tf_op | source)
XLA Modules:
  0.0 83.8 jit_solution(9778569876305511355)
XLA Ops:
  0.6 0.0 copy-start.4
  0.6 0.0 copy-start.3
  0.7 0.0 copy-start.2
  0.7 0.0 copy-start.8
  0.7 0.0 copy-start.7
  0.7 0.0 copy-start.6
  0.7 0.0 copy-start.5
  0.7 0.0 copy-start.1
  0.7 0.0 copy-start
  0.7 3.3 %shard_map.121 = (f32[2,6,16,128]{3,2,1,0:T(8,128)}, f32[6,8,128]{2,1,0:T(8,128)}, f32[6,8,128]{2,1,0:T(8,128)}) custom-call(s32[8]{0:T(128)} %dirs.13, f32[8,16,1024]{2,1,0:T(8,128)} %volts.2, f32[8,16,1024]{2,1,0:T(8,128)} %seg.1, f32[7,16,1024]{2,1,0:T(8,128)} %via_cond.1, s32[7,16,1024]{2,1,0:T(8,128)} %via_mask.1, s32[16,1024]{1,0:T(8,128)} %pad.3, ...), custom_call_target="tpu_custom_call" | custom-call | tf_op jit(solution)/shard_map/pallas_call | solution.py:666
  4.1 16.8 %collective-permute-start.2 = (f32[6,8,128]{2,1,0:T(8,128)}, f32[6,8,128]{2,1,0:T(8,128)S(1)}, u32[]{:S(2)}, u32[]{:S(2)}) collective-permute-start(f32[6,8,128]{2,1,0:T(8,128)} %get-tuple-element.57), channel_id=1, source_target_pairs={{1,2},{3,4},{5,6},{7,8},{9,10},{11,12},{13,14},{2,1},{4,3},{6,5},{... | collective-permute-start | bytes 73736 | tf_op jit(solution)/shard_map/ppermute | solution.py:680
  20.9 0.0 copy-start.10
  20.9 1.9 %collective-permute-start.3 = (f32[6,8,128]{2,1,0:T(8,128)}, f32[6,8,128]{2,1,0:T(8,128)S(1)}, u32[]{:S(2)}, u32[]{:S(2)}) collective-permute-start(f32[6,8,128]{2,1,0:T(8,128)} %get-tuple-element.58), channel_id=1, source_target_pairs={{0,1},{2,3},{4,5},{6,7},{8,9},{10,11},{12,13},{14,15},{1,0},{3,2},... | collective-permute-start | bytes 73736 | tf_op jit(solution)/shard_map/ppermute | solution.py:680
  22.9 0.0 copy-done.4
  22.9 0.0 copy-done.3
  22.9 0.0 copy-done.2
  22.9 0.0 copy-done.8
  22.9 0.0 copy-done.7
  22.9 0.0 copy-done.6
  22.9 0.0 copy-done.5
  22.9 0.0 copy-done.1
  22.9 0.0 copy-done
  22.9 0.0 copy-done.10
  23.0 1.0 %shard_map.122 = (f32[48,1024]{1,0:T(8,128)S(1)}, f32[48,1024]{1,0:T(8,128)S(1)}) custom-call(s32[8]{0:T(128)S(1)} %copy-done.10, f32[8,16,1024]{2,1,0:T(8,128)S(1)} %copy-done, f32[8,16,1024]{2,1,0:T(8,128)S(1)} %copy-done.1, f32[7,16,1024]{2,1,0:T(8,128)S(1)} %copy-done.5, s32[7,16,1024]{2,1,0:T(8,128)S(1)} %copy-done.6, s32[16,1024]{1,0:T(8,128)S(1)} %copy-done.7, ...), custom_call_target="tpu_custom_call" | custom-call | flops 1048576 | bytes 1048576 | tf_op jit(solution)/shard_map/pallas_call | solution.py:666
  24.0 3.1 %collective-permute-start = (f32[48,1024]{1,0:T(8,128)S(1)}, f32[48,1024]{1,0:T(8,128)S(1)}, u32[]{:S(2)}, u32[]{:S(2)}) collective-permute-start(f32[48,1024]{1,0:T(8,128)S(1)} %get-tuple-element.48.after_a), channel_id=1, source_target_pairs={{0,16},{32,48},{64,80},{96,112},{128,144},{160,176},{192,208},{224... | collective-permute-start | bytes 589832 | tf_op jit(solution)/shard_map/ppermute | solution.py:680
  27.1 0.0 copy-start.9
  27.1 0.8 collective-permute-start.1
  27.9 1.8 %shard_map.123 = (f32[8,16,1024]{2,1,0:T(8,128)S(1)}, f32[8,16,1024]{2,1,0:T(8,128)S(1)}, f32[7,16,1024]{2,1,0:T(8,128)S(1)}, f32[8,16,1024]{2,1,0:T(8,128)S(1)}...) custom-call(s32[8]{0:T(128)S(1)} %copy-done.10, f32[48,1024]{1,0:T(8,128)S(1)} %get-tuple-element.48.after_a, ...), custom_call_target="tpu_custom_call" | custom-call | flops 4194304 | bytes 4194304 | tf_op jit(solution)/shard_map/pallas_call | solution.py:666
  29.8 0.0 collective-permute-done.2.gyb
  29.8 0.0 collective-permute-done.3.gya
  29.8 0.0 copy-done.9
  29.8 0.1 shard_map.124
  29.9 1.9 %collective-permute-done.gxa = f32[48,1024]{1,0:T(8,128)S(1)} collective-permute-done((f32[48,1024]{1,0:T(8,128)S(1)}, f32[48,1024]{1,0:T(8,128)S(1)}, u32[]{:S(2)}, u32[]{:S(2)}) %collective-permute-start) | collective-permute-done | bytes 196640 | tf_op jit(solution)/shard_map/ppermute | solution.py:680
  31.8 0.0 collective-permute-done.1.gxb
  31.8 2.2 %shard_map.125 = (f32[8,16,1024]{2,1,0:T(8,128)S(1)}, f32[8,16,1024]{2,1,0:T(8,128)S(1)}, f32[8,16,1024]{2,1,0:T(8,128)S(1)}, f32[2,8,1024]{2,1,0:T(8,128)S(1)},...) custom-call(s32[8]{0:T(128)S(1)} %copy-done.10, f32[8,16,1024]{2,1,0:T(8,128)S(1)} %get-tuple-element.50.cond_o.cond, ...), custom_call_target="tpu_custom_call" | custom-call | flops 1024 | bytes 1024 | tf_op jit(solution)/shard_map/pallas_call | solution.py:666
  34.0 5.8 %collective-permute-start.4 = (f32[240,128]{1,0:T(8,128)S(1)}, f32[240,128]{1,0:T(8,128)S(1)}, u32[]{:S(2)}, u32[]{:S(2)}) collective-permute-start(f32[240,128]{1,0:T(8,128)S(1)} %get-tuple-element.67), channel_id=1, source_target_pairs={{0,16},{32,48},{64,80},{96,112},{128,144},{160,176},{192,208},{224... | collective-permute-start | bytes 368648 | tf_op jit(solution)/shard_map/ppermute | solution.py:680
  39.9 0.7 collective-permute-start.5
  40.5 1.3 %shard_map.126 = (f32[8,128]{1,0:T(8,128)S(1)}, f32[12,8,1024]{2,1,0:T(8,128)S(1)}) custom-call(s32[8]{0:T(128)S(1)} %copy-done.10, f32[8,16,1024]{2,1,0:T(8,128)S(1)} %get-tuple-element.50.cond_o.cond, f32[8,16,1024]{2,1,0:T(8,128)S(1)} %get-tuple-element.62.prior_x, f32[8,16,1024]{2,1,0:T(8,128)S(1)} %get-tuple-element.51.prior_i.prior_y, ...), custom_call_target="tpu_custom_call" | custom-call | flops 4194304 | bytes 4194304 | tf_op jit(solution)/shard_map/pallas_call | solution.py:666
  41.8 0.3 collective-permute-done.4.ma
  42.1 0.0 collective-permute-done.5.mb
  42.1 1.4 %shard_map.127 = (f32[32,1,128]{2,1,0:T(1,128)S(1)}, f32[32,1024]{1,0:T(8,128)S(1)}) custom-call(s32[8]{0:T(128)S(1)} %copy-done.10, f32[8,128]{1,0:T(8,128)S(1)} %get-tuple-element.64.inner, f32[12,8,1024]{2,1,0:T(8,128)S(1)} %get-tuple-element.65.ends, f32[2,8,1024]{2,1,0:T(8,128)S(1)} %get-tuple-element.66.edges, ...), custom_call_target="tpu_custom_call" | custom-call | tf_op jit(solution)/shard_map/pallas_call | solution.py:666
  43.5 22.3 %all_to_all.10.held = f32[32,1,128]{2,1,0:T(1,128)S(1)} all-to-all(f32[32,1,128]{2,1,0:T(1,128)S(1)} %get-tuple-element.72), channel_id=1, replica_groups=mesh['z_lo'=8,'x'=4,'y'=4,'z_hi'=2,'core'=2] {'x','y','core'}, dimensions={0} | all-to-all | bytes 32768 | tf_op jit(solution)/shard_map/all_to_all | solution.py:697
  65.9 0.6 shard_map.129
  66.5 5.4 %all-to-all-start.1 = ((f32[16,1,128]{2,1,0:T(1,128)}), f32[16,1,128]{2,1,0:T(1,128)S(1)}, u32[]{:S(2)}, u32[]{:S(2)}) async-start(f32[16,1,128]{2,1,0:T(1,128)} %shard_map.129), calls=%async_computation.1 | async-start | bytes 16384 | tf_op jit(solution)/shard_map/all_to_all | solution.py:699
  71.9 5.2 %shard_map.128 = (f32[8,16,1024]{2,1,0:T(8,128)}, f32[8,16,1024]{2,1,0:T(8,128)}) custom-call(s32[8]{0:T(128)S(1)} %copy-done.10, f32[8,16,1024]{2,1,0:T(8,128)S(1)} %get-tuple-element.50.cond_o.cond, f32[8,16,1024]{2,1,0:T(8,128)S(1)} %get-tuple-element.61.early, f32[32,1024]{1,0:T(8,128)S(1)} %get-tuple-element.69.sides, f32[8,16,1024]{2,1,0:T(8,128)S(1)} %copy-done.2, ...), custom_call_target="tpu_custom_call" | custom-call | flops 12582912 | bytes 12582912 | tf_op jit(solution)/shard_map/pallas_call | solution.py:666
  77.2 6.0 %all-to-all-done.1.held = f32[16,1,128]{2,1,0:T(1,128)S(1)} async-done(((f32[16,1,128]{2,1,0:T(1,128)}), f32[16,1,128]{2,1,0:T(1,128)S(1)}, u32[]{:S(2)}, u32[]{:S(2)}) %all-to-all-start.1) | async-done | bytes 8224 | tf_op jit(solution)/shard_map/all_to_all | solution.py:699
  83.2 0.7 shard_map.130
Async XLA Ops:
  0.6 22.2 %copy-start.4 = (s32[8,16,1024]{2,1,0:T(8,128)S(1)}, s32[8,16,1024]{2,1,0:T(8,128)}, u32[]{:S(2)}) copy-start(s32[8,16,1024]{2,1,0:T(8,128)} %blk.1) | copy-start | bytes 1572868
  0.6 22.2 %copy-start.3 = (f32[8,16,1024]{2,1,0:T(8,128)S(1)}, f32[8,16,1024]{2,1,0:T(8,128)}, u32[]{:S(2)}) copy-start(f32[8,16,1024]{2,1,0:T(8,128)} %mob.1) | copy-start | bytes 1572868
  0.7 22.2 %copy-start.2 = (f32[8,16,1024]{2,1,0:T(8,128)S(1)}, f32[8,16,1024]{2,1,0:T(8,128)}, u32[]{:S(2)}) copy-start(f32[8,16,1024]{2,1,0:T(8,128)} %stress.1) | copy-start | bytes 1572868
  0.7 22.2 %copy-start.8 = (f32[16,1024]{1,0:T(8,128)S(1)}, f32[16,1024]{1,0:T(8,128)}, u32[]{:S(2)}) copy-start(f32[16,1024]{1,0:T(8,128)} %load.3) | copy-start | bytes 196612
  0.7 22.2 %copy-start.7 = (s32[16,1024]{1,0:T(8,128)S(1)}, s32[16,1024]{1,0:T(8,128)}, u32[]{:S(2)}) copy-start(s32[16,1024]{1,0:T(8,128)} %pad.3) | copy-start | bytes 196612
  0.7 22.2 %copy-start.6 = (s32[7,16,1024]{2,1,0:T(8,128)S(1)}, s32[7,16,1024]{2,1,0:T(8,128)}, u32[]{:S(2)}) copy-start(s32[7,16,1024]{2,1,0:T(8,128)} %via_mask.1) | copy-start | bytes 1376260
  0.7 22.2 %copy-start.5 = (f32[7,16,1024]{2,1,0:T(8,128)S(1)}, f32[7,16,1024]{2,1,0:T(8,128)}, u32[]{:S(2)}) copy-start(f32[7,16,1024]{2,1,0:T(8,128)} %via_cond.1) | copy-start | bytes 1376260
  0.7 22.2 %copy-start.1 = (f32[8,16,1024]{2,1,0:T(8,128)S(1)}, f32[8,16,1024]{2,1,0:T(8,128)}, u32[]{:S(2)}) copy-start(f32[8,16,1024]{2,1,0:T(8,128)} %seg.1) | copy-start | bytes 1572868
  0.7 22.2 %copy-start = (f32[8,16,1024]{2,1,0:T(8,128)S(1)}, f32[8,16,1024]{2,1,0:T(8,128)}, u32[]{:S(2)}) copy-start(f32[8,16,1024]{2,1,0:T(8,128)} %volts.2) | copy-start | bytes 1572868
  4.1 25.7 %collective-permute-start.2 = (f32[6,8,128]{2,1,0:T(8,128)}, f32[6,8,128]{2,1,0:T(8,128)S(1)}, u32[]{:S(2)}, u32[]{:S(2)}) collective-permute-start(f32[6,8,128]{2,1,0:T(8,128)} %get-tuple-element.57), channel_id=1, source_target_pairs={{1,2},{3,4},{5,6},{7,8},{9,10},{11,12},{13,14},{2,1},{4,3},{6,5},{... | collective-permute-start | bytes 73736 | tf_op jit(solution)/shard_map/ppermute | solution.py:680
  20.9 2.0 %copy-start.10 = (s32[8]{0:T(128)S(1)}, s32[8]{0:T(128)}, u32[]{:S(2)}) copy-start(s32[8]{0:T(128)} %dirs.13) | copy-start | bytes 100
  20.9 8.8 %collective-permute-start.3 = (f32[6,8,128]{2,1,0:T(8,128)}, f32[6,8,128]{2,1,0:T(8,128)S(1)}, u32[]{:S(2)}, u32[]{:S(2)}) collective-permute-start(f32[6,8,128]{2,1,0:T(8,128)} %get-tuple-element.58), channel_id=1, source_target_pairs={{0,1},{2,3},{4,5},{6,7},{8,9},{10,11},{12,13},{14,15},{1,0},{3,2},... | collective-permute-start | bytes 73736 | tf_op jit(solution)/shard_map/ppermute | solution.py:680
  24.0 7.9 %collective-permute-start = (f32[48,1024]{1,0:T(8,128)S(1)}, f32[48,1024]{1,0:T(8,128)S(1)}, u32[]{:S(2)}, u32[]{:S(2)}) collective-permute-start(f32[48,1024]{1,0:T(8,128)S(1)} %get-tuple-element.48.after_a), channel_id=1, source_target_pairs={{0,16},{32,48},{64,80},{96,112},{128,144},{160,176},{192,208},{224... | collective-permute-start | bytes 589832 | tf_op jit(solution)/shard_map/ppermute | solution.py:680
  27.1 2.7 %copy-start.9 = (f32[2,6,16,128]{3,2,1,0:T(8,128)S(1)}, f32[2,6,16,128]{3,2,1,0:T(8,128)}, u32[]{:S(2)}) copy-start(f32[2,6,16,128]{3,2,1,0:T(8,128)} %get-tuple-element.56.own) | copy-start | bytes 294916
  27.1 4.7 %collective-permute-start.1 = (f32[48,1024]{1,0:T(8,128)S(1)}, f32[48,1024]{1,0:T(8,128)S(1)}, u32[]{:S(2)}, u32[]{:S(2)}) collective-permute-start(f32[48,1024]{1,0:T(8,128)S(1)} %get-tuple-element.49.after_b), channel_id=1, source_target_pairs={{16,32},{48,64},{80,96},{112,128},{144,160},{176,192},{208,224},{2... | collective-permute-start | bytes 589832 | tf_op jit(solution)/shard_map/ppermute | solution.py:680
  34.0 8.1 %collective-permute-start.4 = (f32[240,128]{1,0:T(8,128)S(1)}, f32[240,128]{1,0:T(8,128)S(1)}, u32[]{:S(2)}, u32[]{:S(2)}) collective-permute-start(f32[240,128]{1,0:T(8,128)S(1)} %get-tuple-element.67), channel_id=1, source_target_pairs={{0,16},{32,48},{64,80},{96,112},{128,144},{160,176},{192,208},{224... | collective-permute-start | bytes 368648 | tf_op jit(solution)/shard_map/ppermute | solution.py:680
  39.9 2.3 %collective-permute-start.5 = (f32[240,128]{1,0:T(8,128)S(1)}, f32[240,128]{1,0:T(8,128)S(1)}, u32[]{:S(2)}, u32[]{:S(2)}) collective-permute-start(f32[240,128]{1,0:T(8,128)S(1)} %get-tuple-element.68), channel_id=1, source_target_pairs={{16,32},{48,64},{80,96},{112,128},{144,160},{176,192},{208,224},{2... | collective-permute-start | bytes 368648 | tf_op jit(solution)/shard_map/ppermute | solution.py:680
  66.5 16.7 %all-to-all-start.1 = ((f32[16,1,128]{2,1,0:T(1,128)}), f32[16,1,128]{2,1,0:T(1,128)S(1)}, u32[]{:S(2)}, u32[]{:S(2)}) async-start(f32[16,1,128]{2,1,0:T(1,128)} %shard_map.129), calls=%async_computation.1 | async-start | bytes 16384 | tf_op jit(solution)/shard_map/all_to_all | solution.py:699
